TPU v7x, 256 devices: a whole 4x4x8 slice. The times are simulated.
256 devices in a mesh: bead: 4 (over x), px: 8 (over y, core), py: 8 (over z).
Axes of the slice: x: 4, y: 4, z: 8, core: 2. Of those that a mesh axis runs over, the one named last changes fastest.
Arguments:
- block_owner: int32 [4096, 1], P(('px', 'py')), may hold values from 0 to 63; in each aligned block of 64 rows (0 to 63, 64 to 127, ...) at most 2 rows name the same one
- block_tile: int32 [4096], P(('px', 'py')), may hold values from 0 to 511
- atom_cell: int32 [4096, 128], P(('px', 'py')), may hold values from 0 to 511
- atom_frac: float32 [4, 4096, 3, 128], P('bead', ('px', 'py')), may hold values from 0 to 1
- charge: float32 [4096, 128], P(('px', 'py')), may hold values from -4 to 4
- zone: int32 [4096, 128], P(('px', 'py')), may hold values 0 or 1
Outputs:
- force: float32 [4, 4096, 3, 128], P('bead', ('px', 'py'))
Inputs may be any that keep to these rules, and one draw needn't show every extreme that they name: `block_owner`: among the 64 blocks held by one device, no owner is named by more than 2 blocks.
All inputs are finite; a program needn't handle non-finite values. No bound on the sum of `zone` on one device may be relied on, other than what follows from the above.
Results may differ from a plain program's by a relative error of at most 0.0003.
Values sent between devices are 32-bit elements; how exact they have to be, the bound alone decides.
A program may use at most 128 MiB of HBM per device.

v0:
```python
import math

import jax
import jax.numpy as jnp
from jax import lax
from jax.sharding import PartitionSpec as P

NG = 256


ewald_beta = 0.75
spring_scale = 0.25
highest = lax.Precision.HIGHEST


def shifted(value, axis, steps):
    count = lax.axis_size(axis)
    pairs = [(source, (source + steps) % count) for source in range(count)]
    return lax.ppermute(value, axis, pairs)


def padded(cells, sides, width):
    for axis, dim in sides:
        count = lax.axis_size(axis)
        head = lax.slice_in_dim(cells, 0, width, axis=dim)
        tail = lax.slice_in_dim(cells, cells.shape[dim] - width, cells.shape[dim], axis=dim)
        cells = jnp.concatenate(
            [
                lax.ppermute(tail, axis, [(i, (i + 1) % count) for i in range(count)]),
                cells,
                lax.ppermute(head, axis, [((i + 1) % count, i) for i in range(count)]),
            ],
            axis=dim,
        )
    return cells


def spline(offset):
    rest = 1.0 - offset
    weights = [
        rest * rest * rest / 6.0,
        (3.0 * offset * offset * offset - 6.0 * offset * offset + 4.0) / 6.0,
        (-3.0 * offset * offset * offset + 3.0 * offset * offset + 3.0 * offset + 1.0) / 6.0,
        offset * offset * offset / 6.0,
    ]
    slopes = [
        -0.5 * rest * rest,
        1.5 * offset * offset - 2.0 * offset,
        -1.5 * offset * offset + offset + 0.5,
        0.5 * offset * offset,
    ]
    return (weights, slopes)


def influence_part(index_values):
    wave = (index_values + NG // 2) % NG - NG // 2
    theta = wave.astype(jnp.float32) * (2.0 * math.pi / NG)
    factor = 6.0 / (4.0 + 2.0 * jnp.cos(theta))
    return (theta * theta, factor * factor)


def influence(index_x, index_y, index_z):
    square_x, factor_x = influence_part(index_x)
    square_y, factor_y = influence_part(index_y)
    square_z, factor_z = influence_part(index_z)
    wave_sq = square_x + square_y + square_z
    safe_sq = jnp.where(wave_sq > 0, wave_sq, 1.0)
    value = (
        4.0
        * math.pi
        / safe_sq
        * jnp.exp(-wave_sq / (4.0 * ewald_beta * ewald_beta))
        * factor_x
        * factor_y
        * factor_z
    )
    kept = jnp.logical_and(wave_sq > 0, index_z % NG != NG // 2)
    return jnp.where(kept, value, 0.0)


def grid_cells(owners, tile_ids, cell_ids, width_x, width_y, count_y):
    tiles_y = width_y // 8
    tiles_z = NG // 8
    tile_x = tile_ids // (tiles_y * tiles_z)
    tile_y = tile_ids // tiles_z % tiles_y
    tile_z = tile_ids % tiles_z
    base_x = (owners // count_y * width_x + tile_x * 8)[..., None] + cell_ids // 64
    base_y = (owners % count_y * width_y + tile_y * 8)[..., None] + cell_ids // 8 % 8
    base_z = (tile_z * 8)[..., None] + cell_ids % 8
    return jnp.stack([base_x, base_y, base_z], -2)


def spline_rows(base_cell, offset):
    weights, slopes = spline(offset)
    slots_iota = jnp.arange(11, dtype=jnp.int32)[None, :, None]
    weight_table = jnp.zeros(base_cell.shape[:1] + (11,) + base_cell.shape[1:], jnp.float32)
    slope_table = jnp.zeros_like(weight_table)
    for shift_k in range(4):
        hit = (base_cell[:, None, :] + shift_k == slots_iota).astype(jnp.float32)
        weight_table = weight_table + hit * weights[shift_k][:, None, :]
        slope_table = slope_table + hit * slopes[shift_k][:, None, :]
    return (weight_table, slope_table)


def dft_tables(length):
    index_all = jnp.arange(length, dtype=jnp.int32)
    angle = (index_all[:, None] * index_all[None, :] % length).astype(jnp.float32) * (
        2.0 * math.pi / length
    )
    return (jnp.cos(angle), jnp.sin(angle))


def transform(spectrum, axis_pos, cosine, sine, sign):
    letters = "abc"
    target = letters[:axis_pos] + "k" + letters[axis_pos + 1 :]
    formula = letters + "," + letters[axis_pos] + "k->" + target
    real_cos = jnp.einsum(formula, spectrum[0], cosine, precision=highest)
    real_sin = jnp.einsum(formula, spectrum[0], sine, precision=highest)
    imag_cos = jnp.einsum(formula, spectrum[1], cosine, precision=highest)
    imag_sin = jnp.einsum(formula, spectrum[1], sine, precision=highest)
    if sign < 0:
        return jnp.stack([real_cos + imag_sin, imag_cos - real_sin])
    return jnp.stack([real_cos - imag_sin, imag_cos + real_sin])


def fold(array, axis_pos):
    full_shape = list(array.shape)
    tile_count = full_shape[axis_pos]
    core_part = lax.slice_in_dim(array, 0, 8, axis=axis_pos + 1)
    rim_part = lax.slice_in_dim(array, 8, 11, axis=axis_pos + 1)
    padding = [(0, 0)] * array.ndim
    padding[axis_pos + 1] = (0, 5)
    rim_part = jnp.pad(rim_part, padding)
    merged_shape = full_shape[:axis_pos] + [tile_count * 8] + full_shape[axis_pos + 2 :]
    core_part = core_part.reshape(merged_shape)
    rim_part = rim_part.reshape(merged_shape)
    tail_pad = [(0, 0)] * len(merged_shape)
    tail_pad[axis_pos] = (0, 3)
    head_pad = [(0, 0)] * len(merged_shape)
    head_pad[axis_pos] = (8, 0)
    moved = lax.slice_in_dim(jnp.pad(rim_part, head_pad), 0, tile_count * 8 + 3, axis=axis_pos)
    return jnp.pad(core_part, tail_pad) + moved


def unfold(array, axis_pos, tile_count):
    full_shape = list(array.shape)
    split_shape = full_shape[:axis_pos] + [tile_count, 8] + full_shape[axis_pos + 1 :]
    core_part = lax.slice_in_dim(array, 0, tile_count * 8, axis=axis_pos).reshape(split_shape)
    following = lax.slice_in_dim(array, 8, tile_count * 8 + 3, axis=axis_pos)
    padding = [(0, 0)] * array.ndim
    padding[axis_pos] = (0, 5)
    following = jnp.pad(following, padding).reshape(split_shape)
    following = lax.slice_in_dim(following, 0, 3, axis=axis_pos + 1)
    return jnp.concatenate([core_part, following], axis_pos + 1)


def local(block_owner, block_tile, atom_cell, atom_frac, charge, zone):
    count_x = lax.axis_size("px")
    count_y = lax.axis_size("py")
    owner_count = count_x * count_y
    width_x = NG // count_x
    width_y = NG // count_y
    blocks = block_owner.shape[0]
    atoms = atom_cell.shape[1]
    capacity = max(2, (2 * blocks + owner_count - 1) // owner_count)
    slot_count = owner_count * capacity
    tiles_x = width_x // 8
    tiles_y = width_y // 8
    tiles_z = NG // 8
    tile_total = tiles_x * tiles_y * tiles_z
    owners = block_owner[:, 0]
    fractions = atom_frac[0]
    charged = charge * zone.astype(jnp.float32)
    member = (owners[:, None] == jnp.arange(owner_count, dtype=jnp.int32)[None, :]).astype(
        jnp.float32
    )
    ranking = jnp.sum((jnp.cumsum(member, 0) - member) * member, 1).astype(jnp.int32)
    target = owners * capacity + ranking
    packed = (block_tile[:, None] * 512 + atom_cell).astype(jnp.float32)
    payload = jnp.concatenate([charged[:, None, :], fractions, packed[:, None, :]], 1).reshape(
        blocks, 5 * atoms
    )
    outgoing = jnp.zeros((slot_count, 5 * atoms), jnp.float32).at[target].set(payload)
    outgoing = outgoing.reshape(owner_count, capacity, 5, atoms)
    incoming = lax.all_to_all(
        outgoing, ("px", "py"), split_axis=0, concat_axis=0, tiled=True
    ).reshape(slot_count // 32, 32, 5, atoms)

    def spread(slots):
        local_cell = slots[:, 4].astype(jnp.int32) % 512
        along_x, unused_x = spline_rows(local_cell // 64, slots[:, 1])
        along_y, unused_y = spline_rows(local_cell // 8 % 8, slots[:, 2])
        along_z, unused_z = spline_rows(local_cell % 8, slots[:, 3])
        plane = (
            (slots[:, 0][:, None, :] * along_x)[:, :, None, :] * along_y[:, None, :, :]
        ).reshape(32, 121, atoms)
        return jnp.einsum("sba,sca->sbc", plane, along_z, precision=highest).reshape(32, 1331)

    contrib = lax.map(spread, incoming).reshape(slot_count, 1331)
    tile_in = (incoming[:, :, 4, 0].astype(jnp.int32) // 512).reshape(slot_count)
    tile_sum = jax.ops.segment_sum(contrib, tile_in, num_segments=tile_total)
    density = tile_sum.reshape(tiles_x, tiles_y, tiles_z, 11, 11, 11).transpose(0, 3, 1, 4, 2, 5)
    density = fold(fold(fold(density, 0), 1), 2)
    density = jnp.concatenate([density[:, :, :3] + density[:, :, NG:], density[:, :, 3:NG]], 2)
    rim_x = shifted(density[width_x:], "px", 1)
    density = jnp.concatenate([density[:3] + rim_x, density[3:width_x]], 0)
    rim_y = shifted(density[:, width_y:], "py", 1)
    density = jnp.concatenate([density[:, :3] + rim_y, density[:, 3:width_y]], 1)
    cosine, sine = dft_tables(NG)
    index_all = jnp.arange(NG, dtype=jnp.int32)
    kept_cols = NG // 2
    spectrum = jnp.stack(
        [
            jnp.einsum("xyz,zk->xyk", density, cosine[:, :kept_cols], precision=highest),
            -jnp.einsum("xyz,zk->xyk", density, sine[:, :kept_cols], precision=highest),
        ]
    )
    spectrum = lax.all_to_all(spectrum, "py", split_axis=3, concat_axis=2, tiled=True)
    spectrum = transform(spectrum, 1, cosine, sine, -1)
    spectrum = lax.all_to_all(spectrum, "px", split_axis=2, concat_axis=1, tiled=True)
    spectrum = transform(spectrum, 0, cosine, sine, -1)
    col_dev = kept_cols // count_y
    wave_y = lax.axis_index("px") * width_x + jnp.arange(width_x, dtype=jnp.int32)
    wave_z = lax.axis_index("py") * col_dev + jnp.arange(col_dev, dtype=jnp.int32)
    spectrum = (
        spectrum
        * influence(index_all[:, None, None], wave_y[None, :, None], wave_z[None, None, :])[None]
    )
    spectrum = transform(spectrum, 0, cosine, sine, 1)
    spectrum = lax.all_to_all(spectrum, "px", split_axis=1, concat_axis=2, tiled=True)
    spectrum = transform(spectrum, 1, cosine, sine, 1)
    spectrum = lax.all_to_all(spectrum, "py", split_axis=2, concat_axis=3, tiled=True)
    ordering = index_all[:kept_cols]
    doubled = jnp.where(ordering == 0, 1.0, 2.0).astype(jnp.float32)
    back_cos = cosine[ordering] * doubled[:, None]
    back_sin = sine[ordering] * doubled[:, None]
    potential = (
        jnp.einsum("xyk,kz->xyz", spectrum[0], back_cos, precision=highest)
        - jnp.einsum("xyk,kz->xyz", spectrum[1], back_sin, precision=highest)
    ) / float(NG * NG * NG)
    extended = jnp.concatenate([potential, shifted(potential[:3], "px", -1)], 0)
    extended = jnp.concatenate([extended, shifted(extended[:, :3], "py", -1)], 1)
    extended = jnp.concatenate([extended, extended[:, :, :3]], 2)
    tiled = unfold(unfold(unfold(extended, 0, tiles_x), 2, tiles_y), 4, tiles_z)
    tiled = tiled.transpose(0, 2, 4, 1, 3, 5).reshape(tile_total, 1331)
    picked = tiled[tile_in].reshape(slot_count // 32, 32, 11, 11, 11)

    def interpolate(items):
        slots, values = items
        local_cell = slots[:, 4].astype(jnp.int32) % 512
        weight_x, slope_x = spline_rows(local_cell // 64, slots[:, 1])
        weight_y, slope_y = spline_rows(local_cell // 8 % 8, slots[:, 2])
        weight_z, slope_z = spline_rows(local_cell % 8, slots[:, 3])
        lifted = jnp.einsum("sijl,sla->sija", values, weight_z, precision=highest)
        lifted_z = jnp.einsum("sijl,sla->sija", values, slope_z, precision=highest)
        row_plain = jnp.sum(lifted * weight_y[:, None, :, :], 2)
        row_slope = jnp.sum(lifted * slope_y[:, None, :, :], 2)
        row_depth = jnp.sum(lifted_z * weight_y[:, None, :, :], 2)
        grad_x = jnp.sum(slope_x * row_plain, 1)
        grad_y = jnp.sum(weight_x * row_slope, 1)
        grad_z = jnp.sum(weight_x * row_depth, 1)
        return -slots[:, 0][:, None, :] * jnp.stack([grad_x, grad_y, grad_z], 1)

    slot_force = lax.map(interpolate, (incoming, picked)).reshape(owner_count, capacity, 3, atoms)
    returned = lax.all_to_all(
        slot_force, ("px", "py"), split_axis=0, concat_axis=0, tiled=True
    ).reshape(slot_count, 3 * atoms)
    mesh_force = returned[target].reshape(blocks, 3, atoms)
    cells = grid_cells(owners, block_tile, atom_cell, width_x, width_y, count_y)
    located = cells.astype(jnp.float32) + fractions
    beside_all = padded(located[None], (("bead", 0),), 1)
    spring = -spring_scale * (2.0 * located - beside_all[0] - beside_all[2])
    return (mesh_force + spring)[None]


def solution(mesh):
    return jax.shard_map(
        local,
        mesh=mesh,
        in_specs=(
            P(("px", "py"), None),
            P(("px", "py")),
            P(("px", "py"), None),
            P("bead", ("px", "py"), None, None),
            P(("px", "py"), None),
            P(("px", "py"), None),
        ),
        out_specs=P("bead", ("px", "py"), None, None),
        check_vma=False,
    )
```

profile of v0, /device:TPU:1, one launch (start us, length us, event | category | flops | bytes accessed | tf_op | source)
XLA Modules:
  0.0 630.2 jit_solution(6969787010792451450)
XLA Ops:
  8.1 13.2 %all-to-all-start = ((f32[64,2,5,128]{3,1,2,0:T(2,128)}), f32[64,2,5,128]{3,1,2,0:T(2,128)S(1)}, u32[]{:S(2)}, u32[]{:S(2)}) async-start(f32[64,2,5,128]{3,1,2,0:T(2,128)} %copy.131), calls=%async_computation | async-start | bytes 655360 | tf_op jit(solution)/shard_map/all_to_all | solution.py:185
  21.3 13.3 %all-to-all-done = f32[64,2,5,128]{3,1,2,0:T(2,128)S(1)} async-done(((f32[64,2,5,128]{3,1,2,0:T(2,128)}), f32[64,2,5,128]{3,1,2,0:T(2,128)S(1)}, u32[]{:S(2)}, u32[]{:S(2)}) %all-to-all-start) | async-done | bytes 327712 | tf_op jit(solution)/shard_map/all_to_all | solution.py:185
  34.9 24.3 %while.26 = (s32[]{:T(128)}, f32[4,32,1331]{2,1,0:T(8,128)S(1)}, f32[4,32,5,128]{3,1,2,0:T(8,128)S(1)}, s32[]{:T(128)}) while((s32[]{:T(128)}, f32[4,32,1331]{2,1,0:T(8,128)S(1)}, f32[4,32,5,128]{3,1,2,0:T(8,128)S(1)}, s32[]{:T(128)}) %tuple.166), condition=%wide.region_4.5_spmd, body=%wide.region_3.4_spmd.sunk | while | flops 67969024 | bytes 8073925 | solution.py:199
  35.8 4.3 fusion.390
  41.9 4.3 fusion.390
  47.9 4.3 fusion.390
  54.0 4.3 fusion.390
  65.8 9.2 %reshape.574 = f32[4,4,32,11,11,11]{2,1,0,5,4,3:T(4,128)} reshape(f32[512,1331]{0,1:T(8,128)} %copy.135) | data formatting | bytes 5451776 | tf_op jit(solution)/shard_map/reshape | solution.py:202
  77.4 7.8 %slice.287 = f32[4,8,4,11,32,11]{4,2,0,5,3,1:T(4,128)} slice(f32[4,11,4,11,32,11]{4,2,0,5,3,1:T(4,128)} %bitcast.413), slice={[0:4], [0:8], [0:4], [0:11], [0:32], [0:11]} | slice | bytes 3964928 | tf_op jit(solution)/shard_map/slice | solution.py:129
  85.2 3.4 copy.196
  88.6 13.1 %pad_bitcast_fusion = (f32[32,4,11,32,11]{3,0,4,2,1:T(8,128)}, f32[32,4,11,32,11]{3,0,4,2,1:T(8,128)}) fusion(f32[4,3,4,11,32,11]{4,1,0,5,3,2:T(4,128)} %copy.196, f32[4,8,4,11,32,11]{4,2,0,5,3,1:T(4,128)} %slice.287), kind=kLoop, calls=%fused_computation.319 | loop fusion | bytes 6690816 | tf_op jit(solution)/shard_map/reshape | solution.py:136
  101.7 10.6 %slice_add_fusion = f32[35,4,11,32,11]{3,0,4,2,1:T(8,128)} fusion(f32[32,4,11,32,11]{3,0,4,2,1:T(8,128)} %get-tuple-element.306, f32[32,4,11,32,11]{3,0,4,2,1:T(8,128)} %get-tuple-element.307), kind=kLoop, calls=%fused_computation.318 | loop fusion | flops 542080 | bytes 6133248 | tf_op jit(solution)/shard_map/add | solution.py:142
  112.3 6.6 %slice.289 = f32[35,4,8,32,11]{3,0,4,2,1:T(8,128)} slice(f32[35,4,11,32,11]{3,0,4,2,1:T(8,128)} %slice_add_fusion), slice={[0:35], [0:4], [0:8], [0:32], [0:11]} | slice | bytes 3153920 | tf_op jit(solution)/shard_map/slice | solution.py:129
  121.1 4.9 pad.52.clone
  126.0 8.7 %copy.138 = f32[35,4,8,32,11]{0,3,4,2,1:T(8,128)} copy(f32[35,4,8,32,11]{3,0,4,2,1:T(8,128)} %slice.289) | data formatting | bytes 3153920 | tf_op jit(solution)/shard_map/slice | solution.py:129
  134.7 5.4 fusion.173
  144.0 4.0 copy.198
  153.7 7.7 %copy.140 = f32[35,35,32,8]{1,3,2,0:T(8,128)} copy(f32[35,35,32,8]{0,2,3,1:T(8,128)} %slice.291) | data formatting | bytes 2508800 | tf_op jit(solution)/shard_map/slice | solution.py:129
  172.3 3.4 collective-permute-done.1
  177.8 4.4 copy.144
  182.2 4.8 reshape.657
  187.1 3.7 all-to-all-start.1
  190.8 25.8 %all-to-all-done.1 = f32[8,1,32768]{2,1,0:T(1,128)S(1)} async-done(((f32[8,1,32768]{2,1,0:T(1,128)}), f32[8,1,32768]{2,1,0:T(1,128)S(1)}, u32[]{:S(2)}, u32[]{:S(2)}) %all-to-all-start.1) | async-done | bytes 1048608 | tf_op jit(solution)/shard_map/all_to_all | solution.py:218
  220.2 3.3 reshape.658
  223.5 4.6 copy.145
  244.7 4.4 copy.148
  249.1 4.8 reshape.659
  254.0 7.2 %all-to-all-start.2 = ((f32[8,1,32768]{2,1,0:T(1,128)}), f32[8,1,32768]{2,1,0:T(1,128)S(1)}, u32[]{:S(2)}, u32[]{:S(2)}) async-start(f32[8,1,32768]{2,1,0:T(1,128)} %reshape.659), calls=%async_computation.2 | async-start | bytes 2097152 | tf_op jit(solution)/shard_map/all_to_all | solution.py:220
  262.6 13.6 %all-to-all-done.2 = f32[8,1,32768]{2,1,0:T(1,128)S(1)} async-done(((f32[8,1,32768]{2,1,0:T(1,128)}), f32[8,1,32768]{2,1,0:T(1,128)S(1)}, u32[]{:S(2)}, u32[]{:S(2)}) %all-to-all-start.2) | async-done | bytes 1048608 | tf_op jit(solution)/shard_map/all_to_all | solution.py:220
  279.4 3.3 reshape.660
  282.7 4.6 copy.216
  309.0 4.4 copy.150
  313.4 3.9 reshape.661
  317.3 18.4 %all_to_all.70 = f32[8,1,32768]{2,1,0:T(1,128)S(1)} all-to-all(f32[8,1,32768]{2,1,0:T(1,128)S(1)} %reshape.661), channel_id=1, replica_groups=mesh['bead'=4,'px'=8,'py'=8] {'px'}, dimensions={0} | all-to-all | bytes 2097152 | tf_op jit(solution)/shard_map/all_to_all | solution.py:230
  338.8 3.3 reshape.662
  342.1 4.6 copy.215
  361.9 4.4 copy.152
  366.3 4.8 reshape.663
  371.1 3.7 all-to-all-start.4
  376.4 25.4 %all-to-all-done.4 = f32[8,1,32768]{2,1,0:T(1,128)S(1)} async-done(((f32[8,1,32768]{2,1,0:T(1,128)}), f32[8,1,32768]{2,1,0:T(1,128)S(1)}, u32[]{:S(2)}, u32[]{:S(2)}) %all-to-all-start.4) | async-done | bytes 1048608 | tf_op jit(solution)/shard_map/all_to_all | solution.py:232
  404.9 3.3 reshape.664
  408.3 6.5 %copy.153 = f32[2,32,8,32,16]{3,4,2,1,0:T(8,128)} copy(f32[2,32,8,32,16]{1,4,0,3,2:T(8,128)} %bitcast.424) | data formatting | bytes 2097152 | tf_op jit(solution)/shard_map/all_to_all | solution.py:232
  417.3 3.5 fusion.237
  420.8 3.5 fusion.181
  429.8 5.5 collective-permute-done.3
  441.3 19.5 %reshape.586 = f32[4,11,4,11,32,8]{5,4,2,3,1,0:T(8,128)} reshape(f32[4,11,4,11,256]{4,2,3,1,0:T(4,128)S(1)} %pad.59.clone) | data formatting | bytes 3964928 | tf_op jit(solution)/shard_map/reshape | solution.py:152
  460.8 22.4 %copy.159 = f32[4,11,4,11,32,3]{4,2,5,3,1,0:T(4,128)S(1)} copy(f32[4,11,4,11,32,3]{5,4,2,3,1,0:T(8,128)} %bitcast.411) | data formatting | bytes 1486848 | tf_op jit(solution)/shard_map/slice | solution.py:153
  483.2 21.5 %reshape.650 = f32[4,11,4,11,32,8]{5,4,3,2,1,0:T(8,128)} reshape(f32[4,11,4,11,256]{4,3,2,1,0:T(8,128)} %fusion.174) | data formatting | bytes 3964928 | tf_op jit(solution)/shard_map/reshape | solution.py:148
  504.7 22.5 %copy.158 = f32[4,11,4,11,32,8]{4,2,5,3,1,0:T(4,128)} copy(f32[4,11,4,11,32,8]{5,4,3,2,1,0:T(8,128)} %reshape.650) | data formatting | bytes 3964928 | tf_op jit(solution)/shard_map/reshape | solution.py:148
  527.2 6.5 %maximum_bitcast_fusion = f32[4,4,32,11,11,11]{2,1,5,4,3,0:T(4,128)S(1)} fusion(f32[4,11,4,11,32,3]{4,2,5,3,1,0:T(4,128)S(1)} %copy.159, f32[4,11,4,11,32,8]{4,2,5,3,1,0:T(4,128)} %copy.158), kind=kLoop, calls=%fused_computation.317 | loop fusion | flops 681472 | bytes 5451776 | tf_op jit(solution)/shard_map/transpose | solution.py:245
  533.7 4.7 copy.160
  538.4 12.6 %reshape.587 = f32[512,1331]{0,1:T(8,128)} reshape(f32[4,4,32,11,11,11]{2,1,0,5,4,3:T(4,128)} %copy.160) | data formatting | bytes 5451776 | tf_op jit(solution)/shard_map/reshape | solution.py:245
  554.9 7.3 %reshape.651 = f32[4,32,11,11,11]{4,3,2,1,0:T(8,128)} reshape(f32[128,1331]{1,0:T(8,128)} %gather_fusion.2) | data formatting | bytes 1362944 | tf_op jit(solution)/shard_map/while | solution.py:264
  562.2 49.5 %while.27 = (s32[]{:T(128)}, f32[4,32,3,128]{3,2,1,0:T(4,128)S(1)}, f32[4,32,5,128]{3,1,2,0:T(8,128)}, f32[4,32,11,11,11]{4,3,2,1,0:T(8,128)}, s32[]{:T(128)}) while((s32[]{:T(128)}, f32[4,32,3,128]{3,2,1,0:T(4,128)S(1)}, f32[4,32,5,128]{3,1,2,0:T(8,128)}, f32[4,32,11,11,11]{4,3,2,1,0:T(8,128)}, s32[]{:T(128)}) %tuple.172), condition=%wide.region_13.14_spmd, body=%wide.region_6.13_spmd.sunk | while | flops 137269248 | bytes 9535573 | solution.py:264
  563.8 5.5 multiply_reduce_fusion.9
  569.3 5.0 multiply_reduce_fusion.10
  576.1 5.5 multiply_reduce_fusion.9
  581.6 5.0 multiply_reduce_fusion.10
  588.4 5.5 multiply_reduce_fusion.9
  593.9 5.0 multiply_reduce_fusion.10
  600.7 5.5 multiply_reduce_fusion.9
  606.3 5.0 multiply_reduce_fusion.10
  612.5 4.7 all-to-all-start.5
  620.0 8.1 %all-to-all-done.5 = f32[64,2,3,128]{3,1,2,0:T(2,128)S(1)} async-done(((f32[64,2,3,128]{3,1,2,0:T(2,128)}), f32[64,2,3,128]{3,1,2,0:T(2,128)S(1)}, u32[]{:S(2)}, u32[]{:S(2)}) %all-to-all-start.5) | async-done | bytes 196640 | tf_op jit(solution)/shard_map/all_to_all | solution.py:265
  (238 shorter events, 147.6 us)
Async XLA Ops:
  2.3 3.9 copy-start.6
  8.1 26.4 %all-to-all-start = ((f32[64,2,5,128]{3,1,2,0:T(2,128)}), f32[64,2,5,128]{3,1,2,0:T(2,128)S(1)}, u32[]{:S(2)}, u32[]{:S(2)}) async-start(f32[64,2,5,128]{3,1,2,0:T(2,128)} %copy.131), calls=%async_computation | async-start | bytes 655360 | tf_op jit(solution)/shard_map/all_to_all | solution.py:185
  59.3 0.7 copy-start
  59.3 1.0 copy-start.8
  112.3 6.6 %slice-start = ((f32[35,4,11,32,11]{3,0,4,2,1:T(8,128)}), f32[35,4,3,32,11]{3,0,4,2,1:T(8,128)S(1)}, s32[]{:S(2)}) async-start(f32[35,4,11,32,11]{3,0,4,2,1:T(8,128)} %slice_add_fusion), calls=%async_computation.6 | async-start | bytes 5406720 | tf_op jit(solution)/shard_map/slice | solution.py:130
  165.8 4.3 collective-permute-start
  170.6 5.1 collective-permute-start.1
  187.1 29.5 %all-to-all-start.1 = ((f32[8,1,32768]{2,1,0:T(1,128)}), f32[8,1,32768]{2,1,0:T(1,128)S(1)}, u32[]{:S(2)}, u32[]{:S(2)}) async-start(f32[8,1,32768]{2,1,0:T(1,128)} %reshape.657), calls=%async_computation.1 | async-start | bytes 2097152 | tf_op jit(solution)/shard_map/all_to_all | solution.py:218
  254.0 22.3 %all-to-all-start.2 = ((f32[8,1,32768]{2,1,0:T(1,128)}), f32[8,1,32768]{2,1,0:T(1,128)S(1)}, u32[]{:S(2)}, u32[]{:S(2)}) async-start(f32[8,1,32768]{2,1,0:T(1,128)} %reshape.659), calls=%async_computation.2 | async-start | bytes 2097152 | tf_op jit(solution)/shard_map/all_to_all | solution.py:220
  295.1 7.1 %copy-start.1 = (f32[256,32,16]{0,1,2:T(8,128)S(1)}, f32[256,32,16]{0,1,2:T(8,128)}, u32[]{:S(2)}) copy-start(f32[256,32,16]{0,1,2:T(8,128)} %fusion.198) | copy-start | bytes 1572868
  371.1 30.7 %all-to-all-start.4 = ((f32[8,1,32768]{2,1,0:T(1,128)}), f32[8,1,32768]{2,1,0:T(1,128)S(1)}, u32[]{:S(2)}, u32[]{:S(2)}) async-start(f32[8,1,32768]{2,1,0:T(1,128)} %reshape.663), calls=%async_computation.4 | async-start | bytes 2097152 | tf_op jit(solution)/shard_map/all_to_all | solution.py:232
  424.3 5.1 collective-permute-start.2
  429.5 5.9 collective-permute-start.3
  562.2 55.1 %copy-start.2 = (f32[1,64,3,128]{3,1,2,0:T(8,128)S(1)}, f32[1,64,3,128]{3,1,2,0:T(8,128)}, u32[]{:S(2)}) copy-start(f32[1,64,3,128]{3,1,2,0:T(8,128)} %param.13) | copy-start | bytes 294916
  562.2 55.1 %copy-start.3 = (s32[64,128]{1,0:T(8,128)S(1)}, s32[64,128]{1,0:T(8,128)}, u32[]{:S(2)}) copy-start(s32[64,128]{1,0:T(8,128)} %get-tuple-element.298) | copy-start | bytes 98308
  562.2 55.1 %copy-start.4 = (s32[64,128]{1,0:T(8,128)S(1)}, s32[64,128]{1,0:T(8,128)}, u32[]{:S(2)}) copy-start(s32[64,128]{1,0:T(8,128)} %get-tuple-element.299) | copy-start | bytes 98308
  562.2 55.1 %copy-start.5 = (s32[64,128]{1,0:T(8,128)S(1)}, s32[64,128]{1,0:T(8,128)}, u32[]{:S(2)}) copy-start(s32[64,128]{1,0:T(8,128)} %get-tuple-element.301) | copy-start | bytes 98308
  562.2 57.8 %copy-start.7 = (s32[64]{0:T(128)S(1)}, s32[64]{0:T(128)}, u32[]{:S(2)}) copy-start(s32[64]{0:T(128)} %copy-done.6) | copy-start | bytes 772
  612.5 15.5 %all-to-all-start.5 = ((f32[64,2,3,128]{3,1,2,0:T(2,128)}), f32[64,2,3,128]{3,1,2,0:T(2,128)S(1)}, u32[]{:S(2)}, u32[]{:S(2)}) async-start(f32[64,2,3,128]{3,1,2,0:T(2,128)} %copy.166), calls=%async_computation.5 | async-start | bytes 393216 | tf_op jit(solution)/shard_map/all_to_all | solution.py:265
  617.4 11.5 %collective-permute-start.5 = (f32[1,64,3,128]{3,2,1,0:T(4,128)S(1)}, f32[1,64,3,128]{3,2,1,0:T(4,128)S(1)}, u32[]{:S(2)}, u32[]{:S(2)}) collective-permute-start(f32[1,64,3,128]{3,2,1,0:T(4,128)S(1)} %fusion.235), channel_id=1, source_target_pairs={{64,0},{128,64},{192,128},{0,192},{65,1},{129,65},{193,129},{1,193... | collective-permute-start | bytes 294920 | tf_op jit(solution)/shard_map/ppermute | solution.py:31
  620.0 8.9 %collective-permute-start.4 = (f32[1,64,3,128]{3,2,1,0:T(4,128)S(1)}, f32[1,64,3,128]{3,2,1,0:T(4,128)S(1)}, u32[]{:S(2)}, u32[]{:S(2)}) collective-permute-start(f32[1,64,3,128]{3,2,1,0:T(4,128)S(1)} %fusion.235), channel_id=1, source_target_pairs={{0,64},{64,128},{128,192},{192,0},{1,65},{65,129},{129,193},{193,1... | collective-permute-start | bytes 294920 | tf_op jit(solution)/shard_map/ppermute | solution.py:29
where the time goes:
time: 640 us; the launch traced here: 630 us
  local copies, waits for them, and re-layouts  307 us (48%)
  matrix products  104 us (16%)
  waiting for transfers between devices  98.5 us (15%)
  other arithmetic  59.4 us (9%)
  starting transfers between devices  41 us (6%)
  blocking collectives  18.4 us (3%)
    unnamed x31, local copies, waits for them, and re-layouts  44.2 us
    reshape x2, local copies, waits for them, and re-layouts, unfold(): lax.slice_in_dim(array, 0, tile_count * 8, axis=axis_pos)  44 us
    slice x5, local copies, waits for them, and re-layouts, fold(): core_part = lax.slice_in_dim(array, 0, 8, axis=axis_pos + 1)  33.3 us
    all_to_all x1, waiting for transfers between devices, local(): lax.all_to_all(spectrum, 'py', split_axis=3, concat_axis=2, tiled=True)  25.8 us
    all_to_all x1, waiting for transfers between devices, local(): lax.all_to_all(spectrum, 'py', split_axis=2, concat_axis=3, tiled=True)  25.4 us
    slice x3, local copies, waits for them, and re-layouts, unfold(): following = lax.slice_in_dim(following, 0, 3, axis=axis_pos + 1)  22.6 us
    dot_general x4, matrix products, interpolate(): lifted = jnp.einsum('sijl,sla->sija', values, weight_z, precision=highest)  22.1 us
    dot_general x4, matrix products, interpolate(): lifted_z = jnp.einsum('sijl,sla->sija', values, slope_z, precision=highest)  20 us
  transfers between devices with their start and end apart: 11, of which 9 were waited for; matrix products, arithmetic and copies ran while one was open for 1% of the time, Pallas kernels for 0%

commit v1 on v0

v1 whole, which is shorter than its diff:
```python
import functools
import math

import jax
import jax.numpy as jnp
import ml_dtypes
import numpy as np
from jax import lax
from jax.experimental import pallas as pl
from jax.experimental.pallas import tpu as pltpu
from jax.sharding import PartitionSpec as P

NG = 256
OWN = 64
f32 = jnp.float32
bf16 = jnp.bfloat16
MESH = pl.DeviceIdType.MESH
VMEM = pltpu.VMEM
SMEM = pltpu.SMEM
ewald_beta = 0.75
spring_scale = 0.25


def halves(table):
    table = table.astype(np.float32)
    high = table.astype(ml_dtypes.bfloat16)
    low = (table - high.astype(np.float32)).astype(ml_dtypes.bfloat16)
    return high, low


def waves(rows, columns):
    angle = (np.outer(rows, columns) % NG) * (2.0 * math.pi / NG)
    return np.cos(angle), np.sin(angle)


@functools.lru_cache(None)
def tables():
    whole = np.arange(NG)
    owner = np.arange(OWN)
    kz = np.stack([2 * owner, 2 * owner + 1])
    cos_z, sin_z = waves(kz.reshape(-1), whole)
    forward_z = np.concatenate([cos_z, -sin_z])
    scale = np.where(kz.reshape(-1) == 0, 1.0, 2.0) / float(NG**3)
    back_z = (forward_z * np.concatenate([scale, scale])[:, None]).T
    main = whole
    rim = np.arange(256)
    rim = 32 * (rim // 32 + 1) + rim % 4
    cos_y, sin_y = waves(np.concatenate([main, rim]), whole)
    forward_y = np.concatenate([cos_y, sin_y], 1)
    back_y = np.concatenate([cos_y.T, sin_y.T], 1)
    step, block, group = np.meshgrid(np.arange(4), np.arange(8), np.arange(8), indexing="ij")
    place = (32 * block + 4 * group + step).reshape(-1)
    cos_x, sin_x = waves(whole, place)
    forward_x = np.concatenate([cos_x, sin_x])
    back_x = np.concatenate([cos_x.T, sin_x.T])
    wave = (whole + NG // 2) % NG - NG // 2
    theta = wave * (2.0 * math.pi / NG)
    factor = (6.0 / (4.0 + 2.0 * np.cos(theta))) ** 2
    factor = factor * np.exp(-theta * theta / (4.0 * ewald_beta * ewald_beta))
    column = np.zeros((256, 128), np.float32)
    column[:, 0], column[:, 1] = theta * theta, factor
    row = np.zeros((8, 256), np.float32)
    row[0], row[1] = theta * theta, factor
    in_z = np.stack([(theta * theta)[kz.T], factor[kz.T]], 1).astype(np.float32)
    return dict(
        forward_z=halves(forward_z),
        back_z=halves(back_z),
        forward_y=halves(forward_y),
        back_y=halves(back_y),
        forward_x=halves(forward_x),
        back_x=halves(back_x),
        column=column,
        row=row,
        in_z=in_z,
    )


def split(value):
    high = value.astype(bf16)
    return high, (value - high.astype(f32)).astype(bf16)


def dots(a_high, a_low, b_high, b_low):
    dot = functools.partial(jnp.dot, preferred_element_type=f32)
    return dot(a_high, b_high) + (dot(a_high, b_low) + dot(a_low, b_high))


def lane_of(rank):
    return lax.broadcasted_iota(jnp.int32, (1,) * (rank - 1) + (128,), rank - 1)


def turn(value, steps):
    steps = steps % 128
    if steps == 0:
        return value
    flat = value.reshape(-1, 128)
    return pltpu.roll(flat, steps, 1).reshape(value.shape)


def blocks_exchanged(parts):
    lane = lane_of(parts[0].ndim)
    low = lane < 64
    even = (lane // 32) % 2 == 0
    first = [
        jnp.where(low, parts[0], turn(parts[2], 64)),
        jnp.where(low, parts[1], turn(parts[3], 64)),
        jnp.where(low, turn(parts[0], 64), parts[2]),
        jnp.where(low, turn(parts[1], 64), parts[3]),
    ]
    return [
        jnp.where(even, first[0], turn(first[1], 32)),
        jnp.where(even, turn(first[0], 96), first[1]),
        jnp.where(even, first[2], turn(first[3], 32)),
        jnp.where(even, turn(first[2], 96), first[3]),
    ]


def bspline(offsets, slopes):
    v = jnp.abs(offsets)
    a = jnp.maximum(2.0 - v, 0.0)
    b = jnp.maximum(1.0 - v, 0.0)
    aa = a * a
    bb = b * b
    weight = aa * a * (1.0 / 6.0) - bb * b * (4.0 / 6.0)
    if not slopes:
        return weight
    half = 0.5 * aa - 2.0 * bb
    return weight, jnp.where(offsets < 0.0, -half, half)


def vmem(count):
    return [pl.BlockSpec(memory_space=VMEM)] * count


def targets(owner_row):
    blocks = owner_row.shape[1]
    up = lax.broadcasted_iota(jnp.int32, (blocks, blocks), 0)
    across = lax.broadcasted_iota(jnp.int32, (blocks, blocks), 1)
    owner_column = jnp.sum(jnp.where(up == across, owner_row, 0).astype(f32), 1, keepdims=True)
    owner_float = owner_row.astype(f32)
    before = jnp.where((owner_column == owner_float) & (up < across), 1.0, 0.0)
    rank = jnp.sum(before, 0, keepdims=True)
    target = 2.0 * owner_float + rank
    slot = lax.broadcasted_iota(jnp.int32, (2 * OWN, blocks), 0).astype(f32)
    return slot == target


def three(value):
    high = value.astype(bf16)
    rest = value - high.astype(f32)
    middle = rest.astype(bf16)
    return high, middle, (rest - middle.astype(f32)).astype(bf16)


def pack_kernel(owner_ref, tile_ref, cell_ref, frac_ref, charge_ref, zone_ref, out_ref):
    chosen = jnp.where(targets(owner_ref[...]), 1.0, 0.0).astype(bf16)
    blocks = cell_ref.shape[0]
    up = lax.broadcasted_iota(jnp.int32, (blocks, blocks), 0)
    across = lax.broadcasted_iota(jnp.int32, (blocks, blocks), 1)
    tile = jnp.sum(jnp.where(up == across, tile_ref[...], 0).astype(f32), 1, keepdims=True)
    tile = tile.astype(jnp.int32)
    cell = cell_ref[...]
    corners = [tile >> 7, (tile >> 5) & 3, tile & 31]
    cells = [cell >> 6, (cell >> 3) & 7, cell & 7]
    fields = [charge_ref[...] * zone_ref[...].astype(f32)]
    for axis in range(3):
        base = (corners[axis] * 8).astype(f32)
        inside = cells[axis].astype(f32) + frac_ref[axis]
        fields.append(base + jnp.minimum(inside, 8.0 - 2.0**-16))
    for place, field in enumerate(fields):
        parts = three(field)
        moved = sum(
            jnp.dot(chosen, part, preferred_element_type=f32) for part in reversed(parts)
        )
        out_ref[pl.ds(place, 2 * OWN, stride=4), :] = moved


def pack(owner_row, tile_row, cell, frac, charge, zone):
    return pl.pallas_call(
        pack_kernel,
        out_shape=jax.ShapeDtypeStruct((8 * OWN, 128), f32),
        in_specs=vmem(6),
        out_specs=pl.BlockSpec(memory_space=VMEM),
        name="pack",
    )(owner_row, tile_row, cell, frac, charge, zone)


def slot_list(slots_ref, list_ref, codes, codes_scalar, sem):
    charge = slots_ref[pl.ds(0, 2 * OWN, stride=4), :]
    along_x = slots_ref[pl.ds(1, 2 * OWN, stride=4), :]
    along_z = slots_ref[pl.ds(3, 2 * OWN, stride=4), :]
    tile_x = (jnp.max(along_x, 1, keepdims=True) * 0.125).astype(jnp.int32)
    tile_z = (jnp.max(along_z, 1, keepdims=True) * 0.125).astype(jnp.int32)
    filled = jnp.max(jnp.abs(charge), 1, keepdims=True) > 0.0
    code = jnp.where(filled, tile_x * 32 + tile_z, -1)
    up = lax.broadcasted_iota(jnp.int32, (128, 128), 0)
    across = lax.broadcasted_iota(jnp.int32, (128, 128), 1)
    row = jnp.sum(jnp.where(up == across, code.astype(f32), 0.0), 0, keepdims=True)
    codes[...] = jnp.broadcast_to(row.astype(jnp.int32), (8, 128))
    copy = pltpu.make_async_copy(codes, codes_scalar, sem)
    copy.start()
    copy.wait()

    def step(slot, carry):
        count, empty = carry
        value = codes_scalar[0, slot]
        held = value >= 0
        list_ref[count] = slot * 128 + jnp.maximum(value, 0)
        return count + held.astype(jnp.int32), jnp.where(held, empty, slot)

    count, empty = lax.fori_loop(0, 2 * OWN, step, (jnp.int32(0), jnp.int32(0)))
    list_ref[count] = empty * 128
    list_ref[255] = (count + 1) // 2


def spread_kernel(slots_ref, ez_high, ez_low, out_ref, list_ref, density, packed_high, packed_low, codes, codes_scalar, sem):
    slot_list(slots_ref, list_ref, codes, codes_scalar, sem)
    density[...] = jnp.zeros_like(density)
    rows16 = lax.broadcasted_iota(jnp.int32, (16, 128), 0).astype(f32) - 1.0
    rows48 = lax.broadcasted_iota(jnp.int32, (48, 128), 0).astype(f32) - 1.0
    nothing = jnp.zeros((16, 128), f32)

    def one(item):
        slot = item >> 7
        tile_x = (item >> 5) & 3
        tile_z = item & 31
        charge = slots_ref[pl.ds(4 * slot, 1), :]
        at_x = slots_ref[pl.ds(4 * slot + 1, 1), :] - (8 * tile_x).astype(f32)
        at_y = slots_ref[pl.ds(4 * slot + 2, 1), :]
        at_z = slots_ref[pl.ds(4 * slot + 3, 1), :] - (8 * tile_z).astype(f32)
        weight_x = bspline(rows16 - at_x, False) * charge
        weight_z = bspline(rows16 - at_z, False)
        weight_y = bspline(rows48 - at_y, False)
        plane = jnp.concatenate([weight_x[i : i + 1] * weight_z for i in range(11)], 0)
        plane = jnp.concatenate(split(plane), 1)
        y_high = weight_y.astype(bf16).astype(f32)
        y_low = weight_y - y_high
        left = jnp.concatenate([y_high, nothing, y_low, nothing], 0)
        right = jnp.concatenate([y_high, nothing, jnp.zeros((64, 128), f32)], 0)
        both = jnp.concatenate([left, right], 1).astype(bf16)
        out = lax.dot_general(plane, both, (((1,), (1,)), ((), ())), preferred_element_type=f32)
        return tile_x, tile_z, out

    def put(tile_x, tile_z, out):
        base = pl.multiple_of(8 * tile_z, 8)
        for i in range(11):
            density[8 * tile_x + i, pl.ds(base, 16), :] += out[16 * i : 16 * i + 16]

    def step(index, carry):
        first = one(list_ref[2 * index])
        second = one(list_ref[2 * index + 1])
        put(*first)
        put(*second)
        return carry

    lax.fori_loop(0, list_ref[255], step, 0)

    lane = lane_of(2)
    low = lane < 64
    even = (lane // 32) % 2 == 0

    def fold(plane, carry):
        density[plane, 0:8, :] += density[plane, 256:264, :]
        return carry

    lax.fori_loop(0, 36, fold, 0)

    def regroup(chunk, carry):
        here = pl.ds(pl.multiple_of(chunk * 32, 32), 32)
        rim = jnp.zeros((32, 128), f32)

        def keep(group, value):
            high, rest = split(value)
            packed_high[group, here, :] = high
            packed_low[group, here, :] = rest

        for group in range(9):
            four = [density[4 * group + i, here, :] for i in range(4)]
            pair_even = jnp.where(low, four[0], four[2]) + turn(jnp.where(low, four[2], four[0]), 64)
            pair_odd = jnp.where(low, four[1], four[3]) + turn(jnp.where(low, four[3], four[1]), 64)
            pair_odd = turn(pair_odd, 32)
            main = jnp.where(even, pair_even, pair_odd)
            side = jnp.where(even, pair_odd, pair_even)
            if group < 8:
                keep(group, main)
                rim = rim + turn(side, 4 * group)
            else:
                last = lane >= 96
                corner = jnp.where((lane >= 96) & (lane < 100), turn(side, 64), 0.0)
                corner = jnp.where((lane >= 100) & (lane < 104), turn(side, 36), corner)
                corner = jnp.where((lane >= 104) & (lane < 108), turn(side, 8), corner)
                keep(8, jnp.where(last, corner, main))
        keep(9, rim)
        return carry

    lax.fori_loop(0, 8, regroup, 0)

    for pair in range(5):
        high = jnp.concatenate([packed_high[2 * pair], packed_high[2 * pair + 1]], 1)
        rest = jnp.concatenate([packed_low[2 * pair], packed_low[2 * pair + 1]], 1)
        result = dots(ez_high[...], ez_low[...], high, rest)
        for part in range(2):
            group = 2 * pair + part
            for c in range(4):
                start = 8 * c + group if group < 8 else 32 + c + 4 * (group - 8)
                out_ref[pl.ds(start, OWN, stride=40), :] = result[
                    64 * c : 64 * c + 64, 128 * part : 128 * part + 128
                ]


def spread(slots):
    table = tables()
    high, low = table["forward_z"]
    return pl.pallas_call(
        spread_kernel,
        out_shape=[
            jax.ShapeDtypeStruct((OWN * 40, 128), f32),
            jax.ShapeDtypeStruct((256,), jnp.int32),
        ],
        in_specs=vmem(3),
        out_specs=[pl.BlockSpec(memory_space=VMEM), pl.BlockSpec(memory_space=SMEM)],
        scratch_shapes=[
            VMEM((36, 264, 128), f32),
            VMEM((10, 256, 128), bf16),
            VMEM((10, 256, 128), bf16),
            VMEM((8, 128), jnp.int32),
            SMEM((8, 128), jnp.int32),
            pltpu.SemaphoreType.DMA,
        ],
        compiler_params=pltpu.CompilerParams(vmem_limit_bytes=48 << 20),
        name="spread",
    )(slots, jnp.asarray(high), jnp.asarray(low))


def shifted(value, steps):
    if steps == 1:
        return jnp.concatenate([value[7:8], value[0:7]], 0)
    return jnp.concatenate([value[1:8], value[0:1]], 0)


def middle_kernel(
    in_z, in_ref, fy_high, fy_low, fx_high, fx_low, bx_high, bx_low, by_high, by_low,
    column_ref, row_ref, out_ref, plane_high, plane_low, back,
):
    lane = lane_of(3)
    sub = lax.broadcasted_iota(jnp.int32, (1, 8, 128), 1)
    lane_group = (lane // 4) % 8

    for q in range(2):
        extra = blocks_exchanged([in_ref[:, 4 * q + j, 32:40, :] for j in range(4)])
        for c in range(4):
            main = blocks_exchanged(
                [in_ref[:, 4 * q + j, 8 * c : 8 * c + 8, :] for j in range(4)]
            )
            for i in range(4):
                value = main[i]
                rim = jnp.where(lane_group == sub, extra[(i + 1) % 4][:, 4 + c : 5 + c, :], 0.0)
                if i < 3:
                    value = value + jnp.where(sub == 0, shifted(extra[i][:, c : c + 1, :], 1), 0.0)
                    corner = shifted(extra[3][:, c : c + 1, :], 1)
                    rim = rim + jnp.where((sub == 0) & (lane_group == i), corner, 0.0)
                for part, array in enumerate((value, rim)):
                    high, rest = split(array.reshape(64, 128))
                    at = (c, slice(64 * i, 64 * i + 64), slice(256 * part + 128 * q, 256 * part + 128 * q + 128))
                    plane_high[at] = high
                    plane_low[at] = rest

    column = column_ref[...]
    row = row_ref[...]

    def one(n, carry):
        real = dots(plane_high[n], plane_low[n], fy_high[...], fy_low[...])
        imag = dots(plane_high[2 + n], plane_low[2 + n], fy_high[...], fy_low[...])
        spec = jnp.concatenate(
            [real[:, :256] + imag[:, 256:], imag[:, :256] - real[:, 256:]], 1
        )
        high, rest = split(spec)
        both = dots(fx_high[...], fx_low[...], high, rest)
        square = column[:, 0:1] + row[0:1, :] + in_z[0, n]
        green = column[:, 1:2] * row[1:2, :] * (in_z[1, n] * (4.0 * math.pi))
        green = jnp.where(square > 0.0, green / jnp.where(square > 0.0, square, 1.0), 0.0)
        spec = jnp.concatenate(
            [
                (both[:256, :256] + both[256:, 256:]) * green,
                (both[:256, 256:] - both[256:, :256]) * green,
            ],
            1,
        )
        high, rest = split(spec)
        both = dots(bx_high[...], bx_low[...], high, rest)
        spec = jnp.concatenate(
            [both[:256, :256] - both[256:, 256:], both[:256, 256:] + both[256:, :256]], 0
        )
        high, rest = split(spec)
        both = dots(high, rest, by_high[...], by_low[...])
        back[n] = both[:256, :512] - both[256:, 512:]
        back[2 + n] = both[256:, :512] + both[:256, 512:]
        return carry

    lax.fori_loop(0, 2, one, 0)

    for q in range(2):
        extra = [jnp.zeros((8, 8, 128), f32) for _ in range(4)]
        for c in range(4):
            main, corner = [], jnp.zeros((8, 1, 128), f32)
            for i in range(4):
                value = back[c, 64 * i : 64 * i + 64, 128 * q : 128 * q + 128].reshape(8, 8, 128)
                rim = back[c, 64 * i : 64 * i + 64, 256 + 128 * q : 384 + 128 * q].reshape(8, 8, 128)
                main.append(value)
                if i < 3:
                    extra[i] = jnp.where(sub == c, shifted(value[:, 0:1, :], -1), extra[i])
                    corner = jnp.where(lane_group == i, shifted(rim[:, 0:1, :], -1), corner)
                side = jnp.sum(jnp.where(lane_group == sub, rim, 0.0), 1, keepdims=True)
                extra[(i + 1) % 4] = jnp.where(sub == 4 + c, side, extra[(i + 1) % 4])
            extra[3] = jnp.where(sub == c, corner, extra[3])
            main = blocks_exchanged(main)
            for j in range(4):
                out_ref[:, 4 * q + j, 8 * c : 8 * c + 8, :] = main[j]
        extra = blocks_exchanged(extra)
        for j in range(4):
            out_ref[:, 4 * q + j, 32:40, :] = extra[j]


def middle(spectrum, in_z):
    table = tables()
    consts = [jnp.asarray(half) for name in ("forward_y", "forward_x", "back_x", "back_y") for half in table[name]]
    return pl.pallas_call(
        middle_kernel,
        out_shape=jax.ShapeDtypeStruct((8, 8, 40, 128), f32),
        in_specs=[pl.BlockSpec(memory_space=SMEM)] + vmem(11),
        out_specs=pl.BlockSpec(memory_space=VMEM),
        scratch_shapes=[
            VMEM((4, 256, 512), bf16),
            VMEM((4, 256, 512), bf16),
            VMEM((4, 256, 512), f32),
        ],
        compiler_params=pltpu.CompilerParams(vmem_limit_bytes=56 << 20),
        name="middle",
    )(in_z, spectrum.reshape(8, 8, 40, 128), *consts, jnp.asarray(table["column"]), jnp.asarray(table["row"]))


def force_kernel(list_ref, slots_ref, in_ref, bz_high, bz_low, out_ref, lines, field):
    out_ref[...] = jnp.zeros_like(out_ref)
    for pair in range(5):
        columns = []
        for group in (2 * pair, 2 * pair + 1):
            starts = [8 * c + group if group < 8 else 32 + c + 4 * (group - 8) for c in range(4)]
            columns.append(
                jnp.concatenate([in_ref[pl.ds(start, OWN, stride=40), :] for start in starts], 0)
            )
        high, rest = split(jnp.concatenate(columns, 1))
        result = dots(bz_high[...], bz_low[...], high, rest)
        lines[2 * pair] = result[:, :128]
        lines[2 * pair + 1] = result[:, 128:]

    lane = lane_of(2)
    low = lane < 64
    even = (lane // 32) % 2 == 0

    def regroup(chunk, carry):
        here = pl.ds(pl.multiple_of(chunk * 32, 32), 32)
        rim = lines[9, here, :]
        for group in range(9):
            main = lines[group, here, :]
            if group < 8:
                side = turn(rim, -4 * group)
            else:
                side = jnp.where(lane < 64, turn(main, -64), jnp.where(lane < 96, turn(main, -36), turn(main, -8)))
            pair_even = jnp.where(even, main, side)
            pair_odd = turn(jnp.where(even, side, main), -32)
            for part, value in enumerate((pair_even, pair_odd)):
                high = value.astype(bf16).astype(f32)
                rest = (value - high).astype(bf16).astype(f32)
                field[4 * group + part, here, :] = jnp.where(low, high, turn(rest, 64))
                field[4 * group + 2 + part, here, :] = jnp.where(low, turn(high, 64), rest)
        return carry

    lax.fori_loop(0, 8, regroup, 0)

    def wrap(plane, carry):
        field[plane, 256:264, :] = field[plane, 0:8, :]
        return carry

    lax.fori_loop(0, 36, wrap, 0)

    rows16 = lax.broadcasted_iota(jnp.int32, (16, 128), 0).astype(f32) - 1.0
    rows48 = lax.broadcasted_iota(jnp.int32, (48, 128), 0).astype(f32) - 1.0
    nothing = jnp.zeros((16, 256), f32)

    def one(item):
        slot = item >> 7
        tile_x = (item >> 5) & 3
        tile_z = item & 31
        charge = slots_ref[pl.ds(4 * slot, 1), :]
        at_x = slots_ref[pl.ds(4 * slot + 1, 1), :] - (8 * tile_x).astype(f32)
        at_y = slots_ref[pl.ds(4 * slot + 2, 1), :]
        at_z = slots_ref[pl.ds(4 * slot + 3, 1), :] - (8 * tile_z).astype(f32)
        weight_x, slope_x = bspline(rows16 - at_x, True)
        weight_z, slope_z = bspline(rows16 - at_z, True)
        along_y = jnp.concatenate(bspline(rows48 - at_y, True), 1)
        y_high = along_y.astype(bf16).astype(f32)
        y_low = along_y - y_high
        both = jnp.concatenate(
            [y_high, nothing, y_high, nothing, y_low, nothing, y_low, nothing], 0
        ).astype(bf16)
        base = pl.multiple_of(8 * tile_z, 8)
        window = jnp.concatenate(
            [field[8 * tile_x + i, pl.ds(base, 16), :] for i in range(11)], 0
        ).astype(bf16)
        out = jnp.dot(jnp.concatenate([window, window], 1), both, preferred_element_type=f32)
        plain = jnp.zeros((16, 128), f32)
        along_x = jnp.zeros((16, 128), f32)
        sloped = jnp.zeros((16, 128), f32)
        for i in range(11):
            value = out[16 * i : 16 * i + 16, :128]
            slope = out[16 * i : 16 * i + 16, 128:]
            plain = plain + weight_x[i : i + 1] * value
            along_x = along_x + slope_x[i : i + 1] * value
            sloped = sloped + weight_x[i : i + 1] * slope
        minus = -charge
        forces = [
            minus * jnp.sum(along_x * weight_z, 0, keepdims=True),
            minus * jnp.sum(sloped * weight_z, 0, keepdims=True),
            minus * jnp.sum(plain * slope_z, 0, keepdims=True),
        ]
        return slot, forces

    def put(slot, forces):
        for axis in range(3):
            out_ref[pl.ds(4 * slot + axis, 1), :] = forces[axis]

    def step(index, carry):
        first = one(list_ref[2 * index])
        second = one(list_ref[2 * index + 1])
        put(*first)
        put(*second)
        return carry

    lax.fori_loop(0, list_ref[255], step, 0)


def forces(listing, slots, potential):
    high, low = tables()["back_z"]
    return pl.pallas_call(
        force_kernel,
        out_shape=jax.ShapeDtypeStruct((8 * OWN, 128), f32),
        in_specs=[pl.BlockSpec(memory_space=SMEM)] + vmem(4),
        out_specs=pl.BlockSpec(memory_space=VMEM),
        scratch_shapes=[VMEM((10, 256, 128), f32), VMEM((36, 264, 128), f32)],
        compiler_params=pltpu.CompilerParams(vmem_limit_bytes=48 << 20),
        name="forces",
    )(listing, slots, potential, jnp.asarray(high), jnp.asarray(low))


def finish_kernel(owner_ref, back_ref, frac_ref, before_ref, after_ref, out_ref):
    chosen = jnp.where(targets(owner_ref[...]), 1.0, 0.0).astype(bf16)
    for axis in range(3):
        moved = sum(
            lax.dot_general(chosen, part, (((0,), (0,)), ((), ())), preferred_element_type=f32)
            for part in reversed(three(back_ref[pl.ds(axis, 2 * OWN, stride=4), :]))
        )
        spring = 2.0 * frac_ref[axis] - before_ref[axis] - after_ref[axis]
        out_ref[axis] = moved - spring_scale * spring


def finish(owner_row, back, frac, before, after):
    return pl.pallas_call(
        finish_kernel,
        out_shape=jax.ShapeDtypeStruct((3, OWN, 128), f32),
        in_specs=vmem(5),
        out_specs=pl.BlockSpec(memory_space=VMEM),
        name="finish",
    )(owner_row, back, frac, before, after)


def place(number, bead):
    return (number // 16, (number // 2) % 8, 2 * bead + number % 2)


def here():
    return lax.axis_index("bead"), lax.axis_index("px"), lax.axis_index("py")


def number_of(at):
    return at[0] * 16 + at[1] * 2 + at[2] % 2


def hop(step):
    return lax.rem(step * 37, OWN)


def block_kernel(src, dst, send_sem, recv_sem, own_sem):
    at = here()
    mine, bead = number_of(at), at[2] // 2
    barrier = pltpu.get_barrier_semaphore()

    def greet(step, carry):
        other = lax.rem(mine + hop(step), OWN)
        pl.semaphore_signal(barrier, inc=1, device_id=place(other, bead), device_id_type=MESH)
        return carry

    lax.fori_loop(1, OWN, greet, 0)
    pl.semaphore_wait(barrier, OWN - 1)
    own = pltpu.make_async_copy(src.at[mine], dst.at[mine], own_sem)
    own.start()

    def send(step, carry):
        other = lax.rem(mine + hop(step), OWN)
        pltpu.make_async_remote_copy(
            src_ref=src.at[other], dst_ref=dst.at[mine], send_sem=send_sem, recv_sem=recv_sem,
            device_id=place(other, bead), device_id_type=MESH,
        ).start()
        return carry

    lax.fori_loop(1, OWN, send, 0)
    own.wait()
    rest = pl.ds(0, OWN - 1)
    pltpu.make_async_copy(src.at[rest], dst.at[rest], send_sem).wait()
    pltpu.make_async_copy(src.at[rest], dst.at[rest], recv_sem).wait()


def route_kernel(outward, src, dst, send_sem, recv_sem, own_sem):
    at = here()
    number, chunk = number_of(at), at[1] * 8 + at[2]
    atoms_bead, grid_bead = at[0], at[2] // 2
    both = atoms_bead == grid_bead
    def grid_device(index):
        return place(index, atoms_bead)

    def atoms_device(index):
        return (grid_bead, index // 8, index % 8)

    if outward:
        to, to_self, mark, origin, from_self = grid_device, number, chunk, atoms_device, chunk
    else:
        to, to_self, mark, origin, from_self = atoms_device, chunk, number, grid_device, number
    barrier = pltpu.get_barrier_semaphore()

    def greet(step, carry):
        other = lax.rem(from_self + hop(step), OWN)
        pl.semaphore_signal(barrier, inc=1, device_id=origin(other), device_id_type=MESH)
        return carry

    def send(step, carry):
        other = lax.rem(to_self + hop(step), OWN)
        pltpu.make_async_remote_copy(
            src_ref=src.at[other], dst_ref=dst.at[mark], send_sem=send_sem, recv_sem=recv_sem,
            device_id=to(other), device_id_type=MESH,
        ).start()
        return carry

    def run(first):
        lax.fori_loop(first, OWN, greet, 0)
        pl.semaphore_wait(barrier, OWN - first)
        if first:
            own = pltpu.make_async_copy(src.at[to_self], dst.at[mark], own_sem)
            own.start()
        lax.fori_loop(first, OWN, send, 0)
        if first:
            own.wait()
        rest = pl.ds(0, OWN - first)
        pltpu.make_async_copy(src.at[rest], dst.at[rest], send_sem).wait()
        pltpu.make_async_copy(src.at[rest], dst.at[rest], recv_sem).wait()

    @pl.when(both)
    def _():
        run(1)

    @pl.when(jnp.logical_not(both))
    def _():
        run(0)


def transfer(kernel, value, rows, identity, name):
    return pl.pallas_call(
        kernel,
        out_shape=jax.ShapeDtypeStruct((OWN, rows, 128), f32),
        in_specs=[pl.BlockSpec(memory_space=pl.ANY)],
        out_specs=pl.BlockSpec(memory_space=pl.ANY),
        scratch_shapes=[pltpu.SemaphoreType.DMA] * 3,
        compiler_params=pltpu.CompilerParams(collective_id=identity, has_side_effects=True),
        name=name,
    )(value.reshape(OWN, rows, 128))


def local(block_owner, block_tile, atom_cell, atom_frac, charge, zone):
    owner_row = block_owner.reshape(1, OWN)
    frac = jnp.transpose(atom_frac[0], (1, 0, 2))
    beads = lax.axis_size("bead")
    before = lax.ppermute(frac, "bead", [(i, (i + 1) % beads) for i in range(beads)])
    after = lax.ppermute(frac, "bead", [((i + 1) % beads, i) for i in range(beads)])
    sent = pack(owner_row, block_tile.reshape(1, OWN), atom_cell, frac, charge, zone)
    slots = transfer(functools.partial(route_kernel, True), sent, 8, 0, "to_grid").reshape(8 * OWN, 128)
    lines, listing = spread(slots)
    spectrum = transfer(block_kernel, lines, 40, 1, "to_waves")
    number = lax.axis_index("bead") * 16 + lax.axis_index("px") * 2 + lax.axis_index("py") % 2
    in_z = lax.dynamic_index_in_dim(jnp.asarray(tables()["in_z"]), number, 0, keepdims=False)
    potential = middle(spectrum, in_z)
    potential = transfer(block_kernel, potential, 40, 1, "to_lines").reshape(OWN * 40, 128)
    force = forces(listing, slots, potential)
    back = transfer(functools.partial(route_kernel, False), force, 8, 2, "to_atoms").reshape(8 * OWN, 128)
    total = finish(owner_row, back, frac, before, after)
    return jnp.transpose(total, (1, 0, 2))[None]


def solution(mesh):
    return jax.shard_map(
        local,
        mesh=mesh,
        in_specs=(
            P(("px", "py"), None),
            P(("px", "py")),
            P(("px", "py"), None),
            P("bead", ("px", "py"), None, None),
            P(("px", "py"), None),
            P(("px", "py"), None),
        ),
        out_specs=P("bead", ("px", "py"), None, None),
        check_vma=False,
    )
```

time: 640 us -> 167 us (0.26); the launches traced: 630 us -> 167 us
  local copies, waits for them, and re-layouts: 307 us -> 7.72 us
  Pallas kernels: 0 us -> 156 us
  matrix products: 104 us -> 0 us
  waiting for transfers between devices: 98.5 us -> 0.01 us
  other arithmetic: 59.4 us -> 0 us
  starting transfers between devices: 41 us -> 3.31 us
  blocking collectives: 18.4 us -> 0 us
    pallas_call x0 -> x9, Pallas kernels: none -> 156 us  [the longest x4 112 us: transfer(): pl.pallas_call(kernel, out_shape=jax.ShapeDtypeStruct((OWN, rows, 128), f...]
    reshape x14 -> x0, local copies, waits for them, and re-layouts: 111 us -> none  [the longest x2 44 us: unfold(): lax.slice_in_dim(array, 0, tile_count * 8, axis=axis_pos)]
    dot_general x32 -> x0, matrix products: 104 us -> none  [the longest x4 22.1 us: interpolate(): lifted = jnp.einsum('sijl,sla->sija', values, weight_z, precision=highest)]
    all_to_all x5 -> x0, waiting for transfers between devices: 86.1 us -> none  [the longest x1 25.8 us: local(): lax.all_to_all(spectrum, 'py', split_axis=3, concat_axis=2, tiled=True)]
    slice x24 -> x0, local copies, waits for them, and re-layouts: 71.1 us -> none  [the longest x5 33.3 us: fold(): core_part = lax.slice_in_dim(array, 0, 8, axis=axis_pos + 1)]
    unnamed x31 -> x22, local copies, waits for them, and re-layouts: 44.2 us -> 6.47 us
    all_to_all x5 -> x0, starting transfers between devices: 32.5 us -> none  [the longest x1 13.2 us: local(): lax.all_to_all(outgoing, ('px', 'py'), split_axis=0, concat_axis=0, tiled...]
    add x19 -> x0, other arithmetic: 21.5 us -> none  [the longest x3 16.7 us: fold(): return jnp.pad(core_part, tail_pad) + moved]
  transfers between devices with their start and end apart: 11 -> 2, of which waited for: 9 -> 0; matrix products, arithmetic and copies ran while one was open for 1% -> 1% of each run, Pallas kernels for 0% -> 92%
where the time goes in v1:
time: 167 us
  Pallas kernels  156 us (93%)
  local copies, waits for them, and re-layouts  7.72 us (5%)
  starting transfers between devices  3.31 us (2%)
    pallas_call x4, Pallas kernels, transfer(): pl.pallas_call(kernel, out_shape=jax.ShapeDtypeStruct((OWN, rows, 128), f...  112 us
    pallas_call x1, Pallas kernels, middle(): pl.pallas_call(middle_kernel, out_shape=jax.ShapeDtypeStruct((8, 8, 40, 1...  14.8 us
    pallas_call x1, Pallas kernels, spread(): pl.pallas_call(spread_kernel, out_shape=[jax.ShapeDtypeStruct((OWN * 40,...  12.6 us
    pallas_call x1, Pallas kernels, forces(): pl.pallas_call(force_kernel, out_shape=jax.ShapeDtypeStruct((8 * OWN, 128...  11.6 us
    unnamed x22, local copies, waits for them, and re-layouts  6.47 us
  transfers between devices with their start and end apart: 2, of which 0 were waited for; matrix products, arithmetic and copies ran while one was open for 1% of the time, Pallas kernels for 92%

profile of v1, /device:TPU:1, one launch (start us, length us, event | category | flops | bytes accessed | tf_op | source)
XLA Modules:
  0.0 166.8 jit_solution(3902571861397050909)
XLA Ops:
  0.0 2.0 %collective-permute-start = (f32[3,64,128]{2,1,0:T(8,128)}, f32[3,64,128]{2,1,0:T(8,128)S(1)}, u32[]{:S(2)}, u32[]{:S(2)}) collective-permute-start(f32[3,64,128]{2,1,0:T(8,128)} %bitcast.27), channel_id=1, source_target_pairs={{0,64},{64,128},{128,192},{192,0},{1,65},{65,129},{129,193},{193,1... | collective-permute-start | bytes 294920 | tf_op jit(solution)/shard_map/ppermute | solution.py:690
  2.0 1.3 collective-permute-start.1
  3.3 2.0 %pack.1 = f32[512,128]{1,0:T(8,128)} custom-call(s32[1,64]{1,0:T(1,128)} %bitcast.31, s32[1,64]{1,0:T(1,128)} %bitcast.33, s32[64,128]{1,0:T(8,128)} %cell_ref.1, f32[3,64,128]{2,1,0:T(8,128)} %bitcast.29, f32[64,128]{1,0:T(8,128)} %charge_ref.1, s32[64,128]{1,0:T(8,128)} %zone_ref.1), custom_call_target="tpu_custom_call" | custom-call | tf_op jit(solution)/shard_map/pack/pallas_call | solution.py:179
  5.3 28.0 %to_grid.1 = f32[64,8,128]{2,1,0:T(8,128)} custom-call(f32[64,8,128]{2,1,0:T(8,128)} %bitcast.25), custom_call_target="tpu_custom_call" | custom-call | tf_op jit(solution)/shard_map/to_grid/pallas_call | solution.py:675
  33.3 0.0 copy-start.1
  33.4 0.9 copy-done.1
  34.3 0.0 copy-start.5
  34.3 0.9 copy-done.5
  35.2 0.0 copy-start.6
  35.2 0.9 copy-done.6
  36.1 12.6 %spread.1 = (f32[2560,128]{1,0:T(8,128)S(1)}, s32[256]{0:T(256)S(1)}) custom-call(f32[512,128]{1,0:T(8,128)S(1)} %bitcast.19, bf16[256,256]{1,0:T(8,128)(2,1)S(1)} %copy-done.5, bf16[256,256]{1,0:T(8,128)(2,1)S(1)} %copy-done.6), custom_call_target="tpu_custom_call" | custom-call | tf_op jit(solution)/shard_map/spread/pallas_call | solution.py:314
  48.7 0.0 copy-start.3
  48.7 1.1 copy-done.3
  49.8 30.4 %to_waves.1 = f32[64,40,128]{2,1,0:T(8,128)} custom-call(f32[64,40,128]{2,1,0:T(8,128)} %bitcast.21), custom_call_target="tpu_custom_call" | custom-call | tf_op jit(solution)/shard_map/to_waves/pallas_call | solution.py:675
  80.2 1.2 dynamic-slice_bitcast_fusion.in_z
  81.5 14.8 %middle.1 = f32[8,8,40,128]{3,2,1,0:T(8,128)} custom-call(f32[2,2]{1,0:T(2,128)} %dynamic-slice_bitcast_fusion.in_z, f32[8,8,40,128]{3,2,1,0:T(8,128)} %bitcast.23, bf16[512,512]{1,0:T(8,128)(2,1)} %constant.65.clone.fy_high, bf16[512,512]{1,0:T(8,128)(2,1)} %constant.66.clone.fy_low, bf16[512,256]{1,0:T(8,128)(2,1)} %constant.67.clone.fx_high, ...), custom_call_target="tpu_custom_call" | custom-call | tf_op jit(solution)/shard_map/middle/pallas_call | solution.py:427
  96.3 0.0 copy-start.2
  96.3 0.0 copy-start.7
  96.3 0.0 copy-start.8
  96.3 24.5 %to_lines.1 = f32[64,40,128]{2,1,0:T(8,128)} custom-call(f32[64,40,128]{2,1,0:T(8,128)} %bitcast.24), custom_call_target="tpu_custom_call" | custom-call | tf_op jit(solution)/shard_map/to_lines/pallas_call | solution.py:675
  120.9 0.0 copy-done.2
  120.9 0.0 copy-done.7
  120.9 0.0 copy-done.8
  120.9 0.0 copy-start
  120.9 1.3 copy-done
  122.2 11.6 %forces.1 = f32[512,128]{1,0:T(8,128)S(1)} custom-call(s32[256]{0:T(256)S(1)} %get-tuple-element.7.list_ref, f32[512,128]{1,0:T(8,128)S(1)} %bitcast.20, f32[2560,128]{1,0:T(8,128)S(1)} %bitcast.18, bf16[256,256]{1,0:T(8,128)(2,1)S(1)} %copy-done.7, bf16[256,256]{1,0:T(8,128)(2,1)S(1)} %copy-done.8), custom_call_target="tpu_custom_call" | custom-call | tf_op jit(solution)/shard_map/forces/pallas_call | solution.py:544
  133.8 0.0 copy-start.4
  133.8 0.7 copy-done.4
  134.5 29.5 %to_atoms.1 = f32[64,8,128]{2,1,0:T(8,128)} custom-call(f32[64,8,128]{2,1,0:T(8,128)} %bitcast.22), custom_call_target="tpu_custom_call" | custom-call | tf_op jit(solution)/shard_map/to_atoms/pallas_call | solution.py:675
  164.0 0.0 collective-permute-done.before_ref
  164.0 0.0 copy-start.9
  164.0 0.0 collective-permute-done.1.after_ref
  164.0 0.0 copy-start.10
  164.0 0.6 copy-done.9
  164.6 0.1 copy-done.10
  164.7 2.1 %finish.1 = f32[3,64,128]{2,1,0:T(8,128)} custom-call(s32[1,64]{1,0:T(1,128)} %bitcast.32, f32[512,128]{1,0:T(8,128)} %bitcast.26, f32[3,64,128]{2,1,0:T(8,128)} %bitcast.30, f32[3,64,128]{2,1,0:T(8,128)} %copy-done.9, f32[3,64,128]{2,1,0:T(8,128)} %copy-done.10), custom_call_target="tpu_custom_call" | custom-call | tf_op jit(solution)/shard_map/finish/pallas_call | solution.py:567
Async XLA Ops:
  0.0 164.0 %collective-permute-start = (f32[3,64,128]{2,1,0:T(8,128)}, f32[3,64,128]{2,1,0:T(8,128)S(1)}, u32[]{:S(2)}, u32[]{:S(2)}) collective-permute-start(f32[3,64,128]{2,1,0:T(8,128)} %bitcast.27), channel_id=1, source_target_pairs={{0,64},{64,128},{128,192},{192,0},{1,65},{65,129},{129,193},{193,1... | collective-permute-start | bytes 294920 | tf_op jit(solution)/shard_map/ppermute | solution.py:690
  2.0 162.0 %collective-permute-start.1 = (f32[3,64,128]{2,1,0:T(8,128)}, f32[3,64,128]{2,1,0:T(8,128)S(1)}, u32[]{:S(2)}, u32[]{:S(2)}) collective-permute-start(f32[3,64,128]{2,1,0:T(8,128)} %bitcast.28), channel_id=1, source_target_pairs={{64,0},{128,64},{192,128},{0,192},{65,1},{129,65},{193,129},{1,193... | collective-permute-start | bytes 294920 | tf_op jit(solution)/shard_map/ppermute | solution.py:691
  33.3 1.0 copy-start.1
  34.3 0.9 copy-start.5
  35.2 0.9 copy-start.6
  48.7 1.1 copy-start.3
  96.3 24.5 %copy-start.2 = (f32[64,8,128]{2,1,0:T(8,128)S(1)}, f32[64,8,128]{2,1,0:T(8,128)}, u32[]{:S(2)}) copy-start(f32[64,8,128]{2,1,0:T(8,128)} %to_grid.1) | copy-start | bytes 786436
  96.3 24.6 %copy-start.7 = (bf16[256,256]{1,0:T(8,128)(2,1)S(1)}, bf16[256,256]{1,0:T(8,128)(2,1)}, u32[]{:S(2)}) copy-start(bf16[256,256]{1,0:T(8,128)(2,1)} %constant.75.clone.bz_high) | copy-start | bytes 393220
  96.3 24.6 %copy-start.8 = (bf16[256,256]{1,0:T(8,128)(2,1)S(1)}, bf16[256,256]{1,0:T(8,128)(2,1)}, u32[]{:S(2)}) copy-start(bf16[256,256]{1,0:T(8,128)(2,1)} %constant.76.clone.bz_low) | copy-start | bytes 393220
  120.9 1.3 copy-start
  133.8 0.7 copy-start.4
  164.0 0.6 copy-start.9
  164.0 0.7 copy-start.10

commit v2 on v1

v2 whole, which is shorter than its diff:
```python
import functools
import math

import jax
import jax.numpy as jnp
import ml_dtypes
import numpy as np
from jax import lax
from jax.experimental import pallas as pl
from jax.experimental.pallas import tpu as pltpu
from jax.sharding import PartitionSpec as P

NG = 256
OWN = 64
f32 = jnp.float32
bf16 = jnp.bfloat16
MESH = pl.DeviceIdType.MESH
VMEM = pltpu.VMEM
SMEM = pltpu.SMEM
ewald_beta = 0.75
spring_scale = 0.25


def halves(table):
    table = table.astype(np.float32)
    high = table.astype(ml_dtypes.bfloat16)
    low = (table - high.astype(np.float32)).astype(ml_dtypes.bfloat16)
    return high, low


def waves(rows, columns):
    angle = (np.outer(rows, columns) % NG) * (2.0 * math.pi / NG)
    return np.cos(angle), np.sin(angle)


@functools.lru_cache(None)
def tables():
    whole = np.arange(NG)
    owner = np.arange(OWN)
    kz = np.stack([2 * owner, 2 * owner + 1])
    cos_z, sin_z = waves(kz.reshape(-1), whole)
    forward_z = np.concatenate([cos_z[:OWN], -sin_z[:OWN], cos_z[OWN:], -sin_z[OWN:]])
    scale = np.where(kz == 0, 1.0, 2.0) / float(NG**3)
    scale = np.repeat(scale, 2, 0).reshape(-1)
    back_z = (forward_z * scale[:, None]).T
    main = whole
    rim = np.arange(256)
    rim = 32 * (rim // 32 + 1) + rim % 4
    cos_y, sin_y = waves(np.concatenate([main, rim]), whole)
    forward_y = np.concatenate([cos_y, sin_y], 1)
    back_y = np.concatenate([cos_y.T, sin_y.T], 1)
    step, block, group = np.meshgrid(np.arange(4), np.arange(8), np.arange(8), indexing="ij")
    place = (32 * block + 4 * group + step).reshape(-1)
    cos_x, sin_x = waves(whole, place)
    forward_x = np.concatenate([cos_x, sin_x])
    back_x = np.concatenate([cos_x.T, sin_x.T])
    wave = (whole + NG // 2) % NG - NG // 2
    theta = wave * (2.0 * math.pi / NG)
    factor = (6.0 / (4.0 + 2.0 * np.cos(theta))) ** 2
    factor = factor * np.exp(-theta * theta / (4.0 * ewald_beta * ewald_beta))
    column = np.zeros((256, 128), np.float32)
    column[:, 0], column[:, 1] = theta * theta, factor
    row = np.zeros((8, 256), np.float32)
    row[0], row[1] = theta * theta, factor
    in_z = np.stack([(theta * theta)[kz.T], factor[kz.T]], 1).astype(np.float32).reshape(-1)
    return dict(
        forward_z=halves(forward_z),
        back_z=halves(back_z),
        forward_y=halves(forward_y),
        back_y=halves(back_y),
        forward_x=halves(forward_x),
        back_x=halves(back_x),
        column=column,
        row=row,
        in_z=in_z,
    )


def split(value):
    high = value.astype(bf16)
    return high, (value - high.astype(f32)).astype(bf16)


def dots(a_high, a_low, b_high, b_low):
    dot = functools.partial(jnp.dot, preferred_element_type=f32)
    return dot(a_high, b_high) + (dot(a_high, b_low) + dot(a_low, b_high))


def lane_of(rank):
    return lax.broadcasted_iota(jnp.int32, (1,) * (rank - 1) + (128,), rank - 1)


def turn(value, steps):
    steps = steps % 128
    if steps == 0:
        return value
    flat = value.reshape(-1, 128)
    return pltpu.roll(flat, steps, 1).reshape(value.shape)


def blocks_exchanged(parts):
    lane = lane_of(parts[0].ndim)
    low = lane < 64
    even = (lane // 32) % 2 == 0
    first = [
        jnp.where(low, parts[0], turn(parts[2], 64)),
        jnp.where(low, parts[1], turn(parts[3], 64)),
        jnp.where(low, turn(parts[0], 64), parts[2]),
        jnp.where(low, turn(parts[1], 64), parts[3]),
    ]
    return [
        jnp.where(even, first[0], turn(first[1], 32)),
        jnp.where(even, turn(first[0], 96), first[1]),
        jnp.where(even, first[2], turn(first[3], 32)),
        jnp.where(even, turn(first[2], 96), first[3]),
    ]


def bspline(offsets, slopes):
    v = jnp.abs(offsets)
    a = jnp.maximum(2.0 - v, 0.0)
    b = jnp.maximum(1.0 - v, 0.0)
    aa = a * a
    bb = b * b
    weight = aa * a * (1.0 / 6.0) - bb * b * (4.0 / 6.0)
    if not slopes:
        return weight
    half = 0.5 * aa - 2.0 * bb
    return weight, jnp.where(offsets < 0.0, -half, half)


def vmem(count):
    return [pl.BlockSpec(memory_space=VMEM)] * count


def targets(owner_row, apart):
    blocks = owner_row.shape[1]
    up = lax.broadcasted_iota(jnp.int32, (blocks, blocks), 0)
    across = lax.broadcasted_iota(jnp.int32, (blocks, blocks), 1)
    owner_column = jnp.sum(jnp.where(up == across, owner_row, 0).astype(f32), 1, keepdims=True)
    owner_float = owner_row.astype(f32)
    before = jnp.where((owner_column == owner_float) & (up < across), 1.0, 0.0)
    rank = jnp.sum(before, 0, keepdims=True)
    target = owner_float + OWN * rank if apart else 2.0 * owner_float + rank
    slot = lax.broadcasted_iota(jnp.int32, (2 * OWN, blocks), 0).astype(f32)
    return slot == target


def three(value):
    high = value.astype(bf16)
    rest = value - high.astype(f32)
    middle = rest.astype(bf16)
    return high, middle, (rest - middle.astype(f32)).astype(bf16)


def remote(src, dst, send_sem, recv_sem, device):
    return pltpu.make_async_remote_copy(
        src_ref=src, dst_ref=dst, send_sem=send_sem, recv_sem=recv_sem,
        device_id=device, device_id_type=MESH,
    )


def settle(ref, sem):
    pltpu.make_async_copy(ref, ref, sem).wait()


def atoms_kernel(
    owner_ref, tile_ref, cell_ref, frac_ref, charge_ref, zone_ref, slots_ref, before_ref, after_ref,
    payload, stage, stage_send, stage_recv, send_sem, recv_sem, own_sem, bead_send, bead_recv,
):
    bead, px, py = here()
    chunk = px * 8 + py
    barrier = pltpu.get_barrier_semaphore()

    def greet(step, carry):
        other = lax.rem(chunk + step, OWN)
        pl.semaphore_signal(barrier, inc=1, device_id=(bead, other // 8, other % 8), device_id_type=MESH)
        return carry

    lax.fori_loop(1, OWN, greet, 0)
    for step in range(1, 4):
        pl.semaphore_signal(barrier, inc=1, device_id=(lax.rem(bead + step, 4), px, py), device_id_type=MESH)

    chosen = jnp.where(targets(owner_ref[...], False), 1.0, 0.0).astype(bf16)
    blocks = cell_ref.shape[0]
    up = lax.broadcasted_iota(jnp.int32, (blocks, blocks), 0)
    across = lax.broadcasted_iota(jnp.int32, (blocks, blocks), 1)
    tile = jnp.sum(jnp.where(up == across, tile_ref[...], 0).astype(f32), 1, keepdims=True)
    tile = tile.astype(jnp.int32)
    cell = cell_ref[...]
    corners = [tile >> 7, (tile >> 5) & 3, tile & 31]
    cells = [cell >> 6, (cell >> 3) & 7, cell & 7]
    fields = [charge_ref[...] * zone_ref[...].astype(f32)]
    for axis in range(3):
        base = (corners[axis] * 8).astype(f32)
        inside = cells[axis].astype(f32) + frac_ref[axis]
        fields.append(base + jnp.minimum(inside, 8.0 - 2.0**-16))
    for place_in, field in enumerate(fields):
        parts = three(field)
        moved = sum(
            jnp.dot(chosen, part, preferred_element_type=f32) for part in reversed(parts)
        )
        payload[pl.ds(place_in, 2 * OWN, stride=4), :] = moved

    pl.semaphore_wait(barrier, OWN - 1 + 3)
    staged = [
        remote(
            payload.at[pl.ds(pl.multiple_of(lax.rem(bead + step, 4) * 128, 128), 128)], stage.at[bead],
            stage_send.at[step - 1], stage_recv.at[step - 1], (lax.rem(bead + step, 4), px, py),
        )
        for step in (1, 3, 2)
    ]
    for copy in staged:
        copy.start()
    springs = [
        remote(frac_ref, target, bead_send.at[i], bead_recv.at[i], (lax.rem(bead + step, 4), px, py))
        for i, (target, step) in enumerate(((before_ref, 1), (after_ref, 3)))
    ]

    mark = pl.ds(pl.multiple_of(chunk * 8, 8), 8)

    def deliver(source, from_bead):
        def send(step, carry):
            j = lax.rem(step + 2 * px + 1, 16)
            device = (bead, j // 2, 2 * from_bead + j % 2)
            mine = jnp.logical_and(j == 2 * px + py % 2, py // 2 == from_bead)
            piece = source(j)

            @pl.when(jnp.logical_not(mine))
            def _():
                remote(piece, slots_ref.at[mark], send_sem, recv_sem, device).start()

            @pl.when(mine)
            def _():
                pltpu.make_async_copy(piece, slots_ref.at[mark], own_sem).start()

            return carry

        lax.fori_loop(0, 16, send, 0)

    deliver(lambda j: payload.at[pl.ds(pl.multiple_of(bead * 128 + j * 8, 8), 8)], bead)
    for copy in springs:
        copy.start()
    for step, copy in zip((1, 3, 2), staged):
        copy.wait_recv()
        other = lax.rem(bead + 4 - step, 4)
        deliver(lambda j: stage.at[other, pl.ds(pl.multiple_of(j * 8, 8), 8)], other)
    settle(slots_ref.at[mark], own_sem)
    rest = pl.ds(0, 8 * OWN - 8)
    settle(slots_ref.at[rest], recv_sem)
    settle(slots_ref.at[rest], send_sem)
    for copy in staged:
        copy.wait_send()
    for copy in springs:
        copy.wait()


def atoms_to_slots(owner_row, tile_row, cell, frac, charge, zone):
    shape = jax.ShapeDtypeStruct((3, OWN, 128), f32)
    dma = pltpu.SemaphoreType.DMA
    return pl.pallas_call(
        atoms_kernel,
        out_shape=[jax.ShapeDtypeStruct((8 * OWN, 128), f32), shape, shape],
        in_specs=vmem(6),
        out_specs=vmem(3),
        scratch_shapes=[
            VMEM((8 * OWN, 128), f32), VMEM((4, 128, 128), f32),
            dma((3,)), dma((3,)), dma, dma, dma, dma((2,)), dma((2,)),
        ],
        compiler_params=pltpu.CompilerParams(collective_id=0, has_side_effects=True),
        name="atoms_to_slots",
    )(owner_row, tile_row, cell, frac, charge, zone)


def slot_list(slots_ref, list_ref, codes, codes_scalar, sem):
    charge = slots_ref[pl.ds(0, 2 * OWN, stride=4), :]
    along_x = slots_ref[pl.ds(1, 2 * OWN, stride=4), :]
    along_z = slots_ref[pl.ds(3, 2 * OWN, stride=4), :]
    tile_x = (jnp.max(along_x, 1, keepdims=True) * 0.125).astype(jnp.int32)
    tile_z = (jnp.max(along_z, 1, keepdims=True) * 0.125).astype(jnp.int32)
    filled = jnp.max(jnp.abs(charge), 1, keepdims=True) > 0.0
    up = lax.broadcasted_iota(jnp.int32, (128, 128), 0)
    across = lax.broadcasted_iota(jnp.int32, (128, 128), 1)
    sub = lax.broadcasted_iota(jnp.int32, (8, 128), 0)
    value = jnp.zeros((8, 128), f32)
    columns = (256 * tile_x + tile_z, 8 * tile_x, 8 * tile_z, filled.astype(jnp.int32))
    for place_in, column in enumerate(columns):
        row = jnp.sum(jnp.where(up == across, column.astype(f32), 0.0), 0, keepdims=True)
        value = jnp.where(sub == place_in, row, value)
    codes[...] = value.astype(jnp.int32)
    copy = pltpu.make_async_copy(codes, codes_scalar, sem)
    copy.start()
    copy.wait()

    def step(slot, carry):
        count, empty = carry
        held = codes_scalar[3, slot] > 0
        list_ref[count] = slot
        return count + held.astype(jnp.int32), jnp.where(held, empty, slot)

    count, empty = lax.fori_loop(0, 2 * OWN, step, (jnp.int32(0), jnp.int32(0)))
    for k in range(3):
        list_ref[count + k] = empty
    list_ref[255] = (count + 3) // 4


def spread_kernel(slots_ref, out_ref, codes_scalar, list_ref, density, codes, sem):
    slot_list(slots_ref, list_ref, codes, codes_scalar, sem)
    density[...] = jnp.zeros_like(density)
    rows16 = lax.broadcasted_iota(jnp.int32, (16, 128), 0).astype(f32) - 1.0
    rows40 = lax.broadcasted_iota(jnp.int32, (40, 128), 0).astype(f32) - 1.0
    nothing = jnp.zeros((24, 128), f32)

    def one(slot):
        plane_x, row_z = codes_scalar[1, slot], codes_scalar[2, slot]
        charge = slots_ref[pl.ds(4 * slot, 1), :]
        at_x = slots_ref[pl.ds(4 * slot + 1, 1), :] - plane_x.astype(f32)
        at_y = slots_ref[pl.ds(4 * slot + 2, 1), :]
        at_z = slots_ref[pl.ds(4 * slot + 3, 1), :] - row_z.astype(f32)
        weight_x = bspline(rows16 - at_x, False) * charge
        weight_z = bspline(rows16 - at_z, False)
        weight_y = bspline(rows40 - at_y, False)
        plane = jnp.concatenate([weight_x[i : i + 1] * weight_z for i in range(11)], 0)
        plane = jnp.concatenate(split(plane), 1)
        y_high = weight_y.astype(bf16).astype(f32)
        y_low = weight_y - y_high
        left = jnp.concatenate([y_high, nothing, y_low, nothing], 0)
        right = jnp.concatenate([y_high, nothing, jnp.zeros((64, 128), f32)], 0)
        both = jnp.concatenate([left, right], 1).astype(bf16)
        out = lax.dot_general(plane, both, (((1,), (1,)), ((), ())), preferred_element_type=f32)
        return plane_x, row_z, out

    def put(plane_x, row_z, out):
        base = pl.multiple_of(row_z, 8)
        for i in range(11):
            density[plane_x + i, pl.ds(base, 16), :] += out[16 * i : 16 * i + 16]

    def step(index, carry):
        for found in [one(list_ref[4 * index + k]) for k in range(4)]:
            put(*found)
        return carry

    lax.fori_loop(0, list_ref[255], step, 0)

    lane = lane_of(2)
    low = lane < 64
    even = (lane // 32) % 2 == 0

    def fold(plane, carry):
        density[plane, 0:8, :] += density[plane, 256:264, :]
        return carry

    lax.fori_loop(0, 36, fold, 0)

    def regroup(chunk, carry):
        here = pl.ds(pl.multiple_of(chunk * 32, 32), 32)
        rim = jnp.zeros((32, 128), f32)

        def keep(group, value):
            out_ref[group, here, :] = value

        for group in range(9):
            four = [density[4 * group + i, here, :] for i in range(4)]
            pair_even = jnp.where(low, four[0], four[2]) + turn(jnp.where(low, four[2], four[0]), 64)
            pair_odd = jnp.where(low, four[1], four[3]) + turn(jnp.where(low, four[3], four[1]), 64)
            pair_odd = turn(pair_odd, 32)
            main = jnp.where(even, pair_even, pair_odd)
            side = jnp.where(even, pair_odd, pair_even)
            if group < 8:
                keep(group, main)
                rim = rim + turn(side, 4 * group)
            else:
                last = lane >= 96
                corner = jnp.where((lane >= 96) & (lane < 100), turn(side, 64), 0.0)
                corner = jnp.where((lane >= 100) & (lane < 104), turn(side, 36), corner)
                corner = jnp.where((lane >= 104) & (lane < 108), turn(side, 8), corner)
                keep(8, jnp.where(last, corner, main))
        keep(9, rim)
        return carry

    lax.fori_loop(0, 8, regroup, 0)


def spread(slots):
    return pl.pallas_call(
        spread_kernel,
        out_shape=[
            jax.ShapeDtypeStruct((10, 256, 128), f32),
            jax.ShapeDtypeStruct((8, 128), jnp.int32),
        ],
        in_specs=vmem(1),
        out_specs=[pl.BlockSpec(memory_space=VMEM), pl.BlockSpec(memory_space=SMEM)],
        scratch_shapes=[
            SMEM((256,), jnp.int32),
            VMEM((36, 264, 128), f32),
            VMEM((8, 128), jnp.int32),
            pltpu.SemaphoreType.DMA,
        ],
        compiler_params=pltpu.CompilerParams(vmem_limit_bytes=24 << 20),
        name="spread",
    )(slots)


TABLES = ("forward_z", "forward_y", "forward_x", "back_x", "back_y", "back_z")
ROWS_OF = (0, 8, 24, 32)


def here():
    return lax.axis_index("bead"), lax.axis_index("px"), lax.axis_index("py")


def place(number, bead):
    return (number // 16, (number // 2) % 8, 2 * bead + number % 2)


def hop(step):
    return lax.rem(step * 37, OWN)


def shifted(value, steps):
    if steps == 1:
        return jnp.concatenate([value[7:8], value[0:7]], 0)
    return jnp.concatenate([value[1:8], value[0:1]], 0)


def wave_kernel(
    codes, in_z, packed, slots_ref, owner_ref, frac_ref, before_ref, after_ref, column_ref, row_ref,
    *rest,
):
    table_refs, rest = rest[:12], rest[12:]
    out_ref, rest = rest[0], rest[1:]
    table_vmem, rest = rest[:12], rest[12:]
    (
        lines, waves_in, waves_out, lines_in, plane_high, plane_low, rims, rims_out,
        lines_z, field, force, force_in, table_sem, out_send, out_recv, back_send, back_recv,
        own_sem, force_send, force_recv,
    ) = rest
    (fz, fy, fx, bx, by, bz) = [(table_vmem[2 * i], table_vmem[2 * i + 1]) for i in range(6)]
    bead, px, py = here()
    mine, grid_bead, chunk = bead * 16 + px * 2 + py % 2, py // 2, px * 8 + py
    same = bead == grid_bead
    barrier = pltpu.get_barrier_semaphore()

    def greet(step, carry):
        other = lax.rem(mine + hop(step), OWN)
        pl.semaphore_signal(barrier, inc=1, device_id=place(other, grid_bead), device_id_type=MESH)
        return carry

    def greet_atoms(step, carry):
        other = lax.rem(mine + hop(step), OWN)
        pl.semaphore_signal(barrier, inc=1, device_id=place(other, bead), device_id_type=MESH)
        return carry

    lax.fori_loop(1, OWN, greet, 0)

    @pl.when(same)
    def _():
        lax.fori_loop(1, OWN, greet_atoms, 0)

    @pl.when(jnp.logical_not(same))
    def _():
        lax.fori_loop(0, OWN, greet_atoms, 0)

    table_copies = [
        pltpu.make_async_copy(table_refs[i], table_vmem[i], table_sem.at[i]) for i in range(12)
    ]
    for copy in table_copies:
        copy.start()
    table_copies[0].wait()
    table_copies[1].wait()

    for pair in range(5):
        high, low = split(jnp.concatenate([packed[2 * pair], packed[2 * pair + 1]], 1))
        result = dots(fz[0][...], fz[1][...], high, low)
        for part in range(2):
            group = 2 * pair + part
            for c in range(4):
                start = ROWS_OF[c] + group if group < 8 else 16 + c + 4 * (group - 8)
                lines[:, start, :] = result[64 * c : 64 * c + 64, 128 * part : 128 * part + 128]

    pl.semaphore_wait(barrier, 2 * OWN - 1 - same.astype(jnp.int32))

    def own(src, dst, rows, sem):
        return pltpu.make_async_copy(src.at[mine, rows], dst.at[mine, rows], sem)

    def send_all(src, dst, rows, send_sem, recv_sem):
        def send(step, carry):
            other = lax.rem(mine + hop(step), OWN)
            remote(
                src.at[other, rows], dst.at[mine, rows], send_sem, recv_sem, place(other, grid_bead)
            ).start()
            return carry

        lax.fori_loop(1, OWN, send, 0)

    rest = pl.ds(0, OWN - 1)
    out_rows = (pl.ds(0, 24), pl.ds(24, 16))
    back_rows = (pl.ds(0, 16), pl.ds(16, 24))
    for n in range(2):
        own(lines, waves_in, out_rows[n], own_sem.at[n]).start()
        send_all(lines, waves_in, out_rows[n], out_send.at[n], out_recv.at[n])

    for copy in table_copies[2:]:
        copy.wait()

    lane = lane_of(3)
    sub = lax.broadcasted_iota(jnp.int32, (1, 8, 128), 1)
    lane_group = (lane // 4) % 8
    column = column_ref[...]
    row = row_ref[...]

    for n in range(2):
        own(lines, waves_in, out_rows[n], own_sem.at[n]).wait()
        settle(waves_in.at[rest, out_rows[n]], out_recv.at[n])
        for q in range(2):
            if n == 0:
                extra = blocks_exchanged(
                    [waves_in[pl.ds(4 * q + j, 8, stride=8), 16:24, :] for j in range(4)]
                )
                for i in range(4):
                    rims[q, i] = extra[i]
            else:
                extra = [rims[q, i] for i in range(4)]
            for half in range(2):
                c = 2 * n + half
                main = blocks_exchanged(
                    [
                        waves_in[pl.ds(4 * q + j, 8, stride=8), ROWS_OF[c] : ROWS_OF[c] + 8, :]
                        for j in range(4)
                    ]
                )
                for i in range(4):
                    value = main[i]
                    rim = jnp.where(lane_group == sub, extra[(i + 1) % 4][:, 4 + c : 5 + c, :], 0.0)
                    if i < 3:
                        value = value + jnp.where(sub == 0, shifted(extra[i][:, c : c + 1, :], 1), 0.0)
                        corner = shifted(extra[3][:, c : c + 1, :], 1)
                        rim = rim + jnp.where((sub == 0) & (lane_group == i), corner, 0.0)
                    for part, array in enumerate((value, rim)):
                        high, low = split(array.reshape(64, 128))
                        start = 256 * part + 128 * q
                        plane_high[half, 64 * i : 64 * i + 64, start : start + 128] = high
                        plane_low[half, 64 * i : 64 * i + 64, start : start + 128] = low

        real = dots(plane_high[0], plane_low[0], fy[0][...], fy[1][...])
        imag = dots(plane_high[1], plane_low[1], fy[0][...], fy[1][...])
        spec = jnp.concatenate(
            [real[:, :256] + imag[:, 256:], imag[:, :256] - real[:, 256:]], 1
        )
        both = dots(fx[0][...], fx[1][...], *split(spec))
        square = column[:, 0:1] + row[0:1, :] + in_z[4 * mine + n]
        green = column[:, 1:2] * row[1:2, :] * (in_z[4 * mine + 2 + n] * (4.0 * math.pi))
        green = jnp.where(square > 0.0, green / jnp.where(square > 0.0, square, 1.0), 0.0)
        spec = jnp.concatenate(
            [
                (both[:256, :256] + both[256:, 256:]) * green,
                (both[:256, 256:] - both[256:, :256]) * green,
            ],
            1,
        )
        both = dots(bx[0][...], bx[1][...], *split(spec))
        spec = jnp.concatenate(
            [both[:256, :256] - both[256:, 256:], both[:256, 256:] + both[256:, :256]], 0
        )
        both = dots(*split(spec), by[0][...], by[1][...])
        back = [both[:256, :512] - both[256:, 512:], both[256:, :512] + both[:256, 512:]]

        for q in range(2):
            if n == 0:
                extra = [jnp.zeros((8, 8, 128), f32) for _ in range(4)]
            else:
                extra = [rims_out[q, i] for i in range(4)]
            for half in range(2):
                c = 2 * n + half
                main, corner = [], jnp.zeros((8, 1, 128), f32)
                for i in range(4):
                    lines_of = slice(64 * i, 64 * i + 64)
                    value = back[half][lines_of, 128 * q : 128 * q + 128].reshape(8, 8, 128)
                    rim = back[half][lines_of, 256 + 128 * q : 384 + 128 * q].reshape(8, 8, 128)
                    main.append(value)
                    if i < 3:
                        extra[i] = jnp.where(sub == c, shifted(value[:, 0:1, :], -1), extra[i])
                        corner = jnp.where(lane_group == i, shifted(rim[:, 0:1, :], -1), corner)
                    side = jnp.sum(jnp.where(lane_group == sub, rim, 0.0), 1, keepdims=True)
                    extra[(i + 1) % 4] = jnp.where(sub == 4 + c, side, extra[(i + 1) % 4])
                extra[3] = jnp.where(sub == c, corner, extra[3])
                main = blocks_exchanged(main)
                for j in range(4):
                    waves_out[pl.ds(4 * q + j, 8, stride=8), ROWS_OF[c] : ROWS_OF[c] + 8, :] = main[j]
            if n == 0:
                for i in range(4):
                    rims_out[q, i] = extra[i]
            else:
                extra = blocks_exchanged(extra)
                for j in range(4):
                    waves_out[pl.ds(4 * q + j, 8, stride=8), 16:24, :] = extra[j]
        own(waves_out, lines_in, back_rows[n], own_sem.at[2 + n]).start()
        send_all(waves_out, lines_in, back_rows[n], back_send.at[n], back_recv.at[n])

    for n in range(2):
        own(waves_out, lines_in, back_rows[n], own_sem.at[2 + n]).wait()
        settle(lines_in.at[rest, back_rows[n]], back_recv.at[n])

    for pair in range(5):
        columns = []
        for group in (2 * pair, 2 * pair + 1):
            starts = [
                ROWS_OF[c] + group if group < 8 else 16 + c + 4 * (group - 8) for c in range(4)
            ]
            columns.append(jnp.concatenate([lines_in[:, start, :] for start in starts], 0))
        result = dots(bz[0][...], bz[1][...], *split(jnp.concatenate(columns, 1)))
        for part in range(2):
            lines_z[2 * pair + part, 0:256, :] = result[:, 128 * part : 128 * part + 128]
            lines_z[2 * pair + part, 256:264, :] = result[0:8, 128 * part : 128 * part + 128]

    lane = lane_of(2)
    low_half = lane < 64
    even = (lane // 32) % 2 == 0

    def regroup(part, carry):
        at = pl.ds(pl.multiple_of(part * 32, 32), 40)
        rim = lines_z[9, at, :]
        for group in range(9):
            main = lines_z[group, at, :]
            if group < 8:
                side = turn(rim, -4 * group)
            else:
                side = jnp.where(
                    lane < 64, turn(main, -64), jnp.where(lane < 96, turn(main, -36), turn(main, -8))
                )
            pair_even = jnp.where(even, main, side)
            pair_odd = turn(jnp.where(even, side, main), -32)
            for odd, value in enumerate((pair_even, pair_odd)):
                high = value.astype(bf16).astype(f32)
                low = value - high
                planes = (jnp.where(low_half, high, turn(low, 64)), jnp.where(low_half, turn(high, 64), low))
                for second in range(2):
                    for k in range(4):
                        window = planes[second][8 * k : 8 * k + 16].astype(bf16)
                        field[(4 * group + 2 * second + odd) * 32 + 4 * part + k] = window
        return carry

    lax.fori_loop(0, 8, regroup, 0)

    rows16 = lax.broadcasted_iota(jnp.int32, (16, 128), 0).astype(f32) - 1.0
    rows40 = lax.broadcasted_iota(jnp.int32, (40, 128), 0).astype(f32) - 1.0
    nothing = jnp.zeros((24, 256), f32)

    def one(number, slot):
        charge, at_x, at_y, at_z = [slot[i : i + 1] for i in range(4)]
        at_x = at_x - codes[1, number].astype(f32)
        at_z = at_z - codes[2, number].astype(f32)
        weight_x, slope_x = bspline(rows16 - at_x, True)
        weight_z, slope_z = bspline(rows16 - at_z, True)
        along_y = jnp.concatenate(bspline(rows40 - at_y, True), 1)
        y_high = along_y.astype(bf16).astype(f32)
        y_low = along_y - y_high
        both = jnp.concatenate(
            [y_high, nothing, y_high, nothing, y_low, nothing, y_low, nothing], 0
        ).astype(bf16)
        base = codes[0, number]
        window = jnp.concatenate([field[base + 32 * i] for i in range(11)], 0)
        out = jnp.dot(jnp.concatenate([window, window], 1), both, preferred_element_type=f32)
        plain = jnp.zeros((16, 128), f32)
        along_x = jnp.zeros((16, 128), f32)
        sloped = jnp.zeros((16, 128), f32)
        for i in range(11):
            value = out[16 * i : 16 * i + 16, :128]
            slope = out[16 * i : 16 * i + 16, 128:]
            plain = plain + weight_x[i : i + 1] * value
            along_x = along_x + slope_x[i : i + 1] * value
            sloped = sloped + weight_x[i : i + 1] * slope
        minus = -charge
        return jnp.concatenate(
            [
                minus * jnp.sum(along_x * weight_z, 0, keepdims=True),
                minus * jnp.sum(sloped * weight_z, 0, keepdims=True),
                minus * jnp.sum(plain * slope_z, 0, keepdims=True),
                charge,
            ],
            0,
        )

    def interpolate(step, carry):
        source = lax.rem(chunk + step, OWN)
        first = pl.ds(pl.multiple_of(8 * source, 8), 8)
        pair = slots_ref[first, :]
        force[source] = jnp.concatenate(
            [one(2 * source, pair[0:4]), one(2 * source + 1, pair[4:8])], 0
        )
        back_to_me = jnp.logical_and(same, source == chunk)

        @pl.when(jnp.logical_not(back_to_me))
        def _():
            remote(
                force.at[source], force_in.at[mine], force_send, force_recv,
                (grid_bead, source // 8, source % 8),
            ).start()

        @pl.when(back_to_me)
        def _():
            pltpu.make_async_copy(force.at[source], force_in.at[mine], own_sem.at[4]).start()

        return carry

    lax.fori_loop(0, OWN, interpolate, 0)

    chosen = jnp.where(targets(owner_ref[...], True), 1.0, 0.0).astype(bf16)

    @pl.when(same)
    def _():
        settle(force_in.at[mine], own_sem.at[4])
        settle(force_in.at[rest], force_recv)
        settle(force_in.at[rest], force_send)

    @pl.when(jnp.logical_not(same))
    def _():
        settle(force_in, force_recv)
        settle(force_in, force_send)

    for axis in range(3):
        both = jnp.concatenate([force_in[:, axis, :], force_in[:, 4 + axis, :]], 0)
        moved = sum(
            lax.dot_general(chosen, part, (((0,), (0,)), ((), ())), preferred_element_type=f32)
            for part in reversed(three(both))
        )
        spring = 2.0 * frac_ref[axis] - before_ref[axis] - after_ref[axis]
        out_ref[axis] = moved - spring_scale * spring

    for n in range(2):
        settle(lines.at[rest, out_rows[n]], out_send.at[n])
        settle(waves_out.at[rest, back_rows[n]], back_send.at[n])


def grid_to_forces(codes, packed, slots, owner_row, frac, before, after):
    table = tables()
    consts = [jnp.asarray(half) for name in TABLES for half in table[name]]
    dma = pltpu.SemaphoreType.DMA
    chunks = VMEM((OWN, 40, 128), f32)
    return pl.pallas_call(
        wave_kernel,
        out_shape=jax.ShapeDtypeStruct((3, OWN, 128), f32),
        in_specs=[pl.BlockSpec(memory_space=SMEM)] * 2
        + vmem(8)
        + [pl.BlockSpec(memory_space=pl.ANY)] * 12,
        out_specs=pl.BlockSpec(memory_space=VMEM),
        scratch_shapes=[VMEM(const.shape, bf16) for const in consts]
        + [
            chunks, chunks, chunks, chunks,
            VMEM((2, 256, 512), bf16), VMEM((2, 256, 512), bf16),
            VMEM((2, 4, 8, 8, 128), f32), VMEM((2, 4, 8, 8, 128), f32),
            VMEM((10, 264, 128), f32), VMEM((36 * 32, 16, 128), bf16),
            VMEM((OWN, 8, 128), f32), VMEM((OWN, 8, 128), f32),
            dma((12,)), dma((2,)), dma((2,)), dma((2,)), dma((2,)), dma((5,)), dma, dma,
        ],
        compiler_params=pltpu.CompilerParams(
            collective_id=1, has_side_effects=True, vmem_limit_bytes=56 << 20
        ),
        name="grid_to_forces",
    )(
        codes, jnp.asarray(table["in_z"]), packed, slots, owner_row, frac, before, after,
        jnp.asarray(table["column"]), jnp.asarray(table["row"]), *consts,
    )


def local(block_owner, block_tile, atom_cell, atom_frac, charge, zone):
    owner_row = block_owner.reshape(1, OWN)
    frac = jnp.transpose(atom_frac[0], (1, 0, 2))
    slots, before, after = atoms_to_slots(
        owner_row, block_tile.reshape(1, OWN), atom_cell, frac, charge, zone
    )
    packed, codes = spread(slots)
    total = grid_to_forces(codes, packed, slots, owner_row, frac, before, after)
    return jnp.transpose(total, (1, 0, 2))[None]


def solution(mesh):
    return jax.shard_map(
        local,
        mesh=mesh,
        in_specs=(
            P(("px", "py"), None),
            P(("px", "py")),
            P(("px", "py"), None),
            P("bead", ("px", "py"), None, None),
            P(("px", "py"), None),
            P(("px", "py"), None),
        ),
        out_specs=P("bead", ("px", "py"), None, None),
        check_vma=False,
    )
```

time: 167 us -> 122 us (0.73)
  Pallas kernels: 156 us -> 118 us
  local copies, waits for them, and re-layouts: 7.72 us -> 4.14 us
  starting transfers between devices: 3.31 us -> 0 us
    pallas_call x9 -> x3, Pallas kernels: 156 us -> 118 us  [the longest x1 79 us: grid_to_forces(): pl.pallas_call(wave_kernel, out_shape=jax.ShapeDtypeStruct((3, OWN, 128),...]
    ppermute x2 -> x0, starting transfers between devices: 3.31 us -> none  [the longest x1 2.04 us: local(): lax.ppermute(frac, 'bead', [(i, (i + 1) % beads) for i in range(beads)])]
    unnamed x22 -> x7, local copies, waits for them, and re-layouts: 6.47 us -> 4.14 us
  transfers between devices with their start and end apart: 2 -> 0, of which waited for: 0 -> 0; matrix products, arithmetic and copies ran while one was open for 1% -> 0% of each run, Pallas kernels for 92% -> 0%
where the time goes in v2:
time: 122 us
  Pallas kernels  118 us (97%)
  local copies, waits for them, and re-layouts  4.14 us (3%)
    pallas_call x1, Pallas kernels, grid_to_forces(): pl.pallas_call(wave_kernel, out_shape=jax.ShapeDtypeStruct((3, OWN, 128),...  79 us
    pallas_call x1, Pallas kernels, atoms_to_slots(): pl.pallas_call(atoms_kernel, out_shape=[jax.ShapeDtypeStruct((8 * OWN, 12...  23.6 us
    pallas_call x1, Pallas kernels, spread(): pl.pallas_call(spread_kernel, out_shape=[jax.ShapeDtypeStruct((10, 256, 1...  15.3 us
    unnamed x7, local copies, waits for them, and re-layouts  4.14 us

profile of v2, /device:TPU:1, one launch (start us, length us, event | category | flops | bytes accessed | tf_op | source)
XLA Modules:
  0.0 122.1 jit_solution(17735733521311434554)
XLA Ops:
  0.0 23.6 %atoms_to_slots.1 = (f32[512,128]{1,0:T(8,128)}, f32[3,64,128]{2,1,0:T(8,128)}, f32[3,64,128]{2,1,0:T(8,128)}) custom-call(s32[1,64]{1,0:T(1,128)} %bitcast.11, s32[1,64]{1,0:T(1,128)} %bitcast.13, s32[64,128]{1,0:T(8,128)} %cell_ref.1, f32[3,64,128]{2,1,0:T(8,128)} %bitcast.8, f32[64,128]{1,0:T(8,128)} %charge_ref.1, s32[64,128]{1,0:T(8,128)} %zone_ref.1), custom_call_target="tpu_custom_call" | custom-call | tf_op jit(solution)/shard_map/atoms_to_slots/pallas_call | solution.py:261
  23.6 0.0 copy-start.1
  23.6 0.9 copy-done.1
  24.6 15.3 %spread.1 = (f32[10,256,128]{2,1,0:T(8,128)S(1)}, s32[8,128]{1,0:T(8,128)S(1)}) custom-call(f32[512,128]{1,0:T(8,128)S(1)} %copy-done.1), custom_call_target="tpu_custom_call" | custom-call | tf_op jit(solution)/shard_map/spread/pallas_call | solution.py:385
  39.9 0.0 copy-start
  39.9 1.1 copy-done
  41.0 0.0 copy-start.2
  41.0 0.6 copy-done.2
  41.6 79.0 %grid_to_forces.1 = f32[3,64,128]{2,1,0:T(8,128)} custom-call(s32[8,128]{1,0:T(8,128)} %copy-done.2, f32[256]{0:T(256)} %constant.42.clone.in_z, f32[10,256,128]{2,1,0:T(8,128)} %copy-done, f32[512,128]{1,0:T(8,128)} %get-tuple-element.10.slots_ref, s32[1,64]{1,0:T(1,128)} %bitcast.12, f32[3,64,128]{2,1,0:T(8,128)} %bitcast.9, ...), custom_call_target="tpu_custom_call" | custom-call | tf_op jit(solution)/shard_map/grid_to_forces/pallas_call | solution.py:740
  120.5 1.5 %copy.23 = f32[1,64,3,128]{3,1,2,0:T(8,128)} copy(f32[1,64,3,128]{3,1,2,0:T(8,128)} %bitcast.10) | data formatting | bytes 196608
Async XLA Ops:
  23.6 1.0 copy-start.1
  39.9 1.1 copy-start
  41.0 0.6 copy-start.2

commit v3 on v2

--- a/solution.py
+++ b/solution.py
@@ -17,6 +17,7 @@
 MESH = pl.DeviceIdType.MESH
 VMEM = pltpu.VMEM
 SMEM = pltpu.SMEM
+HBM = pltpu.HBM
 ewald_beta = 0.75
 spring_scale = 0.25
 
@@ -43,12 +44,10 @@
     scale = np.where(kz == 0, 1.0, 2.0) / float(NG**3)
     scale = np.repeat(scale, 2, 0).reshape(-1)
     back_z = (forward_z * scale[:, None]).T
-    main = whole
-    rim = np.arange(256)
-    rim = 32 * (rim // 32 + 1) + rim % 4
-    cos_y, sin_y = waves(np.concatenate([main, rim]), whole)
-    forward_y = np.concatenate([cos_y, sin_y], 1)
-    back_y = np.concatenate([cos_y.T, sin_y.T], 1)
+    forward_y = np.concatenate(waves(whole, whole), 1)
+    rim = (32 * (whole // 32 + 1) + whole % 4) % NG
+    fold_y = np.concatenate([rim[:, None] == whole[None, :]] * 2).astype(ml_dtypes.bfloat16)
+    unfold_y = np.concatenate([whole[:, None] == rim[None, :]] * 2).astype(ml_dtypes.bfloat16)
     step, block, group = np.meshgrid(np.arange(4), np.arange(8), np.arange(8), indexing="ij")
     place = (32 * block + 4 * group + step).reshape(-1)
     cos_x, sin_x = waves(whole, place)
@@ -58,21 +57,16 @@
     theta = wave * (2.0 * math.pi / NG)
     factor = (6.0 / (4.0 + 2.0 * np.cos(theta))) ** 2
     factor = factor * np.exp(-theta * theta / (4.0 * ewald_beta * ewald_beta))
-    column = np.zeros((256, 128), np.float32)
-    column[:, 0], column[:, 1] = theta * theta, factor
     row = np.zeros((8, 256), np.float32)
     row[0], row[1] = theta * theta, factor
-    in_z = np.stack([(theta * theta)[kz.T], factor[kz.T]], 1).astype(np.float32).reshape(-1)
     return dict(
         forward_z=halves(forward_z),
         back_z=halves(back_z),
         forward_y=halves(forward_y),
-        back_y=halves(back_y),
+        fold_y=(fold_y, unfold_y),
         forward_x=halves(forward_x),
         back_x=halves(back_x),
-        column=column,
         row=row,
-        in_z=in_z,
     )
 
 
@@ -81,9 +75,11 @@
     return high, (value - high.astype(f32)).astype(bf16)
 
 
+product = functools.partial(jnp.dot, preferred_element_type=f32)
+
+
 def dots(a_high, a_low, b_high, b_low):
-    dot = functools.partial(jnp.dot, preferred_element_type=f32)
-    return dot(a_high, b_high) + (dot(a_high, b_low) + dot(a_low, b_high))
+    return product(a_high, b_high) + (product(a_high, b_low) + product(a_low, b_high))
 
 
 def lane_of(rank):
@@ -165,9 +161,22 @@
 
 
 def atoms_kernel(
-    owner_ref, tile_ref, cell_ref, frac_ref, charge_ref, zone_ref, slots_ref, before_ref, after_ref,
-    payload, stage, stage_send, stage_recv, send_sem, recv_sem, own_sem, bead_send, bead_recv,
+    owner_hbm, tile_hbm, cell_hbm, frac_hbm, charge_hbm, zone_hbm, slots_ref, spring_ref, chosen_ref,
+    owner_ref, tile_ref, cell_ref, frac_ref, charge_ref, zone_ref,
+    payload, stage, before_ref, after_ref,
+    stage_send, stage_recv, send_sem, recv_sem, own_sem, bead_send, bead_recv, in_sem,
 ):
+    loads = [
+        pltpu.make_async_copy(src, dst, in_sem.at[i])
+        for i, (src, dst) in enumerate(
+            (
+                (owner_hbm, owner_ref), (tile_hbm, tile_ref), (cell_hbm, cell_ref),
+                (frac_hbm, frac_ref), (charge_hbm, charge_ref), (zone_hbm, zone_ref),
+            )
+        )
+    ]
+    for copy in loads:
+        copy.start()
     bead, px, py = here()
     chunk = px * 8 + py
     barrier = pltpu.get_barrier_semaphore()
@@ -181,6 +190,8 @@
     for step in range(1, 4):
         pl.semaphore_signal(barrier, inc=1, device_id=(lax.rem(bead + step, 4), px, py), device_id_type=MESH)
 
+    for copy in loads:
+        copy.wait()
     chosen = jnp.where(targets(owner_ref[...], False), 1.0, 0.0).astype(bf16)
     blocks = cell_ref.shape[0]
     up = lax.broadcasted_iota(jnp.int32, (blocks, blocks), 0)
@@ -245,29 +256,41 @@
         copy.wait_recv()
         other = lax.rem(bead + 4 - step, 4)
         deliver(lambda j: stage.at[other, pl.ds(pl.multiple_of(j * 8, 8), 8)], other)
+    chosen_ref[...] = jnp.where(targets(owner_ref[...], True), 1.0, 0.0).astype(bf16)
+    for copy in springs:
+        copy.wait()
+    for axis in range(3):
+        bend = 2.0 * frac_ref[axis] - before_ref[axis] - after_ref[axis]
+        spring_ref[axis] = -spring_scale * bend
     settle(slots_ref.at[mark], own_sem)
     rest = pl.ds(0, 8 * OWN - 8)
     settle(slots_ref.at[rest], recv_sem)
     settle(slots_ref.at[rest], send_sem)
     for copy in staged:
         copy.wait_send()
-    for copy in springs:
-        copy.wait()
 
 
 def atoms_to_slots(owner_row, tile_row, cell, frac, charge, zone):
-    shape = jax.ShapeDtypeStruct((3, OWN, 128), f32)
     dma = pltpu.SemaphoreType.DMA
     return pl.pallas_call(
         atoms_kernel,
-        out_shape=[jax.ShapeDtypeStruct((8 * OWN, 128), f32), shape, shape],
-        in_specs=vmem(6),
+        out_shape=[
+            jax.ShapeDtypeStruct((8 * OWN, 128), f32),
+            jax.ShapeDtypeStruct((3, OWN, 128), f32),
+            jax.ShapeDtypeStruct((2 * OWN, OWN), bf16),
+        ],
+        in_specs=[pl.BlockSpec(memory_space=HBM)] * 6,
         out_specs=vmem(3),
         scratch_shapes=[
+            VMEM((1, OWN), jnp.int32), VMEM((1, OWN), jnp.int32), VMEM((OWN, 128), jnp.int32),
+            VMEM((3, OWN, 128), f32), VMEM((OWN, 128), f32), VMEM((OWN, 128), jnp.int32),
             VMEM((8 * OWN, 128), f32), VMEM((4, 128, 128), f32),
-            dma((3,)), dma((3,)), dma, dma, dma, dma((2,)), dma((2,)),
+            VMEM((3, OWN, 128), f32), VMEM((3, OWN, 128), f32),
+            dma((3,)), dma((3,)), dma, dma, dma, dma((2,)), dma((2,)), dma((6,)),
         ],
-        compiler_params=pltpu.CompilerParams(collective_id=0, has_side_effects=True),
+        compiler_params=pltpu.CompilerParams(
+            collective_id=0, has_side_effects=True, vmem_limit_bytes=60 << 20
+        ),
         name="atoms_to_slots",
     )(owner_row, tile_row, cell, frac, charge, zone)
 
@@ -299,17 +322,16 @@
         return count + held.astype(jnp.int32), jnp.where(held, empty, slot)
 
     count, empty = lax.fori_loop(0, 2 * OWN, step, (jnp.int32(0), jnp.int32(0)))
-    for k in range(3):
+    for k in range(15):
         list_ref[count + k] = empty
-    list_ref[255] = (count + 3) // 4
-
-
-def spread_kernel(slots_ref, out_ref, codes_scalar, list_ref, density, codes, sem):
+    list_ref[255] = (count + 15) // 16
+
+
+def spread_kernel(slots_ref, out_hbm, codes_scalar, list_ref, density, codes, out_ref, sem, out_sem):
     slot_list(slots_ref, list_ref, codes, codes_scalar, sem)
     density[...] = jnp.zeros_like(density)
     rows16 = lax.broadcasted_iota(jnp.int32, (16, 128), 0).astype(f32) - 1.0
     rows40 = lax.broadcasted_iota(jnp.int32, (40, 128), 0).astype(f32) - 1.0
-    nothing = jnp.zeros((24, 128), f32)
 
     def one(slot):
         plane_x, row_z = codes_scalar[1, slot], codes_scalar[2, slot]
@@ -319,14 +341,13 @@
         at_z = slots_ref[pl.ds(4 * slot + 3, 1), :] - row_z.astype(f32)
         weight_x = bspline(rows16 - at_x, False) * charge
         weight_z = bspline(rows16 - at_z, False)
-        weight_y = bspline(rows40 - at_y, False)
+        weight_y = jnp.concatenate([bspline(rows40 - at_y, False), jnp.zeros((24, 128), f32)], 0)
         plane = jnp.concatenate([weight_x[i : i + 1] * weight_z for i in range(11)], 0)
         plane = jnp.concatenate(split(plane), 1)
-        y_high = weight_y.astype(bf16).astype(f32)
-        y_low = weight_y - y_high
-        left = jnp.concatenate([y_high, nothing, y_low, nothing], 0)
-        right = jnp.concatenate([y_high, nothing, jnp.zeros((64, 128), f32)], 0)
-        both = jnp.concatenate([left, right], 1).astype(bf16)
+        y_high, y_low = split(weight_y)
+        left = jnp.concatenate([y_high, y_low], 0)
+        right = jnp.concatenate([y_high, jnp.zeros((64, 128), bf16)], 0)
+        both = jnp.concatenate([left, right], 1)
         out = lax.dot_general(plane, both, (((1,), (1,)), ((), ())), preferred_element_type=f32)
         return plane_x, row_z, out
 
@@ -336,7 +357,7 @@
             density[plane_x + i, pl.ds(base, 16), :] += out[16 * i : 16 * i + 16]
 
     def step(index, carry):
-        for found in [one(list_ref[4 * index + k]) for k in range(4)]:
+        for found in [one(list_ref[16 * index + k]) for k in range(16)]:
             put(*found)
         return carry
 
@@ -376,9 +397,13 @@
                 corner = jnp.where((lane >= 104) & (lane < 108), turn(side, 8), corner)
                 keep(8, jnp.where(last, corner, main))
         keep(9, rim)
+        pltpu.make_async_copy(out_ref.at[:, here, :], out_hbm.at[:, here, :], out_sem.at[chunk]).start()
         return carry
 
     lax.fori_loop(0, 8, regroup, 0)
+    for chunk in range(8):
+        here = pl.ds(32 * chunk, 32)
+        pltpu.make_async_copy(out_ref.at[:, here, :], out_hbm.at[:, here, :], out_sem.at[chunk]).wait()
 
 
 def spread(slots):
@@ -389,19 +414,21 @@
             jax.ShapeDtypeStruct((8, 128), jnp.int32),
         ],
         in_specs=vmem(1),
-        out_specs=[pl.BlockSpec(memory_space=VMEM), pl.BlockSpec(memory_space=SMEM)],
+        out_specs=[pl.BlockSpec(memory_space=pl.ANY), pl.BlockSpec(memory_space=SMEM)],
         scratch_shapes=[
             SMEM((256,), jnp.int32),
             VMEM((36, 264, 128), f32),
             VMEM((8, 128), jnp.int32),
+            VMEM((10, 256, 128), f32),
             pltpu.SemaphoreType.DMA,
+            pltpu.SemaphoreType.DMA((8,)),
         ],
-        compiler_params=pltpu.CompilerParams(vmem_limit_bytes=24 << 20),
+        compiler_params=pltpu.CompilerParams(vmem_limit_bytes=60 << 20),
         name="spread",
     )(slots)
 
 
-TABLES = ("forward_z", "forward_y", "forward_x", "back_x", "back_y", "back_z")
+TABLES = ("forward_z", "forward_y", "forward_x", "back_x", "fold_y", "back_z")
 ROWS_OF = (0, 8, 24, 32)
 
 
@@ -424,23 +451,30 @@
 
 
 def wave_kernel(
-    codes, in_z, packed, slots_ref, owner_ref, frac_ref, before_ref, after_ref, column_ref, row_ref,
-    *rest,
+    codes, *rest,
 ):
-    table_refs, rest = rest[:12], rest[12:]
+    table_refs, rest = rest[:17], rest[17:]
     out_ref, rest = rest[0], rest[1:]
-    table_vmem, rest = rest[:12], rest[12:]
+    table_vmem, rest = rest[:17], rest[17:]
+    packed, fz_high, fz_low = table_vmem[:3]
+    row_ref, slots_ref, spring_ref, chosen_ref = table_vmem[13:]
     (
-        lines, waves_in, waves_out, lines_in, plane_high, plane_low, rims, rims_out,
+        lines, waves_in, waves_out, lines_in, plane, plane_rim, rims, rims_out,
         lines_z, field, force, force_in, table_sem, out_send, out_recv, back_send, back_recv,
         own_sem, force_send, force_recv,
     ) = rest
-    (fz, fy, fx, bx, by, bz) = [(table_vmem[2 * i], table_vmem[2 * i + 1]) for i in range(6)]
+    (fz, fy, fx, bx, fold, bz) = [(table_vmem[2 * i + 1], table_vmem[2 * i + 2]) for i in range(6)]
     bead, px, py = here()
     mine, grid_bead, chunk = bead * 16 + px * 2 + py % 2, py // 2, px * 8 + py
     same = bead == grid_bead
     barrier = pltpu.get_barrier_semaphore()
 
+    table_copies = [
+        pltpu.make_async_copy(table_refs[i], table_vmem[i], table_sem.at[i]) for i in range(17)
+    ]
+    for copy in table_copies[:3]:
+        copy.start()
+
     def greet(step, carry):
         other = lax.rem(mine + hop(step), OWN)
         pl.semaphore_signal(barrier, inc=1, device_id=place(other, grid_bead), device_id_type=MESH)
@@ -461,13 +495,10 @@
     def _():
         lax.fori_loop(0, OWN, greet_atoms, 0)
 
-    table_copies = [
-        pltpu.make_async_copy(table_refs[i], table_vmem[i], table_sem.at[i]) for i in range(12)
-    ]
-    for copy in table_copies:
+    for copy in table_copies[3:]:
         copy.start()
-    table_copies[0].wait()
-    table_copies[1].wait()
+    for copy in table_copies[:3]:
+        copy.wait()
 
     for pair in range(5):
         high, low = split(jnp.concatenate([packed[2 * pair], packed[2 * pair + 1]], 1))
@@ -500,14 +531,18 @@
         own(lines, waves_in, out_rows[n], own_sem.at[n]).start()
         send_all(lines, waves_in, out_rows[n], out_send.at[n], out_recv.at[n])
 
-    for copy in table_copies[2:]:
+    for copy in table_copies[3:]:
         copy.wait()
 
     lane = lane_of(3)
     sub = lax.broadcasted_iota(jnp.int32, (1, 8, 128), 1)
     lane_group = (lane // 4) % 8
-    column = column_ref[...]
-    row = row_ref[...]
+    square_y, factor_y = row_ref[0:1, :], row_ref[1:2, :]
+    up = lax.broadcasted_iota(jnp.int32, (256, 256), 0)
+    across = lax.broadcasted_iota(jnp.int32, (256, 256), 1)
+    square_x = jnp.sum(jnp.where(up == across, square_y, 0.0), 1, keepdims=True)
+    factor_x = jnp.sum(jnp.where(up == across, factor_y, 0.0), 1, keepdims=True)
+    mine_z = lax.broadcasted_iota(jnp.int32, (1, 256), 1) - 2 * mine
 
     for n in range(2):
         own(lines, waves_in, out_rows[n], own_sem.at[n]).wait()
@@ -536,20 +571,24 @@
                         value = value + jnp.where(sub == 0, shifted(extra[i][:, c : c + 1, :], 1), 0.0)
                         corner = shifted(extra[3][:, c : c + 1, :], 1)
                         rim = rim + jnp.where((sub == 0) & (lane_group == i), corner, 0.0)
-                    for part, array in enumerate((value, rim)):
-                        high, low = split(array.reshape(64, 128))
-                        start = 256 * part + 128 * q
-                        plane_high[half, 64 * i : 64 * i + 64, start : start + 128] = high
-                        plane_low[half, 64 * i : 64 * i + 64, start : start + 128] = low
-
-        real = dots(plane_high[0], plane_low[0], fy[0][...], fy[1][...])
-        imag = dots(plane_high[1], plane_low[1], fy[0][...], fy[1][...])
+                    lines_of = slice(64 * i, 64 * i + 64)
+                    plane[half, lines_of, 128 * q : 128 * q + 128] = value.reshape(64, 128)
+                    high, low = split(rim.reshape(64, 128))
+                    plane_rim[half, lines_of, 128 * q : 128 * q + 128] = high
+                    plane_rim[half, lines_of, 256 + 128 * q : 384 + 128 * q] = low
+
+        real, imag = [
+            dots(*split(plane[half] + product(plane_rim[half], fold[0][...])), fy[0][...], fy[1][...])
+            for half in range(2)
+        ]
         spec = jnp.concatenate(
             [real[:, :256] + imag[:, 256:], imag[:, :256] - real[:, 256:]], 1
         )
         both = dots(fx[0][...], fx[1][...], *split(spec))
-        square = column[:, 0:1] + row[0:1, :] + in_z[4 * mine + n]
-        green = column[:, 1:2] * row[1:2, :] * (in_z[4 * mine + 2 + n] * (4.0 * math.pi))
+        square_z = jnp.sum(jnp.where(mine_z == n, square_y, 0.0), 1, keepdims=True)
+        factor_z = jnp.sum(jnp.where(mine_z == n, factor_y, 0.0), 1, keepdims=True)
+        square = square_x + square_y + square_z
+        green = factor_x * factor_y * (factor_z * (4.0 * math.pi))
         green = jnp.where(square > 0.0, green / jnp.where(square > 0.0, square, 1.0), 0.0)
         spec = jnp.concatenate(
             [
@@ -562,8 +601,9 @@
         spec = jnp.concatenate(
             [both[:256, :256] - both[256:, 256:], both[:256, 256:] + both[256:, :256]], 0
         )
-        both = dots(*split(spec), by[0][...], by[1][...])
-        back = [both[:256, :512] - both[256:, 512:], both[256:, :512] + both[:256, 512:]]
+        both = dots(*split(spec), fy[0][...], fy[1][...])
+        back = [both[:256, :256] - both[256:, 256:], both[256:, :256] + both[:256, 256:]]
+        back_rim = [product(jnp.concatenate(split(value), 1), fold[1][...]) for value in back]
 
         for q in range(2):
             if n == 0:
@@ -576,7 +616,7 @@
                 for i in range(4):
                     lines_of = slice(64 * i, 64 * i + 64)
                     value = back[half][lines_of, 128 * q : 128 * q + 128].reshape(8, 8, 128)
-                    rim = back[half][lines_of, 256 + 128 * q : 384 + 128 * q].reshape(8, 8, 128)
+                    rim = back_rim[half][lines_of, 128 * q : 128 * q + 128].reshape(8, 8, 128)
                     main.append(value)
                     if i < 3:
                         extra[i] = jnp.where(sub == c, shifted(value[:, 0:1, :], -1), extra[i])
@@ -653,11 +693,8 @@
         weight_x, slope_x = bspline(rows16 - at_x, True)
         weight_z, slope_z = bspline(rows16 - at_z, True)
         along_y = jnp.concatenate(bspline(rows40 - at_y, True), 1)
-        y_high = along_y.astype(bf16).astype(f32)
-        y_low = along_y - y_high
-        both = jnp.concatenate(
-            [y_high, nothing, y_high, nothing, y_low, nothing, y_low, nothing], 0
-        ).astype(bf16)
+        y_high, y_low = split(jnp.concatenate([along_y, nothing], 0))
+        both = jnp.concatenate([y_high, y_high, y_low, y_low], 0)
         base = codes[0, number]
         window = jnp.concatenate([field[base + 32 * i] for i in range(11)], 0)
         out = jnp.dot(jnp.concatenate([window, window], 1), both, preferred_element_type=f32)
@@ -682,30 +719,34 @@
         )
 
     def interpolate(step, carry):
-        source = lax.rem(chunk + step, OWN)
-        first = pl.ds(pl.multiple_of(8 * source, 8), 8)
-        pair = slots_ref[first, :]
-        force[source] = jnp.concatenate(
-            [one(2 * source, pair[0:4]), one(2 * source + 1, pair[4:8])], 0
-        )
-        back_to_me = jnp.logical_and(same, source == chunk)
-
-        @pl.when(jnp.logical_not(back_to_me))
-        def _():
-            remote(
-                force.at[source], force_in.at[mine], force_send, force_recv,
-                (grid_bead, source // 8, source % 8),
-            ).start()
-
-        @pl.when(back_to_me)
-        def _():
-            pltpu.make_async_copy(force.at[source], force_in.at[mine], own_sem.at[4]).start()
+        sources = [lax.rem(chunk + hop(4 * step + k), OWN) for k in range(4)]
+        found = []
+        for source in sources:
+            pair = slots_ref[pl.ds(pl.multiple_of(8 * source, 8), 8), :]
+            found.append(
+                jnp.concatenate([one(2 * source, pair[0:4]), one(2 * source + 1, pair[4:8])], 0)
+            )
+        for source, value in zip(sources, found):
+            force[source] = value
+        for source in sources:
+            back_to_me = jnp.logical_and(same, source == chunk)
+
+            @pl.when(jnp.logical_not(back_to_me))
+            def _():
+                remote(
+                    force.at[source], force_in.at[mine], force_send, force_recv,
+                    (grid_bead, source // 8, source % 8),
+                ).start()
+
+            @pl.when(back_to_me)
+            def _():
+                pltpu.make_async_copy(force.at[source], force_in.at[mine], own_sem.at[4]).start()
 
         return carry
 
-    lax.fori_loop(0, OWN, interpolate, 0)
-
-    chosen = jnp.where(targets(owner_ref[...], True), 1.0, 0.0).astype(bf16)
+    lax.fori_loop(0, OWN // 4, interpolate, 0)
+
+    chosen = chosen_ref[...]
 
     @pl.when(same)
     def _():
@@ -724,53 +765,50 @@
             lax.dot_general(chosen, part, (((0,), (0,)), ((), ())), preferred_element_type=f32)
             for part in reversed(three(both))
         )
-        spring = 2.0 * frac_ref[axis] - before_ref[axis] - after_ref[axis]
-        out_ref[axis] = moved - spring_scale * spring
+        out_ref[axis] = moved + spring_ref[axis]
 
     for n in range(2):
         settle(lines.at[rest, out_rows[n]], out_send.at[n])
         settle(waves_out.at[rest, back_rows[n]], back_send.at[n])
 
 
-def grid_to_forces(codes, packed, slots, owner_row, frac, before, after):
+def grid_to_forces(codes, packed, slots, spring, chosen):
     table = tables()
-    consts = [jnp.asarray(half) for name in TABLES for half in table[name]]
+    consts = [packed] + [jnp.asarray(half) for name in TABLES for half in table[name]]
+    consts += [jnp.asarray(table["row"]), slots, spring, chosen]
     dma = pltpu.SemaphoreType.DMA
     chunks = VMEM((OWN, 40, 128), f32)
     return pl.pallas_call(
         wave_kernel,
         out_shape=jax.ShapeDtypeStruct((3, OWN, 128), f32),
-        in_specs=[pl.BlockSpec(memory_space=SMEM)] * 2
-        + vmem(8)
-        + [pl.BlockSpec(memory_space=pl.ANY)] * 12,
+        in_specs=[pl.BlockSpec(memory_space=SMEM)] + [pl.BlockSpec(memory_space=HBM)] * 17,
         out_specs=pl.BlockSpec(memory_space=VMEM),
-        scratch_shapes=[VMEM(const.shape, bf16) for const in consts]
+        scratch_shapes=[VMEM(const.shape, const.dtype) for const in consts]
         + [
             chunks, chunks, chunks, chunks,
-            VMEM((2, 256, 512), bf16), VMEM((2, 256, 512), bf16),
+            VMEM((2, 256, 256), f32), VMEM((2, 256, 512), bf16),
             VMEM((2, 4, 8, 8, 128), f32), VMEM((2, 4, 8, 8, 128), f32),
             VMEM((10, 264, 128), f32), VMEM((36 * 32, 16, 128), bf16),
             VMEM((OWN, 8, 128), f32), VMEM((OWN, 8, 128), f32),
-            dma((12,)), dma((2,)), dma((2,)), dma((2,)), dma((2,)), dma((5,)), dma, dma,
+            dma((17,)), dma((2,)), dma((2,)), dma((2,)), dma((2,)), dma((5,)), dma, dma,
         ],
         compiler_params=pltpu.CompilerParams(
-            collective_id=1, has_side_effects=True, vmem_limit_bytes=56 << 20
+            collective_id=1, has_side_effects=True, vmem_limit_bytes=60 << 20
         ),
         name="grid_to_forces",
     )(
-        codes, jnp.asarray(table["in_z"]), packed, slots, owner_row, frac, before, after,
-        jnp.asarray(table["column"]), jnp.asarray(table["row"]), *consts,
+        codes, *consts,
     )
 
 
 def local(block_owner, block_tile, atom_cell, atom_frac, charge, zone):
     owner_row = block_owner.reshape(1, OWN)
     frac = jnp.transpose(atom_frac[0], (1, 0, 2))
-    slots, before, after = atoms_to_slots(
+    slots, spring, chosen = atoms_to_slots(
         owner_row, block_tile.reshape(1, OWN), atom_cell, frac, charge, zone
     )
     packed, codes = spread(slots)
-    total = grid_to_forces(codes, packed, slots, owner_row, frac, before, after)
+    total = grid_to_forces(codes, packed, slots, spring, chosen)
     return jnp.transpose(total, (1, 0, 2))[None]
 
 

time: 122 us -> 106 us (0.87)
  Pallas kernels: 118 us -> 104 us
  local copies, waits for them, and re-layouts: 4.14 us -> 1.54 us
    pallas_call x1, Pallas kernels: 79 us -> 70.8 us  [grid_to_forces(): pl.pallas_call(wave_kernel, out_shape=jax.ShapeDtypeStruct((3, OWN, 128),...]
    pallas_call x1, Pallas kernels: 15.3 us -> 10.6 us  [spread(): pl.pallas_call(spread_kernel, out_shape=[jax.ShapeDtypeStruct((10, 256, 1...]
    unnamed x7 -> x1, local copies, waits for them, and re-layouts: 4.14 us -> 1.54 us
where the time goes in v3:
time: 106 us
  Pallas kernels  104 us (98%)
  local copies, waits for them, and re-layouts  1.54 us (1%)
    pallas_call x1, Pallas kernels, grid_to_forces(): pl.pallas_call(wave_kernel, out_shape=jax.ShapeDtypeStruct((3, OWN, 128),...  70.8 us
    pallas_call x1, Pallas kernels, atoms_to_slots(): pl.pallas_call(atoms_kernel, out_shape=[jax.ShapeDtypeStruct((8 * OWN, 12...  23 us
    pallas_call x1, Pallas kernels, spread(): pl.pallas_call(spread_kernel, out_shape=[jax.ShapeDtypeStruct((10, 256, 1...  10.6 us

profile of v3, /device:TPU:1, one launch (start us, length us, event | category | flops | bytes accessed | tf_op | source)
XLA Modules:
  0.0 106.0 jit_solution(6587039815763206575)
XLA Ops:
  0.0 23.0 %atoms_to_slots.1 = (f32[512,128]{1,0:T(8,128)}, f32[3,64,128]{2,1,0:T(8,128)}, bf16[128,64]{1,0:T(8,128)(2,1)}) custom-call(s32[1,64]{1,0:T(1,128)} %bitcast.10, s32[1,64]{1,0:T(1,128)} %bitcast.11, s32[64,128]{1,0:T(8,128)} %cell_hbm.1, f32[3,64,128]{2,1,0:T(8,128)} %bitcast.9, f32[64,128]{1,0:T(8,128)} %charge_hbm.1, s32[64,128]{1,0:T(8,128)} %zone_hbm.1), custom_call_target="tpu_custom_call" | custom-call | tf_op jit(solution)/shard_map/atoms_to_slots/pallas_call | solution.py:275
  23.0 10.6 %spread.1 = (f32[10,256,128]{2,1,0:T(8,128)}, s32[8,128]{1,0:T(8,128)}) custom-call(f32[512,128]{1,0:T(8,128)} %get-tuple-element.10.slots_ref.rest_14_), custom_call_target="tpu_custom_call" | custom-call | tf_op jit(solution)/shard_map/spread/pallas_call | solution.py:410
  33.6 70.8 %grid_to_forces.1 = f32[3,64,128]{2,1,0:T(8,128)} custom-call(s32[8,128]{1,0:T(8,128)} %get-tuple-element.11.codes, f32[10,256,128]{2,1,0:T(8,128)} %get-tuple-element.12.rest_0_, bf16[256,256]{1,0:T(8,128)(2,1)} %constant.26.clone.rest_1_, bf16[256,256]{1,0:T(8,128)(2,1)} %constant.27.clone.rest_2_, bf16[256,512]{1,0:T(8,128)(2,1)} %constant.28.clone.rest_3_, ...), custom_call_target="tpu_custom_call" | custom-call | tf_op jit(solution)/shard_map/grid_to_forces/pallas_call | solution.py:781
  104.4 1.5 %copy.21 = f32[1,64,3,128]{3,1,2,0:T(8,128)} copy(f32[1,64,3,128]{3,1,2,0:T(8,128)} %bitcast.8) | data formatting | bytes 196608

commit v4 on v3

--- a/solution.py
+++ b/solution.py
@@ -232,22 +232,21 @@
 
     def deliver(source, from_bead):
         def send(step, carry):
-            j = lax.rem(step + 2 * px + 1, 16)
-            device = (bead, j // 2, 2 * from_bead + j % 2)
-            mine = jnp.logical_and(j == 2 * px + py % 2, py // 2 == from_bead)
-            piece = source(j)
-
-            @pl.when(jnp.logical_not(mine))
-            def _():
-                remote(piece, slots_ref.at[mark], send_sem, recv_sem, device).start()
-
-            @pl.when(mine)
-            def _():
-                pltpu.make_async_copy(piece, slots_ref.at[mark], own_sem).start()
-
+            j = lax.rem(step + 2 * px + py % 2, 16)
+            remote(
+                source(j), slots_ref.at[mark], send_sem, recv_sem, (bead, j // 2, 2 * from_bead + j % 2)
+            ).start()
             return carry
 
-        lax.fori_loop(0, 16, send, 0)
+        @pl.when(from_bead == py // 2)
+        def _():
+            pltpu.make_async_copy(source(2 * px + py % 2), slots_ref.at[mark], own_sem).start()
+
+        @pl.when(jnp.logical_not(from_bead == py // 2))
+        def _():
+            send(0, 0)
+
+        lax.fori_loop(1, 16, send, 0)
 
     deliver(lambda j: payload.at[pl.ds(pl.multiple_of(bead * 128 + j * 8, 8), 8)], bead)
     for copy in springs:
@@ -295,50 +294,36 @@
     )(owner_row, tile_row, cell, frac, charge, zone)
 
 
-def slot_list(slots_ref, list_ref, codes, codes_scalar, sem):
-    charge = slots_ref[pl.ds(0, 2 * OWN, stride=4), :]
+def tile_codes(slots_ref):
     along_x = slots_ref[pl.ds(1, 2 * OWN, stride=4), :]
     along_z = slots_ref[pl.ds(3, 2 * OWN, stride=4), :]
     tile_x = (jnp.max(along_x, 1, keepdims=True) * 0.125).astype(jnp.int32)
     tile_z = (jnp.max(along_z, 1, keepdims=True) * 0.125).astype(jnp.int32)
-    filled = jnp.max(jnp.abs(charge), 1, keepdims=True) > 0.0
     up = lax.broadcasted_iota(jnp.int32, (128, 128), 0)
     across = lax.broadcasted_iota(jnp.int32, (128, 128), 1)
     sub = lax.broadcasted_iota(jnp.int32, (8, 128), 0)
     value = jnp.zeros((8, 128), f32)
-    columns = (256 * tile_x + tile_z, 8 * tile_x, 8 * tile_z, filled.astype(jnp.int32))
+    columns = (256 * tile_x + tile_z, 8 * tile_x, 8 * tile_z)
     for place_in, column in enumerate(columns):
         row = jnp.sum(jnp.where(up == across, column.astype(f32), 0.0), 0, keepdims=True)
         value = jnp.where(sub == place_in, row, value)
-    codes[...] = value.astype(jnp.int32)
+    return value.astype(jnp.int32)
+
+
+def spread_kernel(slots_ref, out_hbm, codes_scalar, density, codes, out_ref, sem, out_sem):
+    codes[...] = tile_codes(slots_ref)
     copy = pltpu.make_async_copy(codes, codes_scalar, sem)
     copy.start()
+    density[...] = jnp.zeros_like(density)
     copy.wait()
-
-    def step(slot, carry):
-        count, empty = carry
-        held = codes_scalar[3, slot] > 0
-        list_ref[count] = slot
-        return count + held.astype(jnp.int32), jnp.where(held, empty, slot)
-
-    count, empty = lax.fori_loop(0, 2 * OWN, step, (jnp.int32(0), jnp.int32(0)))
-    for k in range(15):
-        list_ref[count + k] = empty
-    list_ref[255] = (count + 15) // 16
-
-
-def spread_kernel(slots_ref, out_hbm, codes_scalar, list_ref, density, codes, out_ref, sem, out_sem):
-    slot_list(slots_ref, list_ref, codes, codes_scalar, sem)
-    density[...] = jnp.zeros_like(density)
     rows16 = lax.broadcasted_iota(jnp.int32, (16, 128), 0).astype(f32) - 1.0
     rows40 = lax.broadcasted_iota(jnp.int32, (40, 128), 0).astype(f32) - 1.0
 
-    def one(slot):
-        plane_x, row_z = codes_scalar[1, slot], codes_scalar[2, slot]
-        charge = slots_ref[pl.ds(4 * slot, 1), :]
-        at_x = slots_ref[pl.ds(4 * slot + 1, 1), :] - plane_x.astype(f32)
-        at_y = slots_ref[pl.ds(4 * slot + 2, 1), :]
-        at_z = slots_ref[pl.ds(4 * slot + 3, 1), :] - row_z.astype(f32)
+    def one(number, slot):
+        plane_x, row_z = codes_scalar[1, number], codes_scalar[2, number]
+        charge, at_x, at_y, at_z = [slot[i : i + 1] for i in range(4)]
+        at_x = at_x - plane_x.astype(f32)
+        at_z = at_z - row_z.astype(f32)
         weight_x = bspline(rows16 - at_x, False) * charge
         weight_z = bspline(rows16 - at_z, False)
         weight_y = jnp.concatenate([bspline(rows40 - at_y, False), jnp.zeros((24, 128), f32)], 0)
@@ -357,11 +342,16 @@
             density[plane_x + i, pl.ds(base, 16), :] += out[16 * i : 16 * i + 16]
 
     def step(index, carry):
-        for found in [one(list_ref[16 * index + k]) for k in range(16)]:
-            put(*found)
+        found = []
+        for k in range(8):
+            pair = slots_ref[pl.ds(pl.multiple_of(64 * index + 8 * k, 8), 8), :]
+            for rank in range(2):
+                found.append(one(16 * index + 2 * k + rank, pair[4 * rank : 4 * rank + 4]))
+        for item in found:
+            put(*item)
         return carry
 
-    lax.fori_loop(0, list_ref[255], step, 0)
+    lax.fori_loop(0, 8, step, 0)
 
     lane = lane_of(2)
     low = lane < 64
@@ -416,7 +406,6 @@
         in_specs=vmem(1),
         out_specs=[pl.BlockSpec(memory_space=pl.ANY), pl.BlockSpec(memory_space=SMEM)],
         scratch_shapes=[
-            SMEM((256,), jnp.int32),
             VMEM((36, 264, 128), f32),
             VMEM((8, 128), jnp.int32),
             VMEM((10, 256, 128), f32),
@@ -430,6 +419,7 @@
 
 TABLES = ("forward_z", "forward_y", "forward_x", "back_x", "fold_y", "back_z")
 ROWS_OF = (0, 8, 24, 32)
+RIMS_OF = (16, 17, 20, 21)
 
 
 def here():
@@ -459,9 +449,9 @@
     packed, fz_high, fz_low = table_vmem[:3]
     row_ref, slots_ref, spring_ref, chosen_ref = table_vmem[13:]
     (
-        lines, waves_in, waves_out, lines_in, plane, plane_rim, rims, rims_out,
-        lines_z, field, force, force_in, table_sem, out_send, out_recv, back_send, back_recv,
-        own_sem, force_send, force_recv,
+        lines, waves_in, waves_out, lines_in, plane, plane_rim,
+        lines_z, last, field, force, force_in, table_sem, out_send, out_recv, back_send, back_recv,
+        own_sem, force_send, force_recv, blocks_sem,
     ) = rest
     (fz, fy, fx, bx, fold, bz) = [(table_vmem[2 * i + 1], table_vmem[2 * i + 2]) for i in range(6)]
     bead, px, py = here()
@@ -480,20 +470,10 @@
         pl.semaphore_signal(barrier, inc=1, device_id=place(other, grid_bead), device_id_type=MESH)
         return carry
 
-    def greet_atoms(step, carry):
-        other = lax.rem(mine + hop(step), OWN)
-        pl.semaphore_signal(barrier, inc=1, device_id=place(other, bead), device_id_type=MESH)
-        return carry
-
     lax.fori_loop(1, OWN, greet, 0)
-
-    @pl.when(same)
-    def _():
-        lax.fori_loop(1, OWN, greet_atoms, 0)
-
-    @pl.when(jnp.logical_not(same))
-    def _():
-        lax.fori_loop(0, OWN, greet_atoms, 0)
+    likes = [(bead, px, lax.rem(py + 2 * k, 8)) for k in range(1, 4)]
+    for like in likes:
+        pl.semaphore_signal(barrier, inc=1, device_id=like, device_id_type=MESH)
 
     for copy in table_copies[3:]:
         copy.start()
@@ -506,10 +486,10 @@
         for part in range(2):
             group = 2 * pair + part
             for c in range(4):
-                start = ROWS_OF[c] + group if group < 8 else 16 + c + 4 * (group - 8)
+                start = ROWS_OF[c] + group if group < 8 else RIMS_OF[c] + 2 * (group - 8)
                 lines[:, start, :] = result[64 * c : 64 * c + 64, 128 * part : 128 * part + 128]
 
-    pl.semaphore_wait(barrier, 2 * OWN - 1 - same.astype(jnp.int32))
+    pl.semaphore_wait(barrier, OWN - 1 + 3)
 
     def own(src, dst, rows, sem):
         return pltpu.make_async_copy(src.at[mine, rows], dst.at[mine, rows], sem)
@@ -525,12 +505,13 @@
         lax.fori_loop(1, OWN, send, 0)
 
     rest = pl.ds(0, OWN - 1)
-    out_rows = (pl.ds(0, 24), pl.ds(24, 16))
-    back_rows = (pl.ds(0, 16), pl.ds(16, 24))
+    half_rows = (pl.ds(0, 20), pl.ds(20, 20))
     for n in range(2):
-        own(lines, waves_in, out_rows[n], own_sem.at[n]).start()
-        send_all(lines, waves_in, out_rows[n], out_send.at[n], out_recv.at[n])
-
+        own(lines, waves_in, half_rows[n], own_sem.at[n]).start()
+        send_all(lines, waves_in, half_rows[n], out_send.at[n], out_recv.at[n])
+
+    for like in likes:
+        pl.semaphore_signal(blocks_sem, inc=1, device_id=like, device_id_type=MESH)
     for copy in table_copies[3:]:
         copy.wait()
 
@@ -545,17 +526,18 @@
     mine_z = lax.broadcasted_iota(jnp.int32, (1, 256), 1) - 2 * mine
 
     for n in range(2):
-        own(lines, waves_in, out_rows[n], own_sem.at[n]).wait()
-        settle(waves_in.at[rest, out_rows[n]], out_recv.at[n])
+        own(lines, waves_in, half_rows[n], own_sem.at[n]).wait()
+        settle(waves_in.at[rest, half_rows[n]], out_recv.at[n])
         for q in range(2):
-            if n == 0:
-                extra = blocks_exchanged(
-                    [waves_in[pl.ds(4 * q + j, 8, stride=8), 16:24, :] for j in range(4)]
-                )
-                for i in range(4):
-                    rims[q, i] = extra[i]
-            else:
-                extra = [rims[q, i] for i in range(4)]
+            padding = jnp.zeros((8, 4, 128), f32)
+            extra = blocks_exchanged(
+                [
+                    jnp.concatenate(
+                        [waves_in[pl.ds(4 * q + j, 8, stride=8), 16 + 4 * n : 20 + 4 * n, :], padding], 1
+                    )
+                    for j in range(4)
+                ]
+            )
             for half in range(2):
                 c = 2 * n + half
                 main = blocks_exchanged(
@@ -566,10 +548,10 @@
                 )
                 for i in range(4):
                     value = main[i]
-                    rim = jnp.where(lane_group == sub, extra[(i + 1) % 4][:, 4 + c : 5 + c, :], 0.0)
+                    rim = jnp.where(lane_group == sub, extra[(i + 1) % 4][:, 2 + half : 3 + half, :], 0.0)
                     if i < 3:
-                        value = value + jnp.where(sub == 0, shifted(extra[i][:, c : c + 1, :], 1), 0.0)
-                        corner = shifted(extra[3][:, c : c + 1, :], 1)
+                        value = value + jnp.where(sub == 0, shifted(extra[i][:, half : half + 1, :], 1), 0.0)
+                        corner = shifted(extra[3][:, half : half + 1, :], 1)
                         rim = rim + jnp.where((sub == 0) & (lane_group == i), corner, 0.0)
                     lines_of = slice(64 * i, 64 * i + 64)
                     plane[half, lines_of, 128 * q : 128 * q + 128] = value.reshape(64, 128)
@@ -606,10 +588,7 @@
         back_rim = [product(jnp.concatenate(split(value), 1), fold[1][...]) for value in back]
 
         for q in range(2):
-            if n == 0:
-                extra = [jnp.zeros((8, 8, 128), f32) for _ in range(4)]
-            else:
-                extra = [rims_out[q, i] for i in range(4)]
+            extra = [jnp.zeros((8, 8, 128), f32) for _ in range(4)]
             for half in range(2):
                 c = 2 * n + half
                 main, corner = [], jnp.zeros((8, 1, 128), f32)
@@ -619,33 +598,29 @@
                     rim = back_rim[half][lines_of, 128 * q : 128 * q + 128].reshape(8, 8, 128)
                     main.append(value)
                     if i < 3:
-                        extra[i] = jnp.where(sub == c, shifted(value[:, 0:1, :], -1), extra[i])
+                        extra[i] = jnp.where(sub == half, shifted(value[:, 0:1, :], -1), extra[i])
                         corner = jnp.where(lane_group == i, shifted(rim[:, 0:1, :], -1), corner)
                     side = jnp.sum(jnp.where(lane_group == sub, rim, 0.0), 1, keepdims=True)
-                    extra[(i + 1) % 4] = jnp.where(sub == 4 + c, side, extra[(i + 1) % 4])
-                extra[3] = jnp.where(sub == c, corner, extra[3])
+                    extra[(i + 1) % 4] = jnp.where(sub == 2 + half, side, extra[(i + 1) % 4])
+                extra[3] = jnp.where(sub == half, corner, extra[3])
                 main = blocks_exchanged(main)
                 for j in range(4):
                     waves_out[pl.ds(4 * q + j, 8, stride=8), ROWS_OF[c] : ROWS_OF[c] + 8, :] = main[j]
-            if n == 0:
-                for i in range(4):
-                    rims_out[q, i] = extra[i]
-            else:
-                extra = blocks_exchanged(extra)
-                for j in range(4):
-                    waves_out[pl.ds(4 * q + j, 8, stride=8), 16:24, :] = extra[j]
-        own(waves_out, lines_in, back_rows[n], own_sem.at[2 + n]).start()
-        send_all(waves_out, lines_in, back_rows[n], back_send.at[n], back_recv.at[n])
+            extra = blocks_exchanged(extra)
+            for j in range(4):
+                waves_out[pl.ds(4 * q + j, 8, stride=8), 16 + 4 * n : 20 + 4 * n, :] = extra[j][:, 0:4, :]
+        own(waves_out, lines_in, half_rows[n], own_sem.at[2 + n]).start()
+        send_all(waves_out, lines_in, half_rows[n], back_send.at[n], back_recv.at[n])
 
     for n in range(2):
-        own(waves_out, lines_in, back_rows[n], own_sem.at[2 + n]).wait()
-        settle(lines_in.at[rest, back_rows[n]], back_recv.at[n])
+        own(waves_out, lines_in, half_rows[n], own_sem.at[2 + n]).wait()
+        settle(lines_in.at[rest, half_rows[n]], back_recv.at[n])
 
     for pair in range(5):
         columns = []
         for group in (2 * pair, 2 * pair + 1):
             starts = [
-                ROWS_OF[c] + group if group < 8 else 16 + c + 4 * (group - 8) for c in range(4)
+                ROWS_OF[c] + group if group < 8 else RIMS_OF[c] + 2 * (group - 8) for c in range(4)
             ]
             columns.append(jnp.concatenate([lines_in[:, start, :] for start in starts], 0))
         result = dots(bz[0][...], bz[1][...], *split(jnp.concatenate(columns, 1)))
@@ -657,8 +632,8 @@
     low_half = lane < 64
     even = (lane // 32) % 2 == 0
 
-    def regroup(part, carry):
-        at = pl.ds(pl.multiple_of(part * 32, 32), 40)
+    def regroup(part, rows):
+        at = pl.ds(pl.multiple_of(part * 32, 32), rows)
         rim = lines_z[9, at, :]
         for group in range(9):
             main = lines_z[group, at, :]
@@ -671,16 +646,28 @@
             pair_even = jnp.where(even, main, side)
             pair_odd = turn(jnp.where(even, side, main), -32)
             for odd, value in enumerate((pair_even, pair_odd)):
+                other = turn(value, 64)
                 high = value.astype(bf16).astype(f32)
-                low = value - high
-                planes = (jnp.where(low_half, high, turn(low, 64)), jnp.where(low_half, turn(high, 64), low))
+                high_other = other.astype(bf16).astype(f32)
+                planes = (
+                    jnp.where(low_half, high, other - high_other),
+                    jnp.where(low_half, high_other, value - high),
+                )
                 for second in range(2):
-                    for k in range(4):
-                        window = planes[second][8 * k : 8 * k + 16].astype(bf16)
-                        field[(4 * group + 2 * second + odd) * 32 + 4 * part + k] = window
+                    plane_x = 4 * group + 2 * second + odd
+                    whole = jnp.concatenate([last[plane_x], planes[second]], 0)
+                    for k in range(rows // 8):
+                        window = whole[8 * k : 8 * k + 16].astype(bf16)
+                        field[plane_x * 32 + 4 * part + k] = window
+                    last[plane_x] = planes[second][rows - 8 : rows]
+
+    def regroup_step(part, carry):
+        regroup(part, 32)
         return carry
 
-    lax.fori_loop(0, 8, regroup, 0)
+    last[...] = jnp.zeros_like(last)
+    lax.fori_loop(0, 8, regroup_step, 0)
+    regroup(8, 8)
 
     rows16 = lax.broadcasted_iota(jnp.int32, (16, 128), 0).astype(f32) - 1.0
     rows40 = lax.broadcasted_iota(jnp.int32, (40, 128), 0).astype(f32) - 1.0
@@ -696,7 +683,7 @@
         y_high, y_low = split(jnp.concatenate([along_y, nothing], 0))
         both = jnp.concatenate([y_high, y_high, y_low, y_low], 0)
         base = codes[0, number]
-        window = jnp.concatenate([field[base + 32 * i] for i in range(11)], 0)
+        window = jnp.concatenate([field[base + 32 * i + 1] for i in range(11)], 0)
         out = jnp.dot(jnp.concatenate([window, window], 1), both, preferred_element_type=f32)
         plain = jnp.zeros((16, 128), f32)
         along_x = jnp.zeros((16, 128), f32)
@@ -718,7 +705,7 @@
             0,
         )
 
-    def interpolate(step, carry):
+    def interpolate(step):
         sources = [lax.rem(chunk + hop(4 * step + k), OWN) for k in range(4)]
         found = []
         for source in sources:
@@ -728,23 +715,34 @@
             )
         for source, value in zip(sources, found):
             force[source] = value
-        for source in sources:
-            back_to_me = jnp.logical_and(same, source == chunk)
-
-            @pl.when(jnp.logical_not(back_to_me))
-            def _():
-                remote(
-                    force.at[source], force_in.at[mine], force_send, force_recv,
-                    (grid_bead, source // 8, source % 8),
-                ).start()
-
-            @pl.when(back_to_me)
-            def _():
-                pltpu.make_async_copy(force.at[source], force_in.at[mine], own_sem.at[4]).start()
-
+        return sources
+
+    def send_force(source):
+        remote(
+            force.at[source], force_in.at[mine], force_send, force_recv,
+            (grid_bead, source // 8, source % 8),
+        ).start()
+
+    pl.semaphore_wait(blocks_sem, 3)
+    sources = interpolate(0)
+
+    @pl.when(same)
+    def _():
+        pltpu.make_async_copy(force.at[chunk], force_in.at[mine], own_sem.at[4]).start()
+
+    @pl.when(jnp.logical_not(same))
+    def _():
+        send_force(chunk)
+
+    for source in sources[1:]:
+        send_force(source)
+
+    def interpolate_step(step, carry):
+        for source in interpolate(step):
+            send_force(source)
         return carry
 
-    lax.fori_loop(0, OWN // 4, interpolate, 0)
+    lax.fori_loop(1, OWN // 4, interpolate_step, 0)
 
     chosen = chosen_ref[...]
 
@@ -768,8 +766,8 @@
         out_ref[axis] = moved + spring_ref[axis]
 
     for n in range(2):
-        settle(lines.at[rest, out_rows[n]], out_send.at[n])
-        settle(waves_out.at[rest, back_rows[n]], back_send.at[n])
+        settle(lines.at[rest, half_rows[n]], out_send.at[n])
+        settle(waves_out.at[rest, half_rows[n]], back_send.at[n])
 
 
 def grid_to_forces(codes, packed, slots, spring, chosen):
@@ -787,10 +785,10 @@
         + [
             chunks, chunks, chunks, chunks,
             VMEM((2, 256, 256), f32), VMEM((2, 256, 512), bf16),
-            VMEM((2, 4, 8, 8, 128), f32), VMEM((2, 4, 8, 8, 128), f32),
-            VMEM((10, 264, 128), f32), VMEM((36 * 32, 16, 128), bf16),
+            VMEM((10, 264, 128), f32), VMEM((36, 8, 128), f32), VMEM((36 * 32 + 1, 16, 128), bf16),
             VMEM((OWN, 8, 128), f32), VMEM((OWN, 8, 128), f32),
             dma((17,)), dma((2,)), dma((2,)), dma((2,)), dma((2,)), dma((5,)), dma, dma,
+            pltpu.SemaphoreType.REGULAR,
         ],
         compiler_params=pltpu.CompilerParams(
             collective_id=1, has_side_effects=True, vmem_limit_bytes=60 << 20

time: 106 us -> 97.7 us (0.922)
  Pallas kernels: 104 us -> 95.1 us
    pallas_call x1, Pallas kernels: 70.8 us -> 60.3 us  [grid_to_forces(): pl.pallas_call(wave_kernel, out_shape=jax.ShapeDtypeStruct((3, OWN, 128),...]
    pallas_call x1, Pallas kernels: 10.6 us -> 11.8 us  [spread(): pl.pallas_call(spread_kernel, out_shape=[jax.ShapeDtypeStruct((10, 256, 1...]
where the time goes in v4:
time: 97.7 us; the launch traced here: 96.7 us
  Pallas kernels  95.1 us (97%)
  local copies, waits for them, and re-layouts  1.54 us (2%)
    pallas_call x1, Pallas kernels, grid_to_forces(): pl.pallas_call(wave_kernel, out_shape=jax.ShapeDtypeStruct((3, OWN, 128),...  60.3 us
    pallas_call x1, Pallas kernels, atoms_to_slots(): pl.pallas_call(atoms_kernel, out_shape=[jax.ShapeDtypeStruct((8 * OWN, 12...  23 us
    pallas_call x1, Pallas kernels, spread(): pl.pallas_call(spread_kernel, out_shape=[jax.ShapeDtypeStruct((10, 256, 1...  11.8 us

profile of v4, /device:TPU:1, one launch (start us, length us, event | category | flops | bytes accessed | tf_op | source)
XLA Modules:
  0.0 96.7 jit_solution(16586716121031196155)
XLA Ops:
  0.0 23.0 %atoms_to_slots.1 = (f32[512,128]{1,0:T(8,128)}, f32[3,64,128]{2,1,0:T(8,128)}, bf16[128,64]{1,0:T(8,128)(2,1)}) custom-call(s32[1,64]{1,0:T(1,128)} %bitcast.10, s32[1,64]{1,0:T(1,128)} %bitcast.11, s32[64,128]{1,0:T(8,128)} %cell_hbm.1, f32[3,64,128]{2,1,0:T(8,128)} %bitcast.9, f32[64,128]{1,0:T(8,128)} %charge_hbm.1, s32[64,128]{1,0:T(8,128)} %zone_hbm.1), custom_call_target="tpu_custom_call" | custom-call | tf_op jit(solution)/shard_map/atoms_to_slots/pallas_call | solution.py:274
  23.0 11.8 %spread.1 = (f32[10,256,128]{2,1,0:T(8,128)}, s32[8,128]{1,0:T(8,128)}) custom-call(f32[512,128]{1,0:T(8,128)} %get-tuple-element.10.slots_ref.rest_14_), custom_call_target="tpu_custom_call" | custom-call | tf_op jit(solution)/shard_map/spread/pallas_call | solution.py:400
  34.8 60.3 %grid_to_forces.1 = f32[3,64,128]{2,1,0:T(8,128)} custom-call(s32[8,128]{1,0:T(8,128)} %get-tuple-element.11.codes, f32[10,256,128]{2,1,0:T(8,128)} %get-tuple-element.12.rest_0_, bf16[256,256]{1,0:T(8,128)(2,1)} %constant.26.clone.rest_1_, bf16[256,256]{1,0:T(8,128)(2,1)} %constant.27.clone.rest_2_, bf16[256,512]{1,0:T(8,128)(2,1)} %constant.28.clone.rest_3_, ...), custom_call_target="tpu_custom_call" | custom-call | tf_op jit(solution)/shard_map/grid_to_forces/pallas_call | solution.py:779
  95.1 1.5 %copy.21 = f32[1,64,3,128]{3,1,2,0:T(8,128)} copy(f32[1,64,3,128]{3,1,2,0:T(8,128)} %bitcast.8) | data formatting | bytes 196608

commit v5 on v4

--- a/solution.py
+++ b/solution.py
@@ -161,10 +161,9 @@
 
 
 def atoms_kernel(
-    owner_hbm, tile_hbm, cell_hbm, frac_hbm, charge_hbm, zone_hbm, slots_ref, spring_ref, chosen_ref,
+    owner_hbm, tile_hbm, cell_hbm, frac_hbm, charge_hbm, zone_hbm, slots_ref,
     owner_ref, tile_ref, cell_ref, frac_ref, charge_ref, zone_ref,
-    payload, stage, before_ref, after_ref,
-    stage_send, stage_recv, send_sem, recv_sem, own_sem, bead_send, bead_recv, in_sem,
+    payload, stage, stage_send, stage_recv, send_sem, recv_sem, own_sem, in_sem, lines_sem,
 ):
     loads = [
         pltpu.make_async_copy(src, dst, in_sem.at[i])
@@ -181,14 +180,11 @@
     chunk = px * 8 + py
     barrier = pltpu.get_barrier_semaphore()
 
-    def greet(step, carry):
-        other = lax.rem(chunk + step, OWN)
-        pl.semaphore_signal(barrier, inc=1, device_id=(bead, other // 8, other % 8), device_id_type=MESH)
-        return carry
-
-    lax.fori_loop(1, OWN, greet, 0)
-    for step in range(1, 4):
-        pl.semaphore_signal(barrier, inc=1, device_id=(lax.rem(bead + step, 4), px, py), device_id_type=MESH)
+    crossing = [(bead, lax.rem(px + step, 8), py) for step in range(1, 8)]
+    greeted = crossing + [(bead, px, lax.rem(py + step, 8)) for step in range(1, 8)]
+    greeted += [(lax.rem(bead + step, 4), px, py) for step in range(1, 4)]
+    for device in greeted:
+        pl.semaphore_signal(barrier, inc=1, device_id=device, device_id_type=MESH)
 
     for copy in loads:
         copy.wait()
@@ -206,6 +202,9 @@
         base = (corners[axis] * 8).astype(f32)
         inside = cells[axis].astype(f32) + frac_ref[axis]
         fields.append(base + jnp.minimum(inside, 8.0 - 2.0**-16))
+    pl.semaphore_wait(barrier, 17)
+    for device in crossing:
+        pl.semaphore_signal(lines_sem, inc=1, device_id=device, device_id_type=MESH)
     for place_in, field in enumerate(fields):
         parts = three(field)
         moved = sum(
@@ -213,7 +212,6 @@
         )
         payload[pl.ds(place_in, 2 * OWN, stride=4), :] = moved
 
-    pl.semaphore_wait(barrier, OWN - 1 + 3)
     staged = [
         remote(
             payload.at[pl.ds(pl.multiple_of(lax.rem(bead + step, 4) * 128, 128), 128)], stage.at[bead],
@@ -223,12 +221,8 @@
     ]
     for copy in staged:
         copy.start()
-    springs = [
-        remote(frac_ref, target, bead_send.at[i], bead_recv.at[i], (lax.rem(bead + step, 4), px, py))
-        for i, (target, step) in enumerate(((before_ref, 1), (after_ref, 3)))
-    ]
-
     mark = pl.ds(pl.multiple_of(chunk * 8, 8), 8)
+    pl.semaphore_wait(lines_sem, 7)
 
     def deliver(source, from_bead):
         def send(step, carry):
@@ -249,18 +243,10 @@
         lax.fori_loop(1, 16, send, 0)
 
     deliver(lambda j: payload.at[pl.ds(pl.multiple_of(bead * 128 + j * 8, 8), 8)], bead)
-    for copy in springs:
-        copy.start()
     for step, copy in zip((1, 3, 2), staged):
         copy.wait_recv()
         other = lax.rem(bead + 4 - step, 4)
         deliver(lambda j: stage.at[other, pl.ds(pl.multiple_of(j * 8, 8), 8)], other)
-    chosen_ref[...] = jnp.where(targets(owner_ref[...], True), 1.0, 0.0).astype(bf16)
-    for copy in springs:
-        copy.wait()
-    for axis in range(3):
-        bend = 2.0 * frac_ref[axis] - before_ref[axis] - after_ref[axis]
-        spring_ref[axis] = -spring_scale * bend
     settle(slots_ref.at[mark], own_sem)
     rest = pl.ds(0, 8 * OWN - 8)
     settle(slots_ref.at[rest], recv_sem)
@@ -273,19 +259,14 @@
     dma = pltpu.SemaphoreType.DMA
     return pl.pallas_call(
         atoms_kernel,
-        out_shape=[
-            jax.ShapeDtypeStruct((8 * OWN, 128), f32),
-            jax.ShapeDtypeStruct((3, OWN, 128), f32),
-            jax.ShapeDtypeStruct((2 * OWN, OWN), bf16),
-        ],
+        out_shape=jax.ShapeDtypeStruct((8 * OWN, 128), f32),
         in_specs=[pl.BlockSpec(memory_space=HBM)] * 6,
-        out_specs=vmem(3),
+        out_specs=pl.BlockSpec(memory_space=pl.ANY),
         scratch_shapes=[
             VMEM((1, OWN), jnp.int32), VMEM((1, OWN), jnp.int32), VMEM((OWN, 128), jnp.int32),
             VMEM((3, OWN, 128), f32), VMEM((OWN, 128), f32), VMEM((OWN, 128), jnp.int32),
             VMEM((8 * OWN, 128), f32), VMEM((4, 128, 128), f32),
-            VMEM((3, OWN, 128), f32), VMEM((3, OWN, 128), f32),
-            dma((3,)), dma((3,)), dma, dma, dma, dma((2,)), dma((2,)), dma((6,)),
+            dma((3,)), dma((3,)), dma, dma, dma, dma((6,)), pltpu.SemaphoreType.REGULAR,
         ],
         compiler_params=pltpu.CompilerParams(
             collective_id=0, has_side_effects=True, vmem_limit_bytes=60 << 20
@@ -310,10 +291,12 @@
     return value.astype(jnp.int32)
 
 
-def spread_kernel(slots_ref, out_hbm, codes_scalar, density, codes, out_ref, sem, out_sem):
+def spread_kernel(slots_ref, out_hbm, codes_hbm, codes_scalar, density, codes, out_ref, sem, out_sem):
     codes[...] = tile_codes(slots_ref)
-    copy = pltpu.make_async_copy(codes, codes_scalar, sem)
+    copy = pltpu.make_async_copy(codes, codes_scalar, sem.at[0])
     copy.start()
+    handed = pltpu.make_async_copy(codes, codes_hbm, sem.at[1])
+    handed.start()
     density[...] = jnp.zeros_like(density)
     copy.wait()
     rows16 = lax.broadcasted_iota(jnp.int32, (16, 128), 0).astype(f32) - 1.0
@@ -391,6 +374,7 @@
         return carry
 
     lax.fori_loop(0, 8, regroup, 0)
+    handed.wait()
     for chunk in range(8):
         here = pl.ds(32 * chunk, 32)
         pltpu.make_async_copy(out_ref.at[:, here, :], out_hbm.at[:, here, :], out_sem.at[chunk]).wait()
@@ -404,12 +388,13 @@
             jax.ShapeDtypeStruct((8, 128), jnp.int32),
         ],
         in_specs=vmem(1),
-        out_specs=[pl.BlockSpec(memory_space=pl.ANY), pl.BlockSpec(memory_space=SMEM)],
+        out_specs=[pl.BlockSpec(memory_space=pl.ANY)] * 2,
         scratch_shapes=[
+            SMEM((8, 128), jnp.int32),
             VMEM((36, 264, 128), f32),
             VMEM((8, 128), jnp.int32),
             VMEM((10, 256, 128), f32),
-            pltpu.SemaphoreType.DMA,
+            pltpu.SemaphoreType.DMA((2,)),
             pltpu.SemaphoreType.DMA((8,)),
         ],
         compiler_params=pltpu.CompilerParams(vmem_limit_bytes=60 << 20),
@@ -441,17 +426,18 @@
 
 
 def wave_kernel(
-    codes, *rest,
+    codes_hbm, *rest,
 ):
     table_refs, rest = rest[:17], rest[17:]
     out_ref, rest = rest[0], rest[1:]
     table_vmem, rest = rest[:17], rest[17:]
     packed, fz_high, fz_low = table_vmem[:3]
-    row_ref, slots_ref, spring_ref, chosen_ref = table_vmem[13:]
+    row_ref, slots_ref, frac_ref, owner_ref = table_vmem[13:]
     (
         lines, waves_in, waves_out, lines_in, plane, plane_rim,
         lines_z, last, field, force, force_in, table_sem, out_send, out_recv, back_send, back_recv,
-        own_sem, force_send, force_recv, blocks_sem,
+        own_sem, force_send, force_recv, blocks_sem, before_ref, after_ref, bead_send, bead_recv,
+        codes, codes_sem, lines_sem,
     ) = rest
     (fz, fy, fx, bx, fold, bz) = [(table_vmem[2 * i + 1], table_vmem[2 * i + 2]) for i in range(6)]
     bead, px, py = here()
@@ -465,20 +451,22 @@
     for copy in table_copies[:3]:
         copy.start()
 
-    def greet(step, carry):
-        other = lax.rem(mine + hop(step), OWN)
-        pl.semaphore_signal(barrier, inc=1, device_id=place(other, grid_bead), device_id_type=MESH)
-        return carry
-
-    lax.fori_loop(1, OWN, greet, 0)
+    crossing = [(bead, lax.rem(px + step, 8), py) for step in range(1, 8)]
+    across = bead * 2 + py % 2
+    along = [lax.rem(across + step, 8) for step in range(1, 8)]
+    greeted = crossing + [(other // 2, px, 2 * grid_bead + other % 2) for other in along]
     likes = [(bead, px, lax.rem(py + 2 * k, 8)) for k in range(1, 4)]
-    for like in likes:
-        pl.semaphore_signal(barrier, inc=1, device_id=like, device_id_type=MESH)
-
+    for device in greeted + likes:
+        pl.semaphore_signal(barrier, inc=1, device_id=device, device_id_type=MESH)
     for copy in table_copies[3:]:
         copy.start()
+    fetched = pltpu.make_async_copy(codes_hbm, codes, codes_sem)
+    fetched.start()
     for copy in table_copies[:3]:
         copy.wait()
+    pl.semaphore_wait(barrier, 17)
+    for device in crossing:
+        pl.semaphore_signal(lines_sem, inc=1, device_id=device, device_id_type=MESH)
 
     for pair in range(5):
         high, low = split(jnp.concatenate([packed[2 * pair], packed[2 * pair + 1]], 1))
@@ -489,7 +477,7 @@
                 start = ROWS_OF[c] + group if group < 8 else RIMS_OF[c] + 2 * (group - 8)
                 lines[:, start, :] = result[64 * c : 64 * c + 64, 128 * part : 128 * part + 128]
 
-    pl.semaphore_wait(barrier, OWN - 1 + 3)
+    pl.semaphore_wait(lines_sem, 7)
 
     def own(src, dst, rows, sem):
         return pltpu.make_async_copy(src.at[mine, rows], dst.at[mine, rows], sem)
@@ -514,6 +502,8 @@
         pl.semaphore_signal(blocks_sem, inc=1, device_id=like, device_id_type=MESH)
     for copy in table_copies[3:]:
         copy.wait()
+    fetched.wait()
+    chosen = jnp.where(targets(owner_ref[...], True), 1.0, 0.0).astype(bf16)
 
     lane = lane_of(3)
     sub = lax.broadcasted_iota(jnp.int32, (1, 8, 128), 1)
@@ -715,7 +705,6 @@
             )
         for source, value in zip(sources, found):
             force[source] = value
-        return sources
 
     def send_force(source):
         remote(
@@ -724,7 +713,13 @@
         ).start()
 
     pl.semaphore_wait(blocks_sem, 3)
-    sources = interpolate(0)
+    springs = [
+        remote(frac_ref, target, bead_send.at[i], bead_recv.at[i], (lax.rem(bead + step, 4), px, py))
+        for i, (target, step) in enumerate(((before_ref, 1), (after_ref, 3)))
+    ]
+    for copy in springs:
+        copy.start()
+    interpolate(0)
 
     @pl.when(same)
     def _():
@@ -734,17 +729,23 @@
     def _():
         send_force(chunk)
 
-    for source in sources[1:]:
-        send_force(source)
+    def send_forces(step, first):
+        for k in range(first, 4):
+            send_force(lax.rem(chunk + hop(4 * step + k), OWN))
+
+    send_forces(0, 1)
 
     def interpolate_step(step, carry):
-        for source in interpolate(step):
-            send_force(source)
+        interpolate(step)
+        send_forces(step - 1, 0)
         return carry
 
-    lax.fori_loop(1, OWN // 4, interpolate_step, 0)
-
-    chosen = chosen_ref[...]
+    interpolate(1)
+    lax.fori_loop(2, OWN // 4, interpolate_step, 0)
+    send_forces(OWN // 4 - 1, 0)
+    for copy in springs:
+        copy.wait()
+    bends = [2.0 * frac_ref[i] - before_ref[i] - after_ref[i] for i in range(3)]
 
     @pl.when(same)
     def _():
@@ -763,23 +764,23 @@
             lax.dot_general(chosen, part, (((0,), (0,)), ((), ())), preferred_element_type=f32)
             for part in reversed(three(both))
         )
-        out_ref[axis] = moved + spring_ref[axis]
+        out_ref[axis] = moved - spring_scale * bends[axis]
 
     for n in range(2):
         settle(lines.at[rest, half_rows[n]], out_send.at[n])
         settle(waves_out.at[rest, half_rows[n]], back_send.at[n])
 
 
-def grid_to_forces(codes, packed, slots, spring, chosen):
+def grid_to_forces(codes, packed, slots, frac, owner_row):
     table = tables()
     consts = [packed] + [jnp.asarray(half) for name in TABLES for half in table[name]]
-    consts += [jnp.asarray(table["row"]), slots, spring, chosen]
+    consts += [jnp.asarray(table["row"]), slots, frac, owner_row]
     dma = pltpu.SemaphoreType.DMA
     chunks = VMEM((OWN, 40, 128), f32)
     return pl.pallas_call(
         wave_kernel,
         out_shape=jax.ShapeDtypeStruct((3, OWN, 128), f32),
-        in_specs=[pl.BlockSpec(memory_space=SMEM)] + [pl.BlockSpec(memory_space=HBM)] * 17,
+        in_specs=[pl.BlockSpec(memory_space=HBM)] * 18,
         out_specs=pl.BlockSpec(memory_space=VMEM),
         scratch_shapes=[VMEM(const.shape, const.dtype) for const in consts]
         + [
@@ -789,6 +790,8 @@
             VMEM((OWN, 8, 128), f32), VMEM((OWN, 8, 128), f32),
             dma((17,)), dma((2,)), dma((2,)), dma((2,)), dma((2,)), dma((5,)), dma, dma,
             pltpu.SemaphoreType.REGULAR,
+            VMEM((3, OWN, 128), f32), VMEM((3, OWN, 128), f32), dma((2,)), dma((2,)),
+            SMEM((8, 128), jnp.int32), dma, pltpu.SemaphoreType.REGULAR,
         ],
         compiler_params=pltpu.CompilerParams(
             collective_id=1, has_side_effects=True, vmem_limit_bytes=60 << 20
@@ -802,11 +805,11 @@
 def local(block_owner, block_tile, atom_cell, atom_frac, charge, zone):
     owner_row = block_owner.reshape(1, OWN)
     frac = jnp.transpose(atom_frac[0], (1, 0, 2))
-    slots, spring, chosen = atoms_to_slots(
+    slots = atoms_to_slots(
         owner_row, block_tile.reshape(1, OWN), atom_cell, frac, charge, zone
     )
     packed, codes = spread(slots)
-    total = grid_to_forces(codes, packed, slots, spring, chosen)
+    total = grid_to_forces(codes, packed, slots, frac, owner_row)
     return jnp.transpose(total, (1, 0, 2))[None]
 
 

time: 97.7 us -> 92.8 us (0.950)
  Pallas kernels: 95.1 us -> 91.1 us
    pallas_call x1, Pallas kernels: 23 us -> 19.5 us  [atoms_to_slots(): pl.pallas_call(atoms_kernel, out_shape=jax.ShapeDtypeStruct((8 * OWN, 128...]
where the time goes in v5:
time: 92.8 us; the launch traced here: 92.6 us
  Pallas kernels  91.1 us (98%)
  local copies, waits for them, and re-layouts  1.54 us (2%)
    pallas_call x1, Pallas kernels, grid_to_forces(): pl.pallas_call(wave_kernel, out_shape=jax.ShapeDtypeStruct((3, OWN, 128),...  60.4 us
    pallas_call x1, Pallas kernels, atoms_to_slots(): pl.pallas_call(atoms_kernel, out_shape=jax.ShapeDtypeStruct((8 * OWN, 128...  19.5 us
    pallas_call x1, Pallas kernels, spread(): pl.pallas_call(spread_kernel, out_shape=[jax.ShapeDtypeStruct((10, 256, 1...  11.2 us

profile of v5, /device:TPU:1, one launch (start us, length us, event | category | flops | bytes accessed | tf_op | source)
XLA Modules:
  0.0 92.6 jit_solution(7890469808411670985)
XLA Ops:
  0.0 19.5 %atoms_to_slots.1.slots_ref.rest_14_ = f32[512,128]{1,0:T(8,128)} custom-call(s32[1,64]{1,0:T(1,128)} %bitcast.11, s32[1,64]{1,0:T(1,128)} %bitcast.13, s32[64,128]{1,0:T(8,128)} %cell_hbm.1, f32[3,64,128]{2,1,0:T(8,128)} %bitcast.8, f32[64,128]{1,0:T(8,128)} %charge_hbm.1, s32[64,128]{1,0:T(8,128)} %zone_hbm.1), custom_call_target="tpu_custom_call" | custom-call | tf_op jit(solution)/shard_map/atoms_to_slots/pallas_call | solution.py:260
  19.5 11.2 %spread.1 = (f32[10,256,128]{2,1,0:T(8,128)}, s32[8,128]{1,0:T(8,128)}) custom-call(f32[512,128]{1,0:T(8,128)} %atoms_to_slots.1.slots_ref.rest_14_), custom_call_target="tpu_custom_call" | custom-call | tf_op jit(solution)/shard_map/spread/pallas_call | solution.py:384
  30.7 60.4 %grid_to_forces.1 = f32[3,64,128]{2,1,0:T(8,128)} custom-call(s32[8,128]{1,0:T(8,128)} %get-tuple-element.7.codes_hbm, f32[10,256,128]{2,1,0:T(8,128)} %get-tuple-element.8.rest_0_, bf16[256,256]{1,0:T(8,128)(2,1)} %constant.26.clone.rest_1_, bf16[256,256]{1,0:T(8,128)(2,1)} %constant.27.clone.rest_2_, bf16[256,512]{1,0:T(8,128)(2,1)} %constant.28.clone.rest_3_, ...), custom_call_target="tpu_custom_call" | custom-call | tf_op jit(solution)/shard_map/grid_to_forces/pallas_call | solution.py:780
  91.1 1.5 %copy.21 = f32[1,64,3,128]{3,1,2,0:T(8,128)} copy(f32[1,64,3,128]{3,1,2,0:T(8,128)} %bitcast.10) | data formatting | bytes 196608

commit v6 on v5

--- a/solution.py
+++ b/solution.py
@@ -117,12 +117,11 @@
     a = jnp.maximum(2.0 - v, 0.0)
     b = jnp.maximum(1.0 - v, 0.0)
     aa = a * a
-    bb = b * b
-    weight = aa * a * (1.0 / 6.0) - bb * b * (4.0 / 6.0)
+    bb = 4.0 * (b * b)
+    weight = aa * a - bb * b
     if not slopes:
         return weight
-    half = 0.5 * aa - 2.0 * bb
-    return weight, jnp.where(offsets < 0.0, -half, half)
+    return weight, jnp.where(offsets < 0.0, bb - aa, aa - bb)
 
 
 def vmem(count):
@@ -202,9 +201,6 @@
         base = (corners[axis] * 8).astype(f32)
         inside = cells[axis].astype(f32) + frac_ref[axis]
         fields.append(base + jnp.minimum(inside, 8.0 - 2.0**-16))
-    pl.semaphore_wait(barrier, 17)
-    for device in crossing:
-        pl.semaphore_signal(lines_sem, inc=1, device_id=device, device_id_type=MESH)
     for place_in, field in enumerate(fields):
         parts = three(field)
         moved = sum(
@@ -212,46 +208,64 @@
         )
         payload[pl.ds(place_in, 2 * OWN, stride=4), :] = moved
 
-    staged = [
-        remote(
-            payload.at[pl.ds(pl.multiple_of(lax.rem(bead + step, 4) * 128, 128), 128)], stage.at[bead],
-            stage_send.at[step - 1], stage_recv.at[step - 1], (lax.rem(bead + step, 4), px, py),
-        )
-        for step in (1, 3, 2)
-    ]
-    for copy in staged:
-        copy.start()
+    pl.semaphore_wait(barrier, 17)
+    for device in crossing:
+        pl.semaphore_signal(lines_sem, inc=1, device_id=device, device_id_type=MESH)
+    staged = []
+    for half in range(2):
+        for step in (1, 3, 2):
+            other = lax.rem(bead + step, 4)
+            start = pl.multiple_of(other * 128 + half * 64, 64)
+            sem = 2 * (step - 1) + half
+            copy = remote(
+                payload.at[pl.ds(start, 64)], stage.at[bead, half * 64 : half * 64 + 64],
+                stage_send.at[sem], stage_recv.at[sem], (other, px, py),
+            )
+            staged.append((step, half, copy))
+            copy.start()
+
     mark = pl.ds(pl.multiple_of(chunk * 8, 8), 8)
     pl.semaphore_wait(lines_sem, 7)
 
-    def deliver(source, from_bead):
+    def deliver_half(turn_of, half):
+        from_bead = lax.rem(bead + turn_of, 4)
+
+        def piece_of(step):
+            j = 8 * half + lax.rem(step + 2 * px + py % 2 + 4 * (py // 2 - from_bead) + 16, 8)
+            at = pl.multiple_of(j * 8, 8)
+            if turn_of == 0:
+                piece = payload.at[pl.ds(pl.multiple_of(bead * 128 + at, 8), 8)]
+            else:
+                piece = stage.at[from_bead, pl.ds(at, 8)]
+            return piece, (bead, j // 2, 2 * from_bead + j % 2)
+
         def send(step, carry):
-            j = lax.rem(step + 2 * px + py % 2, 16)
-            remote(
-                source(j), slots_ref.at[mark], send_sem, recv_sem, (bead, j // 2, 2 * from_bead + j % 2)
-            ).start()
+            piece, device = piece_of(step)
+            remote(piece, slots_ref.at[mark], send_sem, recv_sem, device).start()
             return carry
 
-        @pl.when(from_bead == py // 2)
+        mine = jnp.logical_and(from_bead == py // 2, px // 4 == half)
+
+        @pl.when(mine)
         def _():
-            pltpu.make_async_copy(source(2 * px + py % 2), slots_ref.at[mark], own_sem).start()
-
-        @pl.when(jnp.logical_not(from_bead == py // 2))
+            pltpu.make_async_copy(piece_of(0)[0], slots_ref.at[mark], own_sem).start()
+
+        @pl.when(jnp.logical_not(mine))
         def _():
             send(0, 0)
 
-        lax.fori_loop(1, 16, send, 0)
-
-    deliver(lambda j: payload.at[pl.ds(pl.multiple_of(bead * 128 + j * 8, 8), 8)], bead)
-    for step, copy in zip((1, 3, 2), staged):
+        lax.fori_loop(1, 8, send, 0, unroll=7)
+
+    for half in range(2):
+        deliver_half(0, half)
+    for step, half, copy in staged:
         copy.wait_recv()
-        other = lax.rem(bead + 4 - step, 4)
-        deliver(lambda j: stage.at[other, pl.ds(pl.multiple_of(j * 8, 8), 8)], other)
+        deliver_half(4 - step, half)
     settle(slots_ref.at[mark], own_sem)
     rest = pl.ds(0, 8 * OWN - 8)
     settle(slots_ref.at[rest], recv_sem)
     settle(slots_ref.at[rest], send_sem)
-    for copy in staged:
+    for _, _, copy in staged:
         copy.wait_send()
 
 
@@ -266,7 +280,7 @@
             VMEM((1, OWN), jnp.int32), VMEM((1, OWN), jnp.int32), VMEM((OWN, 128), jnp.int32),
             VMEM((3, OWN, 128), f32), VMEM((OWN, 128), f32), VMEM((OWN, 128), jnp.int32),
             VMEM((8 * OWN, 128), f32), VMEM((4, 128, 128), f32),
-            dma((3,)), dma((3,)), dma, dma, dma, dma((6,)), pltpu.SemaphoreType.REGULAR,
+            dma((6,)), dma((6,)), dma, dma, dma, dma((6,)), pltpu.SemaphoreType.REGULAR,
         ],
         compiler_params=pltpu.CompilerParams(
             collective_id=0, has_side_effects=True, vmem_limit_bytes=60 << 20
@@ -307,7 +321,7 @@
         charge, at_x, at_y, at_z = [slot[i : i + 1] for i in range(4)]
         at_x = at_x - plane_x.astype(f32)
         at_z = at_z - row_z.astype(f32)
-        weight_x = bspline(rows16 - at_x, False) * charge
+        weight_x = bspline(rows16 - at_x, False) * (charge * (1.0 / 216.0))
         weight_z = bspline(rows16 - at_z, False)
         weight_y = jnp.concatenate([bspline(rows40 - at_y, False), jnp.zeros((24, 128), f32)], 0)
         plane = jnp.concatenate([weight_x[i : i + 1] * weight_z for i in range(11)], 0)
@@ -490,7 +504,7 @@
             ).start()
             return carry
 
-        lax.fori_loop(1, OWN, send, 0)
+        lax.fori_loop(1, OWN, send, 0, unroll=9)
 
     rest = pl.ds(0, OWN - 1)
     half_rows = (pl.ds(0, 20), pl.ds(20, 20))
@@ -684,7 +698,7 @@
             plain = plain + weight_x[i : i + 1] * value
             along_x = along_x + slope_x[i : i + 1] * value
             sloped = sloped + weight_x[i : i + 1] * slope
-        minus = -charge
+        minus = charge * (-1.0 / 72.0)
         return jnp.concatenate(
             [
                 minus * jnp.sum(along_x * weight_z, 0, keepdims=True),
@@ -695,8 +709,11 @@
             0,
         )
 
+    def source_at(n):
+        return lax.rem(chunk + hop(OWN - 1 - n), OWN)
+
     def interpolate(step):
-        sources = [lax.rem(chunk + hop(4 * step + k), OWN) for k in range(4)]
+        sources = [source_at(4 * step + k) for k in range(4)]
         found = []
         for source in sources:
             pair = slots_ref[pl.ds(pl.multiple_of(8 * source, 8), 8), :]
@@ -719,7 +736,18 @@
     ]
     for copy in springs:
         copy.start()
+    def send_forces(step, count):
+        for k in range(count):
+            send_force(source_at(4 * step + k))
+
+    def interpolate_step(step, carry):
+        interpolate(step)
+        send_forces(step - 1, 4)
+        return carry
+
     interpolate(0)
+    lax.fori_loop(1, OWN // 4, interpolate_step, 0)
+    send_forces(OWN // 4 - 1, 3)
 
     @pl.when(same)
     def _():
@@ -729,20 +757,6 @@
     def _():
         send_force(chunk)
 
-    def send_forces(step, first):
-        for k in range(first, 4):
-            send_force(lax.rem(chunk + hop(4 * step + k), OWN))
-
-    send_forces(0, 1)
-
-    def interpolate_step(step, carry):
-        interpolate(step)
-        send_forces(step - 1, 0)
-        return carry
-
-    interpolate(1)
-    lax.fori_loop(2, OWN // 4, interpolate_step, 0)
-    send_forces(OWN // 4 - 1, 0)
     for copy in springs:
         copy.wait()
     bends = [2.0 * frac_ref[i] - before_ref[i] - after_ref[i] for i in range(3)]

time: 92.8 us -> 92 us (level)
  no operation moved by 1% of the time
where the time goes in v6:
time: 92 us; the launch traced here: 91.9 us
  Pallas kernels  90.3 us (98%)
  local copies, waits for them, and re-layouts  1.54 us (2%)
    pallas_call x1, Pallas kernels, grid_to_forces(): pl.pallas_call(wave_kernel, out_shape=jax.ShapeDtypeStruct((3, OWN, 128),...  60.1 us
    pallas_call x1, Pallas kernels, atoms_to_slots(): pl.pallas_call(atoms_kernel, out_shape=jax.ShapeDtypeStruct((8 * OWN, 128...  18.9 us
    pallas_call x1, Pallas kernels, spread(): pl.pallas_call(spread_kernel, out_shape=[jax.ShapeDtypeStruct((10, 256, 1...  11.3 us

profile of v6, /device:TPU:1, one launch (start us, length us, event | category | flops | bytes accessed | tf_op | source)
XLA Modules:
  0.0 91.9 jit_solution(11693901105316408961)
XLA Ops:
  0.0 18.9 %atoms_to_slots.1.slots_ref.rest_14_ = f32[512,128]{1,0:T(8,128)} custom-call(s32[1,64]{1,0:T(1,128)} %bitcast.11, s32[1,64]{1,0:T(1,128)} %bitcast.13, s32[64,128]{1,0:T(8,128)} %cell_hbm.1, f32[3,64,128]{2,1,0:T(8,128)} %bitcast.8, f32[64,128]{1,0:T(8,128)} %charge_hbm.1, s32[64,128]{1,0:T(8,128)} %zone_hbm.1), custom_call_target="tpu_custom_call" | custom-call | tf_op jit(solution)/shard_map/atoms_to_slots/pallas_call | solution.py:274
  18.9 11.3 %spread.1 = (f32[10,256,128]{2,1,0:T(8,128)}, s32[8,128]{1,0:T(8,128)}) custom-call(f32[512,128]{1,0:T(8,128)} %atoms_to_slots.1.slots_ref.rest_14_), custom_call_target="tpu_custom_call" | custom-call | tf_op jit(solution)/shard_map/spread/pallas_call | solution.py:398
  30.2 60.1 %grid_to_forces.1 = f32[3,64,128]{2,1,0:T(8,128)} custom-call(s32[8,128]{1,0:T(8,128)} %get-tuple-element.7.codes_hbm, f32[10,256,128]{2,1,0:T(8,128)} %get-tuple-element.8.rest_0_, bf16[256,256]{1,0:T(8,128)(2,1)} %constant.26.clone.rest_1_, bf16[256,256]{1,0:T(8,128)(2,1)} %constant.27.clone.rest_2_, bf16[256,512]{1,0:T(8,128)(2,1)} %constant.28.clone.rest_3_, ...), custom_call_target="tpu_custom_call" | custom-call | tf_op jit(solution)/shard_map/grid_to_forces/pallas_call | solution.py:794
  90.3 1.5 %copy.21 = f32[1,64,3,128]{3,1,2,0:T(8,128)} copy(f32[1,64,3,128]{3,1,2,0:T(8,128)} %bitcast.10) | data formatting | bytes 196608

commit v7 on v6

--- a/solution.py
+++ b/solution.py
@@ -124,6 +124,15 @@
     return weight, jnp.where(offsets < 0.0, bb - aa, aa - bb)
 
 
+def rows_of_y():
+    row = lax.broadcasted_iota(jnp.int32, (40, 128), 0)
+    return jnp.where(row < 36, row, row - 4).astype(f32) - 1.0
+
+
+def with_rims(rows):
+    return jnp.concatenate([rows] + [rows[32:40]] * 3, 0)
+
+
 def vmem(count):
     return [pl.BlockSpec(memory_space=VMEM)] * count
 
@@ -305,16 +314,22 @@
     return value.astype(jnp.int32)
 
 
-def spread_kernel(slots_ref, out_hbm, codes_hbm, codes_scalar, density, codes, out_ref, sem, out_sem):
+def spread_kernel(
+    slots_hbm, out_hbm, codes_hbm, codes_scalar, slots_ref, density, codes, out_ref, sem, out_sem
+):
+    load = pltpu.make_async_copy(slots_hbm, slots_ref, sem.at[2])
+    load.start()
+    density[0:18] = jnp.zeros((18, 264, 128), f32)
+    load.wait()
     codes[...] = tile_codes(slots_ref)
     copy = pltpu.make_async_copy(codes, codes_scalar, sem.at[0])
     copy.start()
     handed = pltpu.make_async_copy(codes, codes_hbm, sem.at[1])
     handed.start()
-    density[...] = jnp.zeros_like(density)
+    density[18:36] = jnp.zeros((18, 264, 128), f32)
     copy.wait()
     rows16 = lax.broadcasted_iota(jnp.int32, (16, 128), 0).astype(f32) - 1.0
-    rows40 = lax.broadcasted_iota(jnp.int32, (40, 128), 0).astype(f32) - 1.0
+    rows40 = rows_of_y()
 
     def one(number, slot):
         plane_x, row_z = codes_scalar[1, number], codes_scalar[2, number]
@@ -323,7 +338,7 @@
         at_z = at_z - row_z.astype(f32)
         weight_x = bspline(rows16 - at_x, False) * (charge * (1.0 / 216.0))
         weight_z = bspline(rows16 - at_z, False)
-        weight_y = jnp.concatenate([bspline(rows40 - at_y, False), jnp.zeros((24, 128), f32)], 0)
+        weight_y = with_rims(bspline(rows40 - at_y, False))
         plane = jnp.concatenate([weight_x[i : i + 1] * weight_z for i in range(11)], 0)
         plane = jnp.concatenate(split(plane), 1)
         y_high, y_low = split(weight_y)
@@ -351,6 +366,7 @@
     lax.fori_loop(0, 8, step, 0)
 
     lane = lane_of(2)
+    lane_group = (lane // 4) % 8
     low = lane < 64
     even = (lane // 32) % 2 == 0
 
@@ -376,12 +392,12 @@
             side = jnp.where(even, pair_odd, pair_even)
             if group < 8:
                 keep(group, main)
-                rim = rim + turn(side, 4 * group)
+                rim = jnp.where(lane_group == group, side, rim)
             else:
                 last = lane >= 96
-                corner = jnp.where((lane >= 96) & (lane < 100), turn(side, 64), 0.0)
-                corner = jnp.where((lane >= 100) & (lane < 104), turn(side, 36), corner)
-                corner = jnp.where((lane >= 104) & (lane < 108), turn(side, 8), corner)
+                corner = jnp.where(lane_group == 0, turn(side, 64), 0.0)
+                corner = jnp.where(lane_group == 1, turn(side, 32), corner)
+                corner = jnp.where(lane_group == 2, side, corner)
                 keep(8, jnp.where(last, corner, main))
         keep(9, rim)
         pltpu.make_async_copy(out_ref.at[:, here, :], out_hbm.at[:, here, :], out_sem.at[chunk]).start()
@@ -401,14 +417,15 @@
             jax.ShapeDtypeStruct((10, 256, 128), f32),
             jax.ShapeDtypeStruct((8, 128), jnp.int32),
         ],
-        in_specs=vmem(1),
+        in_specs=[pl.BlockSpec(memory_space=HBM)],
         out_specs=[pl.BlockSpec(memory_space=pl.ANY)] * 2,
         scratch_shapes=[
             SMEM((8, 128), jnp.int32),
+            VMEM((8 * OWN, 128), f32),
             VMEM((36, 264, 128), f32),
             VMEM((8, 128), jnp.int32),
             VMEM((10, 256, 128), f32),
-            pltpu.SemaphoreType.DMA((2,)),
+            pltpu.SemaphoreType.DMA((3,)),
             pltpu.SemaphoreType.DMA((8,)),
         ],
         compiler_params=pltpu.CompilerParams(vmem_limit_bytes=60 << 20),
@@ -451,7 +468,7 @@
         lines, waves_in, waves_out, lines_in, plane, plane_rim,
         lines_z, last, field, force, force_in, table_sem, out_send, out_recv, back_send, back_recv,
         own_sem, force_send, force_recv, blocks_sem, before_ref, after_ref, bead_send, bead_recv,
-        codes, codes_sem, lines_sem,
+        codes, codes_sem, lines_sem, packed_sem,
     ) = rest
     (fz, fy, fx, bx, fold, bz) = [(table_vmem[2 * i + 1], table_vmem[2 * i + 2]) for i in range(6)]
     bead, px, py = here()
@@ -460,9 +477,11 @@
     barrier = pltpu.get_barrier_semaphore()
 
     table_copies = [
-        pltpu.make_async_copy(table_refs[i], table_vmem[i], table_sem.at[i]) for i in range(17)
+        pltpu.make_async_copy(table_refs[i], table_vmem[i], table_sem.at[i]) for i in range(1, 17)
     ]
-    for copy in table_copies[:3]:
+    packed_copy = pltpu.make_async_copy(table_refs[0], packed, packed_sem)
+    packed_copy.start()
+    for copy in table_copies[:2]:
         copy.start()
 
     crossing = [(bead, lax.rem(px + step, 8), py) for step in range(1, 8)]
@@ -472,15 +491,17 @@
     likes = [(bead, px, lax.rem(py + 2 * k, 8)) for k in range(1, 4)]
     for device in greeted + likes:
         pl.semaphore_signal(barrier, inc=1, device_id=device, device_id_type=MESH)
-    for copy in table_copies[3:]:
+    for copy in table_copies[2:]:
         copy.start()
     fetched = pltpu.make_async_copy(codes_hbm, codes, codes_sem)
     fetched.start()
-    for copy in table_copies[:3]:
-        copy.wait()
     pl.semaphore_wait(barrier, 17)
     for device in crossing:
         pl.semaphore_signal(lines_sem, inc=1, device_id=device, device_id_type=MESH)
+
+    packed_copy.wait()
+    for copy in table_copies[:2]:
+        copy.wait()
 
     for pair in range(5):
         high, low = split(jnp.concatenate([packed[2 * pair], packed[2 * pair + 1]], 1))
@@ -514,7 +535,7 @@
 
     for like in likes:
         pl.semaphore_signal(blocks_sem, inc=1, device_id=like, device_id_type=MESH)
-    for copy in table_copies[3:]:
+    for copy in table_copies[2:]:
         copy.wait()
     fetched.wait()
     chosen = jnp.where(targets(owner_ref[...], True), 1.0, 0.0).astype(bf16)
@@ -633,6 +654,7 @@
             lines_z[2 * pair + part, 256:264, :] = result[0:8, 128 * part : 128 * part + 128]
 
     lane = lane_of(2)
+    lane_group = (lane // 4) % 8
     low_half = lane < 64
     even = (lane // 32) % 2 == 0
 
@@ -642,11 +664,11 @@
         for group in range(9):
             main = lines_z[group, at, :]
             if group < 8:
-                side = turn(rim, -4 * group)
+                side = jnp.where(lane_group == group, rim, 0.0)
             else:
-                side = jnp.where(
-                    lane < 64, turn(main, -64), jnp.where(lane < 96, turn(main, -36), turn(main, -8))
-                )
+                side = jnp.where((lane_group == 2) & (lane >= 96), main, 0.0)
+                side = jnp.where((lane_group == 1) & (lane >= 64) & (lane < 96), turn(main, -32), side)
+                side = jnp.where((lane_group == 0) & (lane >= 32) & (lane < 64), turn(main, -64), side)
             pair_even = jnp.where(even, main, side)
             pair_odd = turn(jnp.where(even, side, main), -32)
             for odd, value in enumerate((pair_even, pair_odd)):
@@ -674,8 +696,7 @@
     regroup(8, 8)
 
     rows16 = lax.broadcasted_iota(jnp.int32, (16, 128), 0).astype(f32) - 1.0
-    rows40 = lax.broadcasted_iota(jnp.int32, (40, 128), 0).astype(f32) - 1.0
-    nothing = jnp.zeros((24, 256), f32)
+    rows40 = rows_of_y()
 
     def one(number, slot):
         charge, at_x, at_y, at_z = [slot[i : i + 1] for i in range(4)]
@@ -684,7 +705,7 @@
         weight_x, slope_x = bspline(rows16 - at_x, True)
         weight_z, slope_z = bspline(rows16 - at_z, True)
         along_y = jnp.concatenate(bspline(rows40 - at_y, True), 1)
-        y_high, y_low = split(jnp.concatenate([along_y, nothing], 0))
+        y_high, y_low = split(with_rims(along_y))
         both = jnp.concatenate([y_high, y_high, y_low, y_low], 0)
         base = codes[0, number]
         window = jnp.concatenate([field[base + 32 * i + 1] for i in range(11)], 0)
@@ -805,7 +826,7 @@
             dma((17,)), dma((2,)), dma((2,)), dma((2,)), dma((2,)), dma((5,)), dma, dma,
             pltpu.SemaphoreType.REGULAR,
             VMEM((3, OWN, 128), f32), VMEM((3, OWN, 128), f32), dma((2,)), dma((2,)),
-            SMEM((8, 128), jnp.int32), dma, pltpu.SemaphoreType.REGULAR,
+            SMEM((8, 128), jnp.int32), dma, pltpu.SemaphoreType.REGULAR, dma,
         ],
         compiler_params=pltpu.CompilerParams(
             collective_id=1, has_side_effects=True, vmem_limit_bytes=60 << 20

time: 92 us -> 91.2 us (level)
  no operation moved by 1% of the time
where the time goes in v7:
time: 91.2 us; the launch traced here: 91 us
  Pallas kernels  89.5 us (98%)
  local copies, waits for them, and re-layouts  1.54 us (2%)
    pallas_call x1, Pallas kernels, grid_to_forces(): pl.pallas_call(wave_kernel, out_shape=jax.ShapeDtypeStruct((3, OWN, 128),...  59.8 us
    pallas_call x1, Pallas kernels, atoms_to_slots(): pl.pallas_call(atoms_kernel, out_shape=jax.ShapeDtypeStruct((8 * OWN, 128...  18.9 us
    pallas_call x1, Pallas kernels, spread(): pl.pallas_call(spread_kernel, out_shape=[jax.ShapeDtypeStruct((10, 256, 1...  10.8 us

profile of v7, /device:TPU:1, one launch (start us, length us, event | category | flops | bytes accessed | tf_op | source)
XLA Modules:
  0.0 91.0 jit_solution(14372515830630368226)
XLA Ops:
  0.0 18.9 %atoms_to_slots.1.slots_hbm.rest_14_ = f32[512,128]{1,0:T(8,128)} custom-call(s32[1,64]{1,0:T(1,128)} %bitcast.11, s32[1,64]{1,0:T(1,128)} %bitcast.13, s32[64,128]{1,0:T(8,128)} %cell_hbm.1, f32[3,64,128]{2,1,0:T(8,128)} %bitcast.8, f32[64,128]{1,0:T(8,128)} %charge_hbm.1, s32[64,128]{1,0:T(8,128)} %zone_hbm.1), custom_call_target="tpu_custom_call" | custom-call | tf_op jit(solution)/shard_map/atoms_to_slots/pallas_call | solution.py:283
  18.9 10.8 %spread.1 = (f32[10,256,128]{2,1,0:T(8,128)}, s32[8,128]{1,0:T(8,128)}) custom-call(f32[512,128]{1,0:T(8,128)} %atoms_to_slots.1.slots_hbm.rest_14_), custom_call_target="tpu_custom_call" | custom-call | tf_op jit(solution)/shard_map/spread/pallas_call | solution.py:414
  29.7 59.8 %grid_to_forces.1 = f32[3,64,128]{2,1,0:T(8,128)} custom-call(s32[8,128]{1,0:T(8,128)} %get-tuple-element.7.codes_hbm, f32[10,256,128]{2,1,0:T(8,128)} %get-tuple-element.8.rest_0_, bf16[256,256]{1,0:T(8,128)(2,1)} %constant.26.clone.rest_1_, bf16[256,256]{1,0:T(8,128)(2,1)} %constant.27.clone.rest_2_, bf16[256,512]{1,0:T(8,128)(2,1)} %constant.28.clone.rest_3_, ...), custom_call_target="tpu_custom_call" | custom-call | tf_op jit(solution)/shard_map/grid_to_forces/pallas_call | solution.py:815
  89.5 1.5 %copy.21 = f32[1,64,3,128]{3,1,2,0:T(8,128)} copy(f32[1,64,3,128]{3,1,2,0:T(8,128)} %bitcast.10) | data formatting | bytes 196608

commit v8 on v7

--- a/solution.py
+++ b/solution.py
@@ -503,17 +503,6 @@
     for copy in table_copies[:2]:
         copy.wait()
 
-    for pair in range(5):
-        high, low = split(jnp.concatenate([packed[2 * pair], packed[2 * pair + 1]], 1))
-        result = dots(fz[0][...], fz[1][...], high, low)
-        for part in range(2):
-            group = 2 * pair + part
-            for c in range(4):
-                start = ROWS_OF[c] + group if group < 8 else RIMS_OF[c] + 2 * (group - 8)
-                lines[:, start, :] = result[64 * c : 64 * c + 64, 128 * part : 128 * part + 128]
-
-    pl.semaphore_wait(lines_sem, 7)
-
     def own(src, dst, rows, sem):
         return pltpu.make_async_copy(src.at[mine, rows], dst.at[mine, rows], sem)
 
@@ -530,6 +519,20 @@
     rest = pl.ds(0, OWN - 1)
     half_rows = (pl.ds(0, 20), pl.ds(20, 20))
     for n in range(2):
+        mine_of = slice(128 * n, 128 * n + 128)
+        for pair in range(5):
+            high, low = split(jnp.concatenate([packed[2 * pair], packed[2 * pair + 1]], 1))
+            result = dots(fz[0][mine_of, :], fz[1][mine_of, :], high, low)
+            for part in range(2):
+                group = 2 * pair + part
+                for half in range(2):
+                    c = 2 * n + half
+                    start = ROWS_OF[c] + group if group < 8 else RIMS_OF[c] + 2 * (group - 8)
+                    lines[:, start, :] = result[
+                        64 * half : 64 * half + 64, 128 * part : 128 * part + 128
+                    ]
+        if n == 0:
+            pl.semaphore_wait(lines_sem, 7)
         own(lines, waves_in, half_rows[n], own_sem.at[n]).start()
         send_all(lines, waves_in, half_rows[n], out_send.at[n], out_recv.at[n])
 

time: 91.2 us -> 90.9 us (level)
  no operation moved by 1% of the time
where the time goes in v8:
time: 90.9 us; the launch traced here: 90.4 us
  Pallas kernels  88.9 us (98%)
  local copies, waits for them, and re-layouts  1.54 us (2%)
    pallas_call x1, Pallas kernels, grid_to_forces(): pl.pallas_call(wave_kernel, out_shape=jax.ShapeDtypeStruct((3, OWN, 128),...  59.2 us
    pallas_call x1, Pallas kernels, atoms_to_slots(): pl.pallas_call(atoms_kernel, out_shape=jax.ShapeDtypeStruct((8 * OWN, 128...  18.9 us
    pallas_call x1, Pallas kernels, spread(): pl.pallas_call(spread_kernel, out_shape=[jax.ShapeDtypeStruct((10, 256, 1...  10.9 us

profile of v8, /device:TPU:1, one launch (start us, length us, event | category | flops | bytes accessed | tf_op | source)
XLA Modules:
  0.0 90.4 jit_solution(888584007733246996)
XLA Ops:
  0.0 18.9 %atoms_to_slots.1.slots_hbm.rest_14_ = f32[512,128]{1,0:T(8,128)} custom-call(s32[1,64]{1,0:T(1,128)} %bitcast.11, s32[1,64]{1,0:T(1,128)} %bitcast.13, s32[64,128]{1,0:T(8,128)} %cell_hbm.1, f32[3,64,128]{2,1,0:T(8,128)} %bitcast.8, f32[64,128]{1,0:T(8,128)} %charge_hbm.1, s32[64,128]{1,0:T(8,128)} %zone_hbm.1), custom_call_target="tpu_custom_call" | custom-call | tf_op jit(solution)/shard_map/atoms_to_slots/pallas_call | solution.py:283
  18.9 10.9 %spread.1 = (f32[10,256,128]{2,1,0:T(8,128)}, s32[8,128]{1,0:T(8,128)}) custom-call(f32[512,128]{1,0:T(8,128)} %atoms_to_slots.1.slots_hbm.rest_14_), custom_call_target="tpu_custom_call" | custom-call | tf_op jit(solution)/shard_map/spread/pallas_call | solution.py:414
  29.7 59.2 %grid_to_forces.1 = f32[3,64,128]{2,1,0:T(8,128)} custom-call(s32[8,128]{1,0:T(8,128)} %get-tuple-element.7.codes_hbm, f32[10,256,128]{2,1,0:T(8,128)} %get-tuple-element.8.rest_0_, bf16[256,256]{1,0:T(8,128)(2,1)} %constant.26.clone.rest_1_, bf16[256,256]{1,0:T(8,128)(2,1)} %constant.27.clone.rest_2_, bf16[256,512]{1,0:T(8,128)(2,1)} %constant.28.clone.rest_3_, ...), custom_call_target="tpu_custom_call" | custom-call | tf_op jit(solution)/shard_map/grid_to_forces/pallas_call | solution.py:818
  88.9 1.5 %copy.21 = f32[1,64,3,128]{3,1,2,0:T(8,128)} copy(f32[1,64,3,128]{3,1,2,0:T(8,128)} %bitcast.10) | data formatting | bytes 196608
